TPU v7x, 512 devices: a whole 4x8x8 slice. The times are simulated.
512 devices in a mesh: patch: 64 (over y, z), band: 8 (over x, core).
Axes of the slice: x: 4, y: 8, z: 8, core: 2. Of those that a mesh axis runs over, the one named last changes fastest.
Arguments:
- visit_tiles: bfloat16 [8, 4096, 128, 128], P('band', 'patch'), may hold values from -8 to 8
- tile_patch: int32 [8, 4096, 1], P('band', 'patch'), may hold values from 0 to 63; in each aligned block of 64 rows (0 to 63, 64 to 127, ..., all dimensions but the last counted through in order) at most 2 rows name the same one
- tile_slot: int32 [8, 4096], P('band', 'patch'), may hold values from 0 to 3
- tile_weight: bfloat16 [8, 4096], P('band', 'patch'), may hold values from 0.5 to 4
- psf_coeff: bfloat16 [8, 4096, 27], P('band', 'patch'), may hold values from -4 to 4
Outputs:
- coadd_image: bfloat16 [8, 16384, 256], P('band', 'patch')
- detection: bfloat16 [8, 4096, 128, 128], P('band', 'patch')
- chi_image: bfloat16 [16384, 256], P('patch')
Inputs may be any that keep to these rules, and one draw needn't show every extreme that they name: `tile_patch`: among the tiles of one device (aligned blocks of 64 tiles of a band), no patch is named more than 2 times, and in some block one patch is named exactly 2 times.
All inputs are finite; a program needn't handle non-finite values.
Results may differ from a plain program's by a relative error of at most 0.012.
Values may be sent and summed in bfloat16 or wider, within the bound.
No kernel may reach another device: no remote copies, remote signals or barrier semaphores. Data moves between devices by JAX's collectives and lax.ppermute only.
A program may use at most 64 MiB of HBM per device.

v0:
```python
import jax
import jax.numpy as jnp
from jax import lax
from jax.sharding import PartitionSpec as P

KR = 10
SB = 2


SIGMAS = (0.7, 1.5, 3.0)
DEGREES = (4, 2, 2)


def padded_2(array, sides, width):
    for axis, dim in sides:
        count, length = (lax.axis_size(axis), array.shape[dim])
        up = [(i, (i + 1) % count) for i in range(count - 1)]
        down = [(j, i) for i, j in up]
        last = lax.slice_in_dim(array, length - width, length, axis=dim)
        first = lax.slice_in_dim(array, 0, width, axis=dim)
        before = lax.ppermute(last, axis, up)
        after = lax.ppermute(first, axis, down)
        array = jnp.concatenate([before, array, after], axis=dim)
    return array


def kernel_taps(sigma_value, exponent):
    offsets = jnp.arange(-KR, KR + 1).astype(jnp.float32)
    gaussian = jnp.exp(-offsets * offsets / (2.0 * sigma_value * sigma_value))
    return (gaussian * (offsets / sigma_value) ** exponent / jnp.sum(gaussian)).astype(jnp.bfloat16)


def smooth_taps():
    offsets = jnp.arange(-KR, KR + 1).astype(jnp.float32)
    gaussian = jnp.exp(-offsets * offsets / 8.0)
    return (gaussian / jnp.sum(gaussian)).astype(jnp.bfloat16)


def band_matrix(tap_table, row_total, col_total, offset_rows):
    distance = jnp.arange(col_total)[None, :] - jnp.arange(row_total)[:, None] - offset_rows
    matrix = jnp.zeros((row_total, col_total), jnp.float32)
    for offset in range(2 * KR + 1):
        matrix = jnp.where(distance == offset - KR, tap_table[offset].astype(jnp.float32), matrix)
    return matrix.astype(jnp.bfloat16)


def basis_list():
    listing = []
    for scale_index in range(len(SIGMAS)):
        for power_x in range(DEGREES[scale_index] + 1):
            for power_y in range(DEGREES[scale_index] + 1 - power_x):
                listing.append((scale_index, power_x, power_y))
    return listing


def power_pairs():
    listing = []
    for scale_index in range(len(SIGMAS)):
        for exponent in range(DEGREES[scale_index] + 1):
            listing.append((scale_index, exponent))
    return listing


def detect(tile_rows, matched, smoother):
    row_count = tile_rows.shape[0]
    side_len = smoother.shape[0]
    difference = (tile_rows.astype(jnp.float32) - matched.astype(jnp.float32)).astype(jnp.bfloat16)
    difference = difference.reshape(row_count, side_len, side_len)
    across = jnp.einsum(
        "rij,kj->rik", difference, smoother, preferred_element_type=jnp.float32
    ).astype(jnp.bfloat16)
    return jnp.einsum("ki,rij->rkj", smoother, across, preferred_element_type=jnp.float32).astype(
        jnp.bfloat16
    )


def in_groups(worker, arrays, group_size):
    row_count = arrays[0].shape[0]
    shaped = tuple(
        (
            member.reshape((row_count // group_size, group_size) + member.shape[1:])
            for member in arrays
        )
    )
    result = lax.map(worker, shaped)
    return result.reshape((row_count,) + result.shape[2:])


def body(visit_tiles, tile_patch, tile_slot, tile_weight, psf_coeff):
    tile_count = visit_tiles.shape[1]
    pixels = visit_tiles.shape[2]
    patch_count = lax.axis_size("patch")
    buckets = 2 * tile_count
    capacity = buckets // patch_count
    slot_count = SB * SB
    tile_rows = visit_tiles.reshape(tile_count, pixels * pixels)
    target = tile_patch[0, :, 0]
    positions = jnp.arange(tile_count)
    same_patch = target[None, :] == target[:, None]
    earlier = positions[None, :] < positions[:, None]
    earlier_count = jnp.sum((same_patch & earlier).astype(jnp.int32), axis=1)
    bucket = target * capacity + earlier_count
    picker = bucket[None, :] == jnp.arange(buckets)[:, None]
    picker_table = picker.astype(jnp.bfloat16)
    send_tiles = jnp.dot(picker_table, tile_rows, preferred_element_type=jnp.float32).astype(
        jnp.bfloat16
    )
    send_tiles = send_tiles.reshape(buckets, pixels, pixels)
    send_weight = jnp.dot(picker_table, tile_weight[0], preferred_element_type=jnp.float32).astype(
        jnp.bfloat16
    )
    send_coeff = jnp.dot(picker_table, psf_coeff[0], preferred_element_type=jnp.float32).astype(
        jnp.bfloat16
    )
    send_slot = jnp.sum(jnp.where(picker, tile_slot[0][None, :], 0), axis=1)
    got_tiles, got_weight, got_slot, got_coeff = (
        lax.all_to_all(send_tiles, "patch", split_axis=0, concat_axis=0, tiled=True),
        lax.all_to_all(send_weight, "patch", split_axis=0, concat_axis=0, tiled=True),
        lax.all_to_all(send_slot, "patch", split_axis=0, concat_axis=0, tiled=True),
        lax.all_to_all(send_coeff, "patch", split_axis=0, concat_axis=0, tiled=True),
    )
    slot_match = got_slot[None, :] == jnp.arange(slot_count)[:, None]
    loading = jnp.where(slot_match, got_weight[None, :], jnp.zeros((), jnp.bfloat16))
    got_rows = got_tiles.reshape(buckets, pixels * pixels)
    numerator = jnp.dot(loading, got_rows, preferred_element_type=jnp.float32)
    weight_sum = jnp.sum(loading.astype(jnp.float32), axis=1)
    blocks = (numerator / jnp.maximum(weight_sum, 1.0)[:, None]).astype(jnp.bfloat16)
    coadd_image = (
        blocks.reshape(SB, SB, pixels, pixels)
        .transpose(0, 2, 1, 3)
        .reshape(SB * pixels, SB * pixels)
    )
    row_total = coadd_image.shape[0]
    col_total = coadd_image.shape[1]
    weight_image = jnp.broadcast_to(
        weight_sum.reshape(SB, 1, SB, 1), (SB, pixels, SB, pixels)
    ).reshape(row_total, col_total)
    coadd_float = coadd_image.astype(jnp.float32)
    chi_terms = weight_image * coadd_float * coadd_float
    chi_image = jnp.sqrt(1.0 + lax.psum(chi_terms, "band")).astype(jnp.bfloat16)
    padded = padded_2(coadd_image, (("patch", 0),), KR)
    pair_listing = power_pairs()
    basis_listing = basis_list()
    row_tables = jnp.stack(
        [
            band_matrix(
                kernel_taps(SIGMAS[scale_index], exponent), row_total, row_total + 2 * KR, KR
            )
            for scale_index, exponent in pair_listing
        ]
    )
    vertical = jnp.einsum(
        "kyc,cx->kyx", row_tables, padded, preferred_element_type=jnp.float32
    ).astype(jnp.bfloat16)
    chosen = jnp.stack(
        [
            vertical[pair_listing.index((scale_index, power_y))]
            for scale_index, power_x, power_y in basis_listing
        ]
    )
    col_tables = jnp.stack(
        [
            band_matrix(kernel_taps(SIGMAS[scale_index], power_x)[::-1], col_total, col_total, 0)
            for scale_index, power_x, power_y in basis_listing
        ]
    )
    basis_images = jnp.einsum(
        "byc,bcx->byx", chosen, col_tables, preferred_element_type=jnp.float32
    ).astype(jnp.bfloat16)
    basis_count = len(basis_listing)
    basis_blocks = basis_images.reshape(basis_count, SB, pixels, SB, pixels).transpose(
        0, 1, 3, 2, 4
    )
    basis_blocks = basis_blocks.reshape(basis_count * slot_count, pixels * pixels)
    smoother = band_matrix(smooth_taps(), pixels, pixels, 0)

    def match_group(group_items):
        group_tiles, group_slot, group_coeff = group_items
        group_match = group_slot[:, None] == jnp.arange(slot_count)[None, :]
        mixing = jnp.where(
            group_match[:, None, :], group_coeff[:, :, None], jnp.zeros((), jnp.bfloat16)
        )
        mixing = mixing.reshape(group_slot.shape[0], basis_count * slot_count)
        matched = jnp.dot(mixing, basis_blocks, preferred_element_type=jnp.float32).astype(
            jnp.bfloat16
        )
        return detect(group_tiles, matched, smoother)

    results = in_groups(match_group, (got_rows, got_slot, got_coeff), 32)
    returned = lax.all_to_all(results, "patch", split_axis=0, concat_axis=0, tiled=True)
    detection = jnp.einsum(
        "rt,rp->tp",
        picker_table,
        returned.reshape(buckets, pixels * pixels),
        preferred_element_type=jnp.float32,
    ).astype(jnp.bfloat16)
    detection = detection.reshape(1, tile_count, pixels, pixels)
    return (coadd_image[None], detection, chi_image)


def solution(mesh):
    return jax.shard_map(
        body,
        mesh=mesh,
        in_specs=(
            P("band", "patch", None, None),
            P("band", "patch", None),
            P("band", "patch"),
            P("band", "patch"),
            P("band", "patch", None),
        ),
        out_specs=(P("band", "patch", None), P("band", "patch", None, None), P("patch", None)),
        check_vma=False,
    )
```

profile of v0, /device:TPU:36, one launch (start us, length us, event | category | flops | bytes accessed | tf_op | source)
XLA Modules:
  0.0 907.0 jit_solution(12670543278150363773)
XLA Ops:
  10.4 16.3 %all-to-all-start.1 = ((bf16[64,2,1]{1,2,0:T(2,128)(2,1)}), bf16[64,2,1]{1,2,0:T(2,128)(2,1)S(1)}, u32[]{:S(2)}, u32[]{:S(2)}) async-start(bf16[64,2,1]{1,2,0:T(2,128)(2,1)} %all_to_all.32), calls=%async_computation.1 | async-start | bytes 65536 | tf_op jit(solution)/shard_map/all_to_all | solution.py:118
  28.3 5.6 all-to-all-done.1
  34.5 9.4 %all-to-all-start = ((s32[64,2,1]{1,2,0:T(1,128)}), s32[64,2,1]{1,2,0:T(1,128)S(1)}, u32[]{:S(2)}, u32[]{:S(2)}) async-start(s32[64,2,1]{1,2,0:T(1,128)} %bitcast.2), calls=%async_computation | async-start | bytes 65536 | tf_op jit(solution)/shard_map/all_to_all | solution.py:119
  43.9 3.3 fusion.165
  47.2 3.3 copy.50
  51.6 12.3 %all-to-all-start.2 = ((bf16[128,128,128]{2,1,0:T(8,128)(2,1)}), bf16[128,128,128]{2,1,0:T(8,128)(2,1)}, u32[]{:S(2)}, u32[]{:S(2)}) async-start(bf16[128,128,128]{2,1,0:T(8,128)(2,1)} %bitcast.619), calls=%async_computation.2 | async-start | bytes 8388608 | tf_op jit(solution)/shard_map/all_to_all | solution.py:117
  88.5 13.3 %fusion.236 = bf16[27,256,256]{2,1,0:T(8,128)(2,1)S(1)} fusion(bf16[]{:T(256)} %bitcast.262, bf16[]{:T(256)} %bitcast.261, bf16[]{:T(256)} %bitcast.260, bf16[]{:T(256)} %bitcast.259, bf16[]{:T(256)} %bitcast.258, bf16[]{:T(256)} %bitcast.257, bf16[]{:T(256)} %bitcast.256, bf16[]{:T(256)} %bitcast.255, bf16[]{:T(256)} %bitcast.254, bf16[]{:T(256)} %bitcast.253, ...), kind=kLoop, calls=%fused_computation.222 | loop fusion | flops 2818047 | bytes 131114
  101.8 13.3 %fusion.235 = bf16[27,256,256]{2,1,0:T(8,128)(2,1)S(1)} fusion(bf16[27,256,256]{2,1,0:T(8,128)(2,1)S(1)} %fusion.236, bf16[]{:T(256)} %bitcast.262, bf16[]{:T(256)} %bitcast.261, bf16[]{:T(256)} %bitcast.260, bf16[]{:T(256)} %bitcast.259, bf16[]{:T(256)} %bitcast.258, bf16[]{:T(256)} %bitcast.257, bf16[]{:T(256)} %bitcast.256, bf16[]{:T(256)} %bitcast.255, ...), kind=kLoop, calls=%fused_computation.221 | loop fusion | flops 2818048 | bytes 131114
  115.0 13.3 %fusion.234 = bf16[27,256,256]{2,1,0:T(8,128)(2,1)S(1)} fusion(bf16[27,256,256]{2,1,0:T(8,128)(2,1)S(1)} %fusion.235, bf16[]{:T(256)} %bitcast.262, bf16[]{:T(256)} %bitcast.261, bf16[]{:T(256)} %bitcast.260, bf16[]{:T(256)} %bitcast.259, bf16[]{:T(256)} %bitcast.258, bf16[]{:T(256)} %bitcast.257, bf16[]{:T(256)} %bitcast.256, bf16[]{:T(256)} %bitcast.255, ...), kind=kLoop, calls=%fused_computation.220 | loop fusion | flops 2818048 | bytes 131114
  128.3 13.3 %fusion.233 = bf16[27,256,256]{2,1,0:T(8,128)(2,1)S(1)} fusion(bf16[27,256,256]{2,1,0:T(8,128)(2,1)S(1)} %fusion.234, bf16[]{:T(256)} %bitcast.262, bf16[]{:T(256)} %bitcast.261, bf16[]{:T(256)} %bitcast.260, bf16[]{:T(256)} %bitcast.259, bf16[]{:T(256)} %bitcast.258, bf16[]{:T(256)} %bitcast.257, bf16[]{:T(256)} %bitcast.256, bf16[]{:T(256)} %bitcast.255, ...), kind=kLoop, calls=%fused_computation.219 | loop fusion | flops 2818048 | bytes 131114
  141.6 13.3 %fusion.237 = bf16[27,256,256]{2,1,0:T(8,128)(2,1)S(1)} fusion(bf16[27,256,256]{2,1,0:T(8,128)(2,1)S(1)} %fusion.233, bf16[]{:T(256)} %bitcast.262, bf16[]{:T(256)} %bitcast.261, bf16[]{:T(256)} %bitcast.260, bf16[]{:T(256)} %bitcast.259, bf16[]{:T(256)} %bitcast.258, bf16[]{:T(256)} %bitcast.257, bf16[]{:T(256)} %bitcast.256, bf16[]{:T(256)} %bitcast.255, ...), kind=kLoop, calls=%fused_computation.223 | loop fusion | flops 2818048 | bytes 131114
  154.9 13.2 %fusion.240 = bf16[27,256,256]{2,1,0:T(8,128)(2,1)S(1)} fusion(bf16[27,256,256]{2,1,0:T(8,128)(2,1)S(1)} %fusion.237, bf16[]{:T(256)} %bitcast.283, bf16[]{:T(256)} %bitcast.282, bf16[]{:T(256)} %bitcast.281, bf16[]{:T(256)} %bitcast.280, bf16[]{:T(256)} %bitcast.279, bf16[]{:T(256)} %bitcast.278, bf16[]{:T(256)} %bitcast.277, bf16[]{:T(256)} %bitcast.276, ...), kind=kLoop, calls=%fused_computation.226 | loop fusion | flops 2818048 | bytes 131114
  168.1 13.2 %fusion.239 = bf16[27,256,256]{2,1,0:T(8,128)(2,1)S(1)} fusion(bf16[27,256,256]{2,1,0:T(8,128)(2,1)S(1)} %fusion.240, bf16[]{:T(256)} %bitcast.283, bf16[]{:T(256)} %bitcast.282, bf16[]{:T(256)} %bitcast.281, bf16[]{:T(256)} %bitcast.280, bf16[]{:T(256)} %bitcast.279, bf16[]{:T(256)} %bitcast.278, bf16[]{:T(256)} %bitcast.277, bf16[]{:T(256)} %bitcast.276, ...), kind=kLoop, calls=%fused_computation.225 | loop fusion | flops 2818048 | bytes 131114
  181.2 13.2 %fusion.238 = bf16[27,256,256]{2,1,0:T(8,128)(2,1)S(1)} fusion(bf16[27,256,256]{2,1,0:T(8,128)(2,1)S(1)} %fusion.239, bf16[]{:T(256)} %bitcast.283, bf16[]{:T(256)} %bitcast.282, bf16[]{:T(256)} %bitcast.281, bf16[]{:T(256)} %bitcast.280, bf16[]{:T(256)} %bitcast.279, bf16[]{:T(256)} %bitcast.278, bf16[]{:T(256)} %bitcast.277, bf16[]{:T(256)} %bitcast.276, ...), kind=kLoop, calls=%fused_computation.224 | loop fusion | flops 2818048 | bytes 131114
  194.4 13.2 %fusion.241 = bf16[27,256,256]{2,1,0:T(8,128)(2,1)S(1)} fusion(bf16[27,256,256]{2,1,0:T(8,128)(2,1)S(1)} %fusion.238, bf16[]{:T(256)} %bitcast.283, bf16[]{:T(256)} %bitcast.282, bf16[]{:T(256)} %bitcast.281, bf16[]{:T(256)} %bitcast.280, bf16[]{:T(256)} %bitcast.279, bf16[]{:T(256)} %bitcast.278, bf16[]{:T(256)} %bitcast.277, bf16[]{:T(256)} %bitcast.276, ...), kind=kLoop, calls=%fused_computation.227 | loop fusion | flops 2818048 | bytes 131114
  207.5 13.5 %fusion.243 = bf16[27,256,256]{2,1,0:T(8,128)(2,1)S(1)} fusion(bf16[27,256,256]{2,1,0:T(8,128)(2,1)S(1)} %fusion.241, bf16[]{:T(256)} %bitcast.304, bf16[]{:T(256)} %bitcast.303, bf16[]{:T(256)} %bitcast.302, bf16[]{:T(256)} %bitcast.301, bf16[]{:T(256)} %bitcast.300, bf16[]{:T(256)} %bitcast.299, bf16[]{:T(256)} %bitcast.298, bf16[]{:T(256)} %bitcast.297, ...), kind=kLoop, calls=%fused_computation.229 | loop fusion | flops 2818048 | bytes 131114
  221.0 13.5 %fusion.242 = bf16[27,256,256]{2,1,0:T(8,128)(2,1)S(1)} fusion(bf16[27,256,256]{2,1,0:T(8,128)(2,1)S(1)} %fusion.243, bf16[]{:T(256)} %bitcast.304, bf16[]{:T(256)} %bitcast.303, bf16[]{:T(256)} %bitcast.302, bf16[]{:T(256)} %bitcast.301, bf16[]{:T(256)} %bitcast.300, bf16[]{:T(256)} %bitcast.299, bf16[]{:T(256)} %bitcast.298, bf16[]{:T(256)} %bitcast.297, ...), kind=kLoop, calls=%fused_computation.228 | loop fusion | flops 2818048 | bytes 131114
  234.5 13.5 %fusion.244 = bf16[27,256,256]{2,1,0:T(8,128)(2,1)S(1)} fusion(bf16[27,256,256]{2,1,0:T(8,128)(2,1)S(1)} %fusion.242, bf16[]{:T(256)} %bitcast.304, bf16[]{:T(256)} %bitcast.303, bf16[]{:T(256)} %bitcast.302, bf16[]{:T(256)} %bitcast.301, bf16[]{:T(256)} %bitcast.300, bf16[]{:T(256)} %bitcast.299, bf16[]{:T(256)} %bitcast.298, bf16[]{:T(256)} %bitcast.297, ...), kind=kLoop, calls=%fused_computation.230 | loop fusion | flops 2818048 | bytes 131114
  248.0 13.2 %fusion.251 = bf16[27,256,256]{2,1,0:T(8,128)(2,1)S(1)} fusion(bf16[27,256,256]{2,1,0:T(8,128)(2,1)S(1)} %fusion.244, bf16[]{:T(256)} %bitcast.325, bf16[]{:T(256)} %bitcast.324, bf16[]{:T(256)} %bitcast.323, bf16[]{:T(256)} %bitcast.322, bf16[]{:T(256)} %bitcast.321, bf16[]{:T(256)} %bitcast.320, bf16[]{:T(256)} %bitcast.319, bf16[]{:T(256)} %bitcast.318, ...), kind=kLoop, calls=%fused_computation.237 | loop fusion | flops 2818048 | bytes 131114
  261.2 13.2 %fusion.252 = bf16[27,256,256]{2,1,0:T(8,128)(2,1)S(1)} fusion(bf16[27,256,256]{2,1,0:T(8,128)(2,1)S(1)} %fusion.251, bf16[]{:T(256)} %bitcast.325, bf16[]{:T(256)} %bitcast.324, bf16[]{:T(256)} %bitcast.323, bf16[]{:T(256)} %bitcast.322, bf16[]{:T(256)} %bitcast.321, bf16[]{:T(256)} %bitcast.320, bf16[]{:T(256)} %bitcast.319, bf16[]{:T(256)} %bitcast.318, ...), kind=kLoop, calls=%fused_computation.238 | loop fusion | flops 2818048 | bytes 131114
  274.4 13.1 %fusion.230 = bf16[27,256,256]{2,1,0:T(8,128)(2,1)S(1)} fusion(bf16[27,256,256]{2,1,0:T(8,128)(2,1)S(1)} %fusion.252, bf16[]{:T(256)} %bitcast.346, bf16[]{:T(256)} %bitcast.345, bf16[]{:T(256)} %bitcast.344, bf16[]{:T(256)} %bitcast.343, bf16[]{:T(256)} %bitcast.342, bf16[]{:T(256)} %bitcast.341, bf16[]{:T(256)} %bitcast.340, bf16[]{:T(256)} %bitcast.339, ...), kind=kLoop, calls=%fused_computation.212 | loop fusion | flops 2818048 | bytes 131114
  287.6 13.1 %fusion.246 = bf16[27,256,256]{2,1,0:T(8,128)(2,1)S(1)} fusion(bf16[27,256,256]{2,1,0:T(8,128)(2,1)S(1)} %fusion.230, bf16[]{:T(256)} %bitcast.367, bf16[]{:T(256)} %bitcast.366, bf16[]{:T(256)} %bitcast.365, bf16[]{:T(256)} %bitcast.364, bf16[]{:T(256)} %bitcast.363, bf16[]{:T(256)} %bitcast.362, bf16[]{:T(256)} %bitcast.361, bf16[]{:T(256)} %bitcast.360, ...), kind=kLoop, calls=%fused_computation.232 | loop fusion | flops 2818048 | bytes 131114
  300.7 13.1 %fusion.245 = bf16[27,256,256]{2,1,0:T(8,128)(2,1)S(1)} fusion(bf16[27,256,256]{2,1,0:T(8,128)(2,1)S(1)} %fusion.246, bf16[]{:T(256)} %bitcast.367, bf16[]{:T(256)} %bitcast.366, bf16[]{:T(256)} %bitcast.365, bf16[]{:T(256)} %bitcast.364, bf16[]{:T(256)} %bitcast.363, bf16[]{:T(256)} %bitcast.362, bf16[]{:T(256)} %bitcast.361, bf16[]{:T(256)} %bitcast.360, ...), kind=kLoop, calls=%fused_computation.231 | loop fusion | flops 2818048 | bytes 131114
  313.9 13.1 %fusion.247 = bf16[27,256,256]{2,1,0:T(8,128)(2,1)S(1)} fusion(bf16[27,256,256]{2,1,0:T(8,128)(2,1)S(1)} %fusion.245, bf16[]{:T(256)} %bitcast.367, bf16[]{:T(256)} %bitcast.366, bf16[]{:T(256)} %bitcast.365, bf16[]{:T(256)} %bitcast.364, bf16[]{:T(256)} %bitcast.363, bf16[]{:T(256)} %bitcast.362, bf16[]{:T(256)} %bitcast.361, bf16[]{:T(256)} %bitcast.360, ...), kind=kLoop, calls=%fused_computation.233 | loop fusion | flops 2818048 | bytes 131114
  327.0 13.1 %fusion.253 = bf16[27,256,256]{2,1,0:T(8,128)(2,1)S(1)} fusion(bf16[27,256,256]{2,1,0:T(8,128)(2,1)S(1)} %fusion.247, bf16[]{:T(256)} %bitcast.388, bf16[]{:T(256)} %bitcast.387, bf16[]{:T(256)} %bitcast.386, bf16[]{:T(256)} %bitcast.385, bf16[]{:T(256)} %bitcast.384, bf16[]{:T(256)} %bitcast.383, bf16[]{:T(256)} %bitcast.382, bf16[]{:T(256)} %bitcast.381, ...), kind=kLoop, calls=%fused_computation.239 | loop fusion | flops 2818048 | bytes 131114
  340.1 13.1 %fusion.254 = bf16[27,256,256]{2,1,0:T(8,128)(2,1)S(1)} fusion(bf16[27,256,256]{2,1,0:T(8,128)(2,1)S(1)} %fusion.253, bf16[]{:T(256)} %bitcast.388, bf16[]{:T(256)} %bitcast.387, bf16[]{:T(256)} %bitcast.386, bf16[]{:T(256)} %bitcast.385, bf16[]{:T(256)} %bitcast.384, bf16[]{:T(256)} %bitcast.383, bf16[]{:T(256)} %bitcast.382, bf16[]{:T(256)} %bitcast.381, ...), kind=kLoop, calls=%fused_computation.240 | loop fusion | flops 2818048 | bytes 131114
  353.2 13.5 %fusion.231 = bf16[27,256,256]{2,1,0:T(8,128)(2,1)S(1)} fusion(bf16[27,256,256]{2,1,0:T(8,128)(2,1)S(1)} %fusion.254, bf16[]{:T(256)} %bitcast.409, bf16[]{:T(256)} %bitcast.408, bf16[]{:T(256)} %bitcast.407, bf16[]{:T(256)} %bitcast.406, bf16[]{:T(256)} %bitcast.405, bf16[]{:T(256)} %bitcast.404, bf16[]{:T(256)} %bitcast.403, bf16[]{:T(256)} %bitcast.402, ...), kind=kLoop, calls=%fused_computation.213 | loop fusion | flops 2818048 | bytes 131114
  366.7 13.3 %fusion.249 = bf16[27,256,256]{2,1,0:T(8,128)(2,1)S(1)} fusion(bf16[27,256,256]{2,1,0:T(8,128)(2,1)S(1)} %fusion.231, bf16[]{:T(256)} %bitcast.430, bf16[]{:T(256)} %bitcast.429, bf16[]{:T(256)} %bitcast.428, bf16[]{:T(256)} %bitcast.427, bf16[]{:T(256)} %bitcast.426, bf16[]{:T(256)} %bitcast.425, bf16[]{:T(256)} %bitcast.424, bf16[]{:T(256)} %bitcast.423, ...), kind=kLoop, calls=%fused_computation.235 | loop fusion | flops 2818048 | bytes 131114
  380.0 13.3 %fusion.248 = bf16[27,256,256]{2,1,0:T(8,128)(2,1)S(1)} fusion(bf16[27,256,256]{2,1,0:T(8,128)(2,1)S(1)} %fusion.249, bf16[]{:T(256)} %bitcast.430, bf16[]{:T(256)} %bitcast.429, bf16[]{:T(256)} %bitcast.428, bf16[]{:T(256)} %bitcast.427, bf16[]{:T(256)} %bitcast.426, bf16[]{:T(256)} %bitcast.425, bf16[]{:T(256)} %bitcast.424, bf16[]{:T(256)} %bitcast.423, ...), kind=kLoop, calls=%fused_computation.234 | loop fusion | flops 2818048 | bytes 131114
  393.4 13.3 %fusion.250 = bf16[27,256,256]{2,1,0:T(8,128)(2,1)S(1)} fusion(bf16[27,256,256]{2,1,0:T(8,128)(2,1)S(1)} %fusion.248, bf16[]{:T(256)} %bitcast.430, bf16[]{:T(256)} %bitcast.429, bf16[]{:T(256)} %bitcast.428, bf16[]{:T(256)} %bitcast.427, bf16[]{:T(256)} %bitcast.426, bf16[]{:T(256)} %bitcast.425, bf16[]{:T(256)} %bitcast.424, bf16[]{:T(256)} %bitcast.423, ...), kind=kLoop, calls=%fused_computation.236 | loop fusion | flops 2818048 | bytes 131114
  406.7 13.2 %fusion.255 = bf16[27,256,256]{2,1,0:T(8,128)(2,1)S(1)} fusion(bf16[27,256,256]{2,1,0:T(8,128)(2,1)S(1)} %fusion.250, bf16[]{:T(256)} %bitcast.451, bf16[]{:T(256)} %bitcast.450, bf16[]{:T(256)} %bitcast.449, bf16[]{:T(256)} %bitcast.448, bf16[]{:T(256)} %bitcast.447, bf16[]{:T(256)} %bitcast.446, bf16[]{:T(256)} %bitcast.445, bf16[]{:T(256)} %bitcast.444, ...), kind=kLoop, calls=%fused_computation.241 | loop fusion | flops 2818048 | bytes 131114
  420.0 13.2 %fusion.256 = bf16[27,256,256]{2,1,0:T(8,128)(2,1)S(1)} fusion(bf16[27,256,256]{2,1,0:T(8,128)(2,1)S(1)} %fusion.255, bf16[]{:T(256)} %bitcast.451, bf16[]{:T(256)} %bitcast.450, bf16[]{:T(256)} %bitcast.449, bf16[]{:T(256)} %bitcast.448, bf16[]{:T(256)} %bitcast.447, bf16[]{:T(256)} %bitcast.446, bf16[]{:T(256)} %bitcast.445, bf16[]{:T(256)} %bitcast.444, ...), kind=kLoop, calls=%fused_computation.242 | loop fusion | flops 2818048 | bytes 131114
  433.2 13.1 %fusion.232 = bf16[27,256,256]{2,1,0:T(8,128)(2,1)S(1)} fusion(bf16[27,256,256]{2,1,0:T(8,128)(2,1)S(1)} %fusion.256, bf16[]{:T(256)} %bitcast.472, bf16[]{:T(256)} %bitcast.471, bf16[]{:T(256)} %bitcast.470, bf16[]{:T(256)} %bitcast.469, bf16[]{:T(256)} %bitcast.468, bf16[]{:T(256)} %bitcast.467, bf16[]{:T(256)} %bitcast.466, bf16[]{:T(256)} %bitcast.465, ...), kind=kLoop, calls=%fused_computation.214 | loop fusion | flops 2818048 | bytes 131114 | tf_op jit(solution)/shard_map/stack | solution.py:161
  446.4 14.0 %fusion.215 = bf16[11,256,276]{1,2,0:T(8,128)(2,1)} fusion(bf16[]{:T(256)} %bitcast.242, bf16[]{:T(256)} %bitcast.243, bf16[]{:T(256)} %bitcast.244, bf16[]{:T(256)} %bitcast.245, bf16[]{:T(256)} %bitcast.246, bf16[]{:T(256)} %bitcast.247, bf16[]{:T(256)} %bitcast.248, bf16[]{:T(256)} %bitcast.249, bf16[]{:T(256)} %bitcast.250, bf16[]{:T(256)} %bitcast.251, ...), kind=kLoop, calls=%fused_computation.196 | loop fusion | flops 3108863 | bytes 143402
  460.3 13.8 %fusion.216 = bf16[11,256,276]{1,2,0:T(8,128)(2,1)} fusion(bf16[11,256,276]{1,2,0:T(8,128)(2,1)} %fusion.215, bf16[]{:T(256)} %bitcast.263, bf16[]{:T(256)} %bitcast.264, bf16[]{:T(256)} %bitcast.265, bf16[]{:T(256)} %bitcast.266, bf16[]{:T(256)} %bitcast.267, bf16[]{:T(256)} %bitcast.268, bf16[]{:T(256)} %bitcast.269, bf16[]{:T(256)} %bitcast.270, ...), kind=kLoop, calls=%fused_computation.197 | loop fusion | flops 3108864 | bytes 154112
  474.2 14.2 %fusion.217 = bf16[11,256,276]{1,2,0:T(8,128)(2,1)} fusion(bf16[11,256,276]{1,2,0:T(8,128)(2,1)} %fusion.216, bf16[]{:T(256)} %bitcast.284, bf16[]{:T(256)} %bitcast.285, bf16[]{:T(256)} %bitcast.286, bf16[]{:T(256)} %bitcast.287, bf16[]{:T(256)} %bitcast.288, bf16[]{:T(256)} %bitcast.289, bf16[]{:T(256)} %bitcast.290, bf16[]{:T(256)} %bitcast.291, ...), kind=kLoop, calls=%fused_computation.198 | loop fusion | flops 3108864 | bytes 154112
  488.4 13.9 %fusion.218 = bf16[11,256,276]{1,2,0:T(8,128)(2,1)} fusion(bf16[11,256,276]{1,2,0:T(8,128)(2,1)} %fusion.217, bf16[]{:T(256)} %bitcast.305, bf16[]{:T(256)} %bitcast.306, bf16[]{:T(256)} %bitcast.307, bf16[]{:T(256)} %bitcast.308, bf16[]{:T(256)} %bitcast.309, bf16[]{:T(256)} %bitcast.310, bf16[]{:T(256)} %bitcast.311, bf16[]{:T(256)} %bitcast.312, ...), kind=kLoop, calls=%fused_computation.199 | loop fusion | flops 3108864 | bytes 154112
  502.2 13.8 %fusion.219 = bf16[11,256,276]{1,2,0:T(8,128)(2,1)} fusion(bf16[11,256,276]{1,2,0:T(8,128)(2,1)} %fusion.218, bf16[]{:T(256)} %bitcast.326, bf16[]{:T(256)} %bitcast.327, bf16[]{:T(256)} %bitcast.328, bf16[]{:T(256)} %bitcast.329, bf16[]{:T(256)} %bitcast.330, bf16[]{:T(256)} %bitcast.331, bf16[]{:T(256)} %bitcast.332, bf16[]{:T(256)} %bitcast.333, ...), kind=kLoop, calls=%fused_computation.200 | loop fusion | flops 3108864 | bytes 154112
  516.1 13.8 %fusion.220 = bf16[11,256,276]{1,2,0:T(8,128)(2,1)} fusion(bf16[11,256,276]{1,2,0:T(8,128)(2,1)} %fusion.219, bf16[]{:T(256)} %bitcast.347, bf16[]{:T(256)} %bitcast.348, bf16[]{:T(256)} %bitcast.349, bf16[]{:T(256)} %bitcast.350, bf16[]{:T(256)} %bitcast.351, bf16[]{:T(256)} %bitcast.352, bf16[]{:T(256)} %bitcast.353, bf16[]{:T(256)} %bitcast.354, ...), kind=kLoop, calls=%fused_computation.201 | loop fusion | flops 3108864 | bytes 154112
  529.9 14.0 %fusion.221 = bf16[11,256,276]{1,2,0:T(8,128)(2,1)} fusion(bf16[11,256,276]{1,2,0:T(8,128)(2,1)} %fusion.220, bf16[]{:T(256)} %bitcast.368, bf16[]{:T(256)} %bitcast.369, bf16[]{:T(256)} %bitcast.370, bf16[]{:T(256)} %bitcast.371, bf16[]{:T(256)} %bitcast.372, bf16[]{:T(256)} %bitcast.373, bf16[]{:T(256)} %bitcast.374, bf16[]{:T(256)} %bitcast.375, ...), kind=kLoop, calls=%fused_computation.202 | loop fusion | flops 3108864 | bytes 154112
  543.9 14.2 %fusion.222 = bf16[11,256,276]{1,2,0:T(8,128)(2,1)} fusion(bf16[11,256,276]{1,2,0:T(8,128)(2,1)} %fusion.221, bf16[]{:T(256)} %bitcast.389, bf16[]{:T(256)} %bitcast.390, bf16[]{:T(256)} %bitcast.391, bf16[]{:T(256)} %bitcast.392, bf16[]{:T(256)} %bitcast.393, bf16[]{:T(256)} %bitcast.394, bf16[]{:T(256)} %bitcast.395, bf16[]{:T(256)} %bitcast.396, ...), kind=kLoop, calls=%fused_computation.203 | loop fusion | flops 3108864 | bytes 154112
  558.0 14.0 %fusion.223 = bf16[11,256,276]{1,2,0:T(8,128)(2,1)} fusion(bf16[11,256,276]{1,2,0:T(8,128)(2,1)} %fusion.222, bf16[]{:T(256)} %bitcast.410, bf16[]{:T(256)} %bitcast.411, bf16[]{:T(256)} %bitcast.412, bf16[]{:T(256)} %bitcast.413, bf16[]{:T(256)} %bitcast.414, bf16[]{:T(256)} %bitcast.415, bf16[]{:T(256)} %bitcast.416, bf16[]{:T(256)} %bitcast.417, ...), kind=kLoop, calls=%fused_computation.204 | loop fusion | flops 3108864 | bytes 154112
  572.1 13.9 %fusion.224 = bf16[11,256,276]{1,2,0:T(8,128)(2,1)} fusion(bf16[11,256,276]{1,2,0:T(8,128)(2,1)} %fusion.223, bf16[]{:T(256)} %bitcast.431, bf16[]{:T(256)} %bitcast.432, bf16[]{:T(256)} %bitcast.433, bf16[]{:T(256)} %bitcast.434, bf16[]{:T(256)} %bitcast.435, bf16[]{:T(256)} %bitcast.436, bf16[]{:T(256)} %bitcast.437, bf16[]{:T(256)} %bitcast.438, ...), kind=kLoop, calls=%fused_computation.205 | loop fusion | flops 3108864 | bytes 154112
  586.0 13.8 %fusion.225 = bf16[11,256,276]{1,2,0:T(8,128)(2,1)} fusion(bf16[11,256,276]{1,2,0:T(8,128)(2,1)} %fusion.224, bf16[]{:T(256)} %bitcast.452, bf16[]{:T(256)} %bitcast.453, bf16[]{:T(256)} %bitcast.454, bf16[]{:T(256)} %bitcast.455, bf16[]{:T(256)} %bitcast.456, bf16[]{:T(256)} %bitcast.457, bf16[]{:T(256)} %bitcast.458, bf16[]{:T(256)} %bitcast.459, ...), kind=kLoop, calls=%fused_computation.206 | loop fusion | flops 3108864 | bytes 154112 | tf_op jit(solution)/shard_map/stack | solution.py:144
  606.3 12.9 %all-to-all-start.3 = ((bf16[64,2,27]{2,1,0:T(2,128)(2,1)}), bf16[64,2,27]{2,1,0:T(2,128)(2,1)}, u32[]{:S(2)}, u32[]{:S(2)}) async-start(bf16[64,2,27]{2,1,0:T(2,128)(2,1)} %bitcast.634), calls=%async_computation.3 | async-start | bytes 65536 | tf_op jit(solution)/shard_map/all_to_all | solution.py:120
  619.2 4.5 fusion.169
  625.8 3.4 collective-permute-start
  629.2 5.8 collective-permute-start.1
  637.0 7.4 reshape_reshape.3
  650.0 6.5 reshape.2369
  658.0 4.9 copy.54
  662.8 81.7 %while.11 = (s32[]{:T(128)}, bf16[4,32,128,128]{3,2,1,0:T(8,128)(2,1)}, bf16[4,32,16384]{2,1,0:T(8,128)(2,1)}, s32[4,32]{1,0:T(4,128)}, bf16[4,32,27]{2,1,0:T(8,...) while((s32[]{:T(128)}, ...), condition=%wide.region_8.9_spmd.clone, body=%wide.region_7.8_spmd.clone.sunk | while | flops 386764288 | bytes 14062443 | solution.py:85
  667.6 13.9 %fusion.322 = bf16[1,32,128,128]{2,3,1,0:T(8,128)(2,1)S(1)} fusion(bf16[32,128,128]{2,1,0:T(8,128)(2,1)S(1)} %bitcast.618, bf16[]{:T(256)} %get-tuple-element.659, bf16[]{:T(256)} %get-tuple-element.660, bf16[]{:T(256)} %get-tuple-element.661, bf16[]{:T(256)} %get-tuple-element.662, bf16[]{:T(256)} %get-tuple-element.663, bf16[]{:T(256)} %get-tuple-element.664, ...), kind=kOutput, calls=%fused_computation.7.clone.1 | convolution fusion | flops 270893056 | bytes 2097194 | tf_op jit(solution)/shard_map/while/body/eval_jaxpr/ki,rij->rkj/dot_general | solution.py:72
  684.8 3.0 fusion.321
  688.1 13.9 %fusion.322 = bf16[1,32,128,128]{2,3,1,0:T(8,128)(2,1)S(1)} fusion(bf16[32,128,128]{2,1,0:T(8,128)(2,1)S(1)} %bitcast.618, bf16[]{:T(256)} %get-tuple-element.659, bf16[]{:T(256)} %get-tuple-element.660, bf16[]{:T(256)} %get-tuple-element.661, bf16[]{:T(256)} %get-tuple-element.662, bf16[]{:T(256)} %get-tuple-element.663, bf16[]{:T(256)} %get-tuple-element.664, ...), kind=kOutput, calls=%fused_computation.7.clone.1 | convolution fusion | flops 270893056 | bytes 2097194 | tf_op jit(solution)/shard_map/while/body/eval_jaxpr/ki,rij->rkj/dot_general | solution.py:72
  705.2 3.0 fusion.321
  708.5 13.9 %fusion.322 = bf16[1,32,128,128]{2,3,1,0:T(8,128)(2,1)S(1)} fusion(bf16[32,128,128]{2,1,0:T(8,128)(2,1)S(1)} %bitcast.618, bf16[]{:T(256)} %get-tuple-element.659, bf16[]{:T(256)} %get-tuple-element.660, bf16[]{:T(256)} %get-tuple-element.661, bf16[]{:T(256)} %get-tuple-element.662, bf16[]{:T(256)} %get-tuple-element.663, bf16[]{:T(256)} %get-tuple-element.664, ...), kind=kOutput, calls=%fused_computation.7.clone.1 | convolution fusion | flops 270893056 | bytes 2097194 | tf_op jit(solution)/shard_map/while/body/eval_jaxpr/ki,rij->rkj/dot_general | solution.py:72
  725.6 3.0 fusion.321
  728.9 13.9 %fusion.322 = bf16[1,32,128,128]{2,3,1,0:T(8,128)(2,1)S(1)} fusion(bf16[32,128,128]{2,1,0:T(8,128)(2,1)S(1)} %bitcast.618, bf16[]{:T(256)} %get-tuple-element.659, bf16[]{:T(256)} %get-tuple-element.660, bf16[]{:T(256)} %get-tuple-element.661, bf16[]{:T(256)} %get-tuple-element.662, bf16[]{:T(256)} %get-tuple-element.663, bf16[]{:T(256)} %get-tuple-element.664, ...), kind=kOutput, calls=%fused_computation.7.clone.1 | convolution fusion | flops 270893056 | bytes 2097194 | tf_op jit(solution)/shard_map/while/body/eval_jaxpr/ki,rij->rkj/dot_general | solution.py:72
  744.5 10.9 %all-to-all-start.4 = ((bf16[128,128,128]{2,1,0:T(8,128)(2,1)}), bf16[128,128,128]{2,1,0:T(8,128)(2,1)}, u32[]{:S(2)}, u32[]{:S(2)}) async-start(bf16[128,128,128]{2,1,0:T(8,128)(2,1)} %bitcast.624), calls=%async_computation.4 | async-start | bytes 8388608 | tf_op jit(solution)/shard_map/all_to_all | solution.py:190
  757.2 71.2 %all-reduce.2.cloned.1.call-done = f32[256,256]{1,0:T(8,128)} async-done(((f32[256,256]{1,0:T(8,128)}), f32[256,256]{1,0:T(8,128)}) %all-reduce.2.cloned.1.call-update) | async-done | bytes 262160 | tf_op jit(solution)/shard_map/psum | solution.py:140
  830.1 57.0 %all-to-all-done.4 = bf16[128,128,128]{2,1,0:T(8,128)(2,1)} async-done(((bf16[128,128,128]{2,1,0:T(8,128)(2,1)}), bf16[128,128,128]{2,1,0:T(8,128)(2,1)}, u32[]{:S(2)}, u32[]{:S(2)}) %all-to-all-start.4) | async-done | bytes 4194336 | tf_op jit(solution)/shard_map/all_to_all | solution.py:190
  887.1 6.9 copy.44
  894.0 3.8 fusion.168
  (144 shorter events, 71.0 us)
Async XLA Ops:
  7.2 56.8 %copy-start = (bf16[1,64,27]{1,2,0:T(8,128)(2,1)S(1)}, bf16[1,64,27]{1,2,0:T(8,128)(2,1)}, u32[]{:S(2)}) copy-start(bf16[1,64,27]{1,2,0:T(8,128)(2,1)} %param.11) | copy-start | bytes 10372
  8.8 55.2 %copy-start.7 = (s32[64]{0:T(128)}, s32[64]{0:T(128)S(1)}, u32[]{:S(2)}) copy-start(s32[64]{0:T(128)S(1)} %multiply_add_fusion) | copy-start | bytes 772
  10.4 23.5 %all-to-all-start.1 = ((bf16[64,2,1]{1,2,0:T(2,128)(2,1)}), bf16[64,2,1]{1,2,0:T(2,128)(2,1)S(1)}, u32[]{:S(2)}, u32[]{:S(2)}) async-start(bf16[64,2,1]{1,2,0:T(2,128)(2,1)} %all_to_all.32), calls=%async_computation.1 | async-start | bytes 65536 | tf_op jit(solution)/shard_map/all_to_all | solution.py:118
  33.9 0.6 copy-start.6
  34.5 16.5 %all-to-all-start = ((s32[64,2,1]{1,2,0:T(1,128)}), s32[64,2,1]{1,2,0:T(1,128)S(1)}, u32[]{:S(2)}, u32[]{:S(2)}) async-start(s32[64,2,1]{1,2,0:T(1,128)} %bitcast.2), calls=%async_computation | async-start | bytes 65536 | tf_op jit(solution)/shard_map/all_to_all | solution.py:119
  51.0 0.6 copy-start.4
  51.6 554.7 %all-to-all-start.2 = ((bf16[128,128,128]{2,1,0:T(8,128)(2,1)}), bf16[128,128,128]{2,1,0:T(8,128)(2,1)}, u32[]{:S(2)}, u32[]{:S(2)}) async-start(bf16[128,128,128]{2,1,0:T(8,128)(2,1)} %bitcast.619), calls=%async_computation.2 | async-start | bytes 8388608 | tf_op jit(solution)/shard_map/all_to_all | solution.py:117
  605.8 0.5 copy-start.9
  606.3 56.5 %all-to-all-start.3 = ((bf16[64,2,27]{2,1,0:T(2,128)(2,1)}), bf16[64,2,27]{2,1,0:T(2,128)(2,1)}, u32[]{:S(2)}, u32[]{:S(2)}) async-start(bf16[64,2,27]{2,1,0:T(2,128)(2,1)} %bitcast.634), calls=%async_computation.3 | async-start | bytes 65536 | tf_op jit(solution)/shard_map/all_to_all | solution.py:120
  623.9 0.7 copy-start.2
  624.5 0.7 copy-start.5
  625.8 18.5 %collective-permute-start = (bf16[10,256]{1,0:T(8,128)(2,1)}, bf16[10,256]{1,0:T(8,128)(2,1)}, u32[]{:S(2)}, u32[]{:S(2)}) collective-permute-start(bf16[10,256]{1,0:T(8,128)(2,1)} %get-tuple-element.172), channel_id=1, source_target_pairs={{0,8},{8,16},{16,24},{24,32},{32,40},{40,48},{48,56},{56,64},{64,7... | collective-permute-start | bytes 15368 | tf_op jit(solution)/shard_map/ppermute | solution.py:21
  629.2 15.2 %collective-permute-start.1 = (bf16[10,256]{1,0:T(8,128)(2,1)S(1)}, bf16[10,256]{1,0:T(8,128)(2,1)}, u32[]{:S(2)}, u32[]{:S(2)}) collective-permute-start(bf16[10,256]{1,0:T(8,128)(2,1)S(1)} %get-tuple-element.173), channel_id=1, source_target_pairs={{8,0},{16,8},{24,16},{32,24},{40,32},{48,40},{56,48},{64,56},{72,6... | collective-permute-start | bytes 15368 | tf_op jit(solution)/shard_map/ppermute | solution.py:22
  744.5 11.0 %copy-start.10 = (f32[4]{0:T(128)S(1)}, f32[4]{0:T(128)}, u32[]{:S(2)}) copy-start(f32[4]{0:T(128)} %copy-done.9) | copy-start | bytes 52
  744.5 11.2 %copy-start.3 = (bf16[2,128,2,128]{3,2,1,0:T(2,128)(2,1)S(1)}, bf16[2,128,2,128]{3,2,1,0:T(2,128)(2,1)}, u32[]{:S(2)}) copy-start(bf16[2,128,2,128]{3,2,1,0:T(2,128)(2,1)} %copy-done.2) | copy-start | bytes 393220
  744.5 142.6 %all-to-all-start.4 = ((bf16[128,128,128]{2,1,0:T(8,128)(2,1)}), bf16[128,128,128]{2,1,0:T(8,128)(2,1)}, u32[]{:S(2)}, u32[]{:S(2)}) async-start(bf16[128,128,128]{2,1,0:T(8,128)(2,1)} %bitcast.624), calls=%async_computation.4 | async-start | bytes 8388608 | tf_op jit(solution)/shard_map/all_to_all | solution.py:190
  755.4 73.0 %all-reduce.2.cloned.1.call-start = ((), (), s32[]{:S(2)}) async-start(), calls=%async_computation.5 | async-start | bytes 524288 | tf_op jit(solution)/shard_map/psum | solution.py:140
  830.1 63.9 %copy-start.8 = (s32[64]{0:T(128)S(1)}, s32[64]{0:T(128)}, u32[]{:S(2)}) copy-start(s32[64]{0:T(128)} %copy-done.7) | copy-start | bytes 772
  894.0 5.7 copy-start.1
Sparse Core Ops, SparseCore 0:
  759.1 69.1 all-reduce.1
where the time goes:
time: 921 us; the launch traced here: 907 us
  other arithmetic  528 us (57%)
  waiting for transfers between devices  134 us (15%)
  matrix products  85.4 us (9%)
  local copies, waits for them, and re-layouts  73.6 us (8%)
  starting transfers between devices  71 us (8%)
  between operations  15 us (2%)
    unnamed x36, other arithmetic  484 us
    psum x1, waiting for transfers between devices, body(): chi_image = jnp.sqrt(1.0 + lax.psum(chi_terms, 'band')).astype(jnp.bfloat16)  71.2 us
    all_to_all x1, waiting for transfers between devices, body(): lax.all_to_all(results, 'patch', split_axis=0, concat_axis=0, tiled=True)  57 us
    dot_general x4, matrix products, detect(): jnp.einsum('ki,rij->rkj', smoother, across, preferred_element_type=jnp.fl...  55.4 us
  transfers between devices with their start and end apart: 8, of which 4 were waited for; matrix products, arithmetic and copies ran while one was open for 65% of the time, Pallas kernels for 0%

commit v1 on v0

v1 whole, which is shorter than its diff:
```python
import functools

import jax
import jax.numpy as jnp
import ml_dtypes
import numpy as np
from jax import lax
from jax.experimental import pallas as pl
from jax.experimental.pallas import tpu as pltpu
from jax.sharding import PartitionSpec as P

KR = 10
SB = 2
PIX = 128
HALF = 64
HALO = 16
SPAN = HALF + HALO
BINS = 256
GROUP = 4
NB = 27
SIGMAS = (0.7, 1.5, 3.0)
DEGREES = (4, 2, 2)
BF16 = jnp.bfloat16
F32 = jnp.float32

PAIRS = [(s, p) for s in range(3) for p in range(DEGREES[s] + 1)]
BASIS = [
    (s, i, j)
    for s in range(3)
    for i in range(DEGREES[s] + 1)
    for j in range(DEGREES[s] + 1 - i)
]


def rounded(values):
    return np.asarray(values, np.float32).astype(ml_dtypes.bfloat16)


def kernel_taps(sigma_value, exponent):
    offsets = np.arange(-KR, KR + 1).astype(np.float32)
    gaussian = np.exp(-offsets * offsets / np.float32(2.0 * sigma_value * sigma_value))
    taps = gaussian * (offsets / np.float32(sigma_value)) ** exponent / np.sum(gaussian)
    return rounded(taps).astype(np.float64)


def smooth_taps():
    offsets = np.arange(-KR, KR + 1).astype(np.float32)
    gaussian = np.exp(-offsets * offsets / np.float32(8.0))
    return rounded(gaussian / np.sum(gaussian)).astype(np.float64)


def tap_matrix(taps, source, target):
    distance = source[:, None] - target[None, :]
    inside = np.abs(distance) <= KR
    return np.where(inside, taps[np.clip(distance + KR, 0, 2 * KR)], 0.0)


def constants():
    pixel = np.arange(PIX)
    smoother = tap_matrix(smooth_taps(), pixel, pixel)
    columns = np.concatenate([pixel, PIX + np.arange(64), np.arange(64) - 64])
    across = np.concatenate(
        [tap_matrix(kernel_taps(SIGMAS[s], i), columns, pixel) @ smoother.T for s, i in PAIRS], axis=1
    )
    upper_rows = np.concatenate([np.arange(HALF), PIX + np.arange(HALO)])
    lower_rows = np.concatenate([np.arange(HALO) - HALO, HALF + np.arange(HALF)])
    down = [
        np.concatenate(
            [-(smoother @ tap_matrix(kernel_taps(SIGMAS[s], j), rows, pixel).T) for s, j in PAIRS],
            axis=1,
        )
        for rows in (upper_rows, lower_rows)
    ]
    upper = np.concatenate([down[0], smoother], axis=1)
    return rounded(across), rounded(upper), rounded(down[1]), rounded(smoother.T)


def exchange_matrix():
    order = np.arange(256).reshape(16, 16).T.reshape(256)
    return np.eye(256, dtype=np.float32)[order].astype(ml_dtypes.bfloat16)


def swap_blocks(exchange, read, write, count):
    for first in range(0, count, 2):
        pair = jnp.concatenate(
            [read(first).reshape(256, PIX), read(first + 1).reshape(256, PIX)], axis=1
        )
        moved = jnp.dot(exchange, pair, preferred_element_type=F32).astype(BF16)
        write(first, moved[:, :PIX].reshape(16, 16, PIX))
        write(first + 1, moved[:, PIX:].reshape(16, 16, PIX))


def pack_kernel(exchange_ref, tile_ref, out_ref):
    exchange = exchange_ref[...]

    def read(block):
        return tile_ref[:, block * 16 : block * 16 + 16, :]

    def write(block, value):
        out_ref[block * 16 : block * 16 + 16, :, :] = value

    swap_blocks(exchange, read, write, HALF // 16)


def pack(exchange, tiles, half):
    count = tiles.shape[0]
    return pl.pallas_call(
        pack_kernel,
        grid=(count // 16,),
        in_specs=[
            pl.BlockSpec((256, 256), lambda g: (0, 0)),
            pl.BlockSpec((16, HALF, PIX), lambda g: (g, half, 0)),
        ],
        out_specs=pl.BlockSpec((HALF, 16, PIX), lambda g: (0, g, 0)),
        out_shape=jax.ShapeDtypeStruct((HALF, count, PIX), BF16),
        cost_estimate=pl.CostEstimate(
            flops=2 * 256 * count * HALF * PIX, bytes_accessed=4 * count * HALF * PIX, transcendentals=0
        ),
    )(exchange, tiles)


CHUNK = 512


def coadd_kernel(bin_ref, weight_ref, row_ref, coadd_ref, sum_ref):
    total = row_ref.shape[0]
    numbers = lax.broadcasted_iota(jnp.int32, (BINS, CHUNK), 0)
    ones = jnp.ones((CHUNK, PIX), BF16)
    running = jnp.zeros((BINS, 2 * PIX), F32)
    for start in range(0, total, CHUNK):
        match = bin_ref[:, start : start + CHUNK] == numbers
        loading = jnp.where(match, weight_ref[:, start : start + CHUNK], 0.0).astype(BF16)
        values = jnp.concatenate([row_ref[start : start + CHUNK, :], ones], axis=1)
        running = running + jnp.dot(loading, values, preferred_element_type=F32)
    weight_sum = running[:, PIX:]
    coadd_ref[...] = (running[:, :PIX] / jnp.maximum(weight_sum, 1.0)).astype(BF16)
    sum_ref[...] = weight_sum


def coadd_rows(bins, weights, rows):
    total = rows.shape[0]
    return pl.pallas_call(
        coadd_kernel,
        out_shape=(
            jax.ShapeDtypeStruct((BINS, PIX), BF16),
            jax.ShapeDtypeStruct((BINS, PIX), F32),
        ),
        compiler_params=pltpu.CompilerParams(vmem_limit_bytes=24 * 1024 * 1024),
        cost_estimate=pl.CostEstimate(
            flops=4 * BINS * total * PIX, bytes_accessed=2 * total * PIX, transcendentals=0
        ),
    )(bins, weights, rows)


def detect_kernel(
    upper,
    place_ref,
    coeff_ref,
    exchange_ref,
    gathered_ref,
    other_ref,
    across_ref,
    down_ref,
    smoother_ref,
    out_ref,
    image_ref,
    window_ref,
    mixed_ref,
):
    exchange = exchange_ref[...]
    lane = lax.broadcasted_iota(jnp.int32, (SPAN, PIX), 1)
    row = lax.broadcasted_iota(jnp.int32, (SPAN, PIX), 0)
    tile_count = out_ref.shape[0]

    def regroup(block, carry):
        base = pl.multiple_of(block * 16, 16)

        def read(number):
            return gathered_ref[number * 16 : number * 16 + 16, pl.ds(base, 16), :]

        def write(number, value):
            image_ref[pl.ds(base, 16), number * 16 : number * 16 + 16, :] = value

        swap_blocks(exchange, read, write, HALF // 16)
        return carry

    lax.fori_loop(0, BINS // 16, regroup, 0)

    def group(number, carry):
        for local in range(GROUP):
            place = place_ref[number * GROUP + local]
            column = place // 128
            level = place % 128
            own = image_ref[place]
            beside_place = place + 128 - 256 * column
            beside = image_ref[beside_place]
            if upper:
                step, edge = 1, level == 127
                own_edge = image_ref[jnp.where(edge, place, place + step), 0:HALO, :]
                beside_edge = image_ref[jnp.where(edge, beside_place, beside_place + step), 0:HALO, :]
                own = jnp.concatenate([own, own_edge], axis=0)
                beside = jnp.concatenate([beside, beside_edge], axis=0)
                outside = edge & (row >= HALF)
            else:
                step, edge = -1, level == 0
                own_edge = image_ref[jnp.where(edge, place, place + step), HALF - HALO : HALF, :]
                beside_edge = image_ref[
                    jnp.where(edge, beside_place, beside_place + step), HALF - HALO : HALF, :
                ]
                own = jnp.concatenate([own_edge, own], axis=0)
                beside = jnp.concatenate([beside_edge, beside], axis=0)
                outside = edge & (row < HALO)
            wrong_side = (lane // 64) != column
            zero = jnp.zeros((SPAN, PIX), F32)
            own = jnp.where(outside, zero, own.astype(F32))
            beside = jnp.where(outside | wrong_side, zero, beside.astype(F32))
            window_ref[local * SPAN : (local + 1) * SPAN, 0:PIX] = own.astype(BF16)
            window_ref[local * SPAN : (local + 1) * SPAN, PIX:] = beside.astype(BF16)
        window = window_ref[...]
        for scale in range(3):
            members = [k for k, pair in enumerate(PAIRS) if pair[0] == scale]
            first, last = members[0], members[-1] + 1
            filtered = jnp.dot(
                window, across_ref[:, first * PIX : last * PIX], preferred_element_type=F32
            )
            for local in range(GROUP):
                rows = slice(local * SPAN, (local + 1) * SPAN)
                base = (number * GROUP + local) * NB
                for power_y in range(DEGREES[scale] + 1):
                    total = None
                    for power_x in range(DEGREES[scale] + 1 - power_y):
                        scalar = coeff_ref[base + BASIS.index((scale, power_x, power_y))]
                        term = scalar * filtered[rows, power_x * PIX : (power_x + 1) * PIX]
                        total = term if total is None else total + term
                    spot = (first + power_y) * SPAN
                    mixed_ref[spot : spot + SPAN, local * PIX : (local + 1) * PIX] = total.astype(BF16)
        begin = pl.multiple_of(number * GROUP, GROUP)
        if upper:
            tiles = other_ref[pl.ds(begin, GROUP)].reshape(GROUP * PIX, PIX)
            smooth = jnp.dot(tiles, smoother_ref[...], preferred_element_type=F32).astype(BF16)
            spot = len(PAIRS) * SPAN
            for local in range(GROUP):
                mixed_ref[spot : spot + PIX, local * PIX : (local + 1) * PIX] = smooth[
                    local * PIX : (local + 1) * PIX
                ]
        result = jnp.dot(down_ref[...], mixed_ref[...], preferred_element_type=F32)
        for local in range(GROUP):
            piece = result[:, local * PIX : (local + 1) * PIX]
            if not upper:
                piece = piece + other_ref[begin + local]
            out_ref[begin + local] = piece.astype(out_ref.dtype)
        return carry

    lax.fori_loop(0, tile_count // GROUP, group, 0)


def detect_half(upper, place, coeff, exchange, gathered, other, across, down, smoother):
    tile_count = other.shape[0]
    depth = down.shape[1]
    smem = pl.BlockSpec(memory_space=pltpu.SMEM)
    vmem = pl.BlockSpec(memory_space=pltpu.VMEM)
    return pl.pallas_call(
        functools.partial(detect_kernel, upper),
        in_specs=[smem, smem] + [vmem] * 6,
        out_specs=vmem,
        out_shape=jax.ShapeDtypeStruct((tile_count, PIX, PIX), F32 if upper else BF16),
        scratch_shapes=[
            pltpu.VMEM((BINS, HALF, PIX), BF16),
            pltpu.VMEM((GROUP * SPAN, 2 * PIX), BF16),
            pltpu.VMEM((depth, GROUP * PIX), BF16),
        ],
        compiler_params=pltpu.CompilerParams(vmem_limit_bytes=40 * 1024 * 1024),
        cost_estimate=pl.CostEstimate(
            flops=2 * tile_count * (SPAN * 256 * 1408 + depth * PIX * PIX),
            bytes_accessed=12 * 1024 * 1024,
            transcendentals=0,
        ),
    )(place, coeff, exchange, gathered, other, across, down, smoother)


def body(visit_tiles, tile_patch, tile_slot, tile_weight, psf_coeff):
    tile_count = visit_tiles.shape[1]
    tiles = visit_tiles[0]
    across, upper, lower, smoother = (jnp.asarray(m) for m in constants())
    exchange = jnp.asarray(exchange_matrix())
    place = (tile_slot[0] % 2) * 128 + 2 * tile_patch[0, :, 0] + tile_slot[0] // 2
    about = jnp.concatenate([place.astype(F32), tile_weight[0].astype(F32)]).reshape(1, 2 * tile_count)
    about = lax.all_gather(about, "patch", axis=0, tiled=True)
    bins = about[:, :tile_count].astype(jnp.int32).reshape(1, -1)
    weights = about[:, tile_count:].reshape(1, -1)
    coeff = psf_coeff[0].astype(F32).reshape(-1)

    def rows_of(packed):
        return lax.all_to_all(packed, "patch", split_axis=0, concat_axis=0, tiled=True).reshape(-1, PIX)

    first_rows = rows_of(pack(exchange, tiles, 0))
    first_coadd, weight_sum = coadd_rows(bins, weights, first_rows)
    second_packed, first_coadd = lax.optimization_barrier((pack(exchange, tiles, 1), first_coadd))
    first_gathered = lax.all_gather(first_coadd, "patch", axis=0, tiled=False)
    second_rows = rows_of(second_packed)
    second_coadd, _ = coadd_rows(bins, weights, second_rows)
    second_gathered = lax.all_gather(second_coadd, "patch", axis=0, tiled=False)

    partial = detect_half(
        True, place, coeff, exchange, first_gathered, tiles, across, upper, smoother
    )
    detection = detect_half(
        False, place, coeff, exchange, second_gathered, partial, across, lower, smoother
    )

    patch = lax.axis_index("patch")

    def own_part(gathered):
        shaped = gathered.reshape(HALF, 2, 128, PIX)
        return lax.dynamic_slice_in_dim(shaped, 2 * patch, 2, axis=2).transpose(2, 0, 1, 3)

    coadd_image = jnp.stack([own_part(first_gathered), own_part(second_gathered)], axis=1)
    own_sum = lax.dynamic_slice_in_dim(weight_sum.reshape(2, 128, PIX), 2 * patch, 2, axis=1)
    own_sum = own_sum.transpose(1, 0, 2)[:, None, None]
    coadd_float = coadd_image.astype(F32)
    terms = (own_sum * coadd_float * coadd_float).reshape(SB * PIX, SB * PIX).astype(BF16)
    terms = lax.all_gather(terms, "band", axis=0, tiled=False)
    chi_image = jnp.sqrt(1.0 + jnp.sum(terms.astype(F32), axis=0)).astype(BF16)
    return (coadd_image.reshape(1, SB * PIX, SB * PIX), detection[None], chi_image)


def solution(mesh):
    return jax.shard_map(
        body,
        mesh=mesh,
        in_specs=(
            P("band", "patch", None, None),
            P("band", "patch", None),
            P("band", "patch"),
            P("band", "patch"),
            P("band", "patch", None),
        ),
        out_specs=(P("band", "patch", None), P("band", "patch", None, None), P("patch", None)),
        check_vma=False,
    )
```

time: 921 us -> 323 us (0.35)
  the two profiles are of different devices: /device:TPU:36 before, /device:TPU:1 now
where the time goes in v1:
time: 323 us; the launch traced here: 319 us
  waiting for transfers between devices  150 us (46%)
  blocking collectives  80.4 us (25%)
  Pallas kernels  44.4 us (14%)
  starting transfers between devices  17.3 us (5%)
  between operations  14 us (4%)
  local copies, waits for them, and re-layouts  9.05 us (3%)
  other arithmetic  4.19 us (1%)
    all_gather x1, waiting for transfers between devices, body(): second_gathered = lax.all_gather(second_coadd, 'patch', axis=0, tiled=False)  86.4 us
    all_gather x1, waiting for transfers between devices, body(): first_gathered = lax.all_gather(first_coadd, 'patch', axis=0, tiled=False)  63.3 us
    all_gather x1, blocking collectives, body(): about = lax.all_gather(about, 'patch', axis=0, tiled=True)  54 us
    pallas_call x2, Pallas kernels, detect_half(): pl.pallas_call(functools.partial(detect_kernel, upper), in_specs=[smem, s...  34 us
    all_to_all x1, blocking collectives, rows_of(): lax.all_to_all(packed, 'patch', split_axis=0, concat_axis=0, tiled=True)  26.4 us
    all_to_all x1, starting transfers between devices, rows_of(): lax.all_to_all(packed, 'patch', split_axis=0, concat_axis=0, tiled=True)  17.1 us
    pallas_call x2, Pallas kernels, pack(): pl.pallas_call(pack_kernel, grid=(count // 16,), in_specs=[pl.BlockSpec((...  7.71 us
  transfers between devices with their start and end apart: 4, of which 2 were waited for; matrix products, arithmetic and copies ran while one was open for 1% of the time, Pallas kernels for 12%

profile of v1, /device:TPU:1, one launch (start us, length us, event | category | flops | bytes accessed | tf_op | source)
XLA Modules:
  0.0 319.1 jit_solution(3312591357328972189)
XLA Ops:
  7.2 0.0 copy-start.12
  7.2 0.0 copy-start.11
  7.2 0.0 copy-start.10
  7.2 3.9 %shard_map.122 = bf16[64,64,128]{2,1,0:T(8,128)(2,1)} custom-call(bf16[256,256]{1,0:T(8,128)(2,1)} %constant.55.clone.exchange_ref, bf16[64,128,128]{2,1,0:T(8,128)(2,1)} %bitcast.42), custom_call_target="tpu_custom_call" | custom-call | flops 268435456 | bytes 2097152 | tf_op jit(solution)/shard_map/pallas_call | solution.py:107
  11.1 17.1 %all-to-all-start = ((bf16[64,64,128]{2,1,0:T(8,128)(2,1)}), bf16[64,64,128]{2,1,0:T(8,128)(2,1)S(1)}, u32[]{:S(2)}, u32[]{:S(2)}) async-start(bf16[64,64,128]{2,1,0:T(8,128)(2,1)} %shard_map.122), calls=%async_computation | async-start | bytes 2097152 | tf_op jit(solution)/shard_map/all_to_all | solution.py:294
  28.2 0.0 all-gather.10.cloned.1.call-start
  28.3 0.0 copy-done.12
  28.3 0.0 copy-done.11
  28.3 0.0 copy-done.10
  28.3 0.1 maximum_bitcast_fusion
  28.4 54.0 %all-gather.3 = f32[64,1,128]{2,1,0:T(1,128)S(1)} all-gather(f32[1,1,128]{2,1,0:T(1,128)S(1)} %maximum_bitcast_fusion), channel_id=2, replica_groups=mesh['patch'=64,'band'=8] {'patch'}, dimensions={0}, use_global_device_ids=true | all-gather | bytes 33280 | tf_op jit(solution)/shard_map/all_gather | solution.py:288
  82.4 0.1 fusion.6
  82.5 0.1 reshape.73.weight_ref
  82.6 0.1 reshape.72.bin_ref
  82.7 3.8 %shard_map.121 = bf16[64,64,128]{2,1,0:T(8,128)(2,1)} custom-call(bf16[256,256]{1,0:T(8,128)(2,1)} %constant.55.clone.exchange_ref, bf16[64,128,128]{2,1,0:T(8,128)(2,1)} %bitcast.43), custom_call_target="tpu_custom_call" | custom-call | flops 268435456 | bytes 2097152 | tf_op jit(solution)/shard_map/pallas_call | solution.py:107
  86.5 0.0 all-to-all-done
  86.5 0.0 copy-start.9
  86.5 0.0 copy-start
  86.5 0.0 copy-start.1
  86.5 0.0 copy-start.7
  86.6 1.3 shard_map.123
  87.9 0.0 copy-start.4
  87.9 0.0 copy-start.5
  87.9 0.0 all-gather.10.cloned.1.call-update
  87.9 0.0 all-gather.12.cloned.1.call-start
  88.0 26.4 %all_to_all.10 = bf16[64,64,128]{2,1,0:T(8,128)(2,1)S(1)} all-to-all(bf16[64,64,128]{2,1,0:T(8,128)(2,1)} %shard_map.121), channel_id=1, replica_groups=mesh['patch'=64,'band'=8] {'patch'}, dimensions={0} | all-to-all | bytes 2097152 | tf_op jit(solution)/shard_map/all_to_all | solution.py:294
  114.4 1.4 shard_map.124
  115.7 0.0 all-gather.12.cloned.1.call-update
  115.8 0.0 all-gather.8.cloned.1.call-start
  115.8 0.8 mul.52
  116.6 1.9 mul.53
  118.5 63.3 %all-gather.10.cloned.1.call-done = bf16[16384,128]{1,0:T(8,128)(2,1)} async-done(((bf16[256,128]{1,0:T(8,128)(2,1)}), bf16[16384,128]{1,0:T(8,128)(2,1)}) %all-gather.10.cloned.1.call-update) | async-done | bytes 4194320 | tf_op jit(solution)/shard_map/all_gather | solution.py:299
  181.8 1.0 dynamic-slice_bitcast_fusion.1
  182.8 86.4 %all-gather.12.cloned.1.call-done = bf16[16384,128]{1,0:T(8,128)(2,1)} async-done(((bf16[256,128]{1,0:T(8,128)(2,1)}), bf16[16384,128]{1,0:T(8,128)(2,1)}) %all-gather.12.cloned.1.call-update) | async-done | bytes 4194320 | tf_op jit(solution)/shard_map/all_gather | solution.py:302
  269.2 1.0 dynamic-slice_bitcast_fusion
  270.3 0.2 pad_maximum_fusion
  270.5 0.7 copy.18
  271.2 1.0 reshape.78
  272.2 0.0 copy-start.8
  272.2 1.7 fusion
  273.9 0.0 all-gather.8.cloned.1.call-update
  273.9 0.0 copy-done.9
  273.9 0.1 copy.19
  274.0 0.1 reshape.81.coeff_ref
  274.2 0.0 copy-done
  274.2 0.0 copy-done.1
  274.2 0.0 copy-done.7
  274.2 0.0 copy-done.4
  274.2 0.0 copy-done.5
  274.2 0.0 copy-start.2
  274.2 2.2 copy-done.2
  276.4 0.0 copy-start.3
  276.4 0.0 copy-start.6
  276.4 16.5 %shard_map.125.other_ref = f32[64,128,128]{2,1,0:T(8,128)S(1)} custom-call(s32[64]{0:T(128)S(1)} %get-tuple-element.14.place_ref, f32[1728]{0:T(1024)S(1)} %reshape.81.coeff_ref, bf16[256,256]{1,0:T(8,128)(2,1)S(1)} %copy-done.1, bf16[64,256,128]{2,1,0:T(8,128)(2,1)S(1)} %bitcast.48, bf16[64,128,128]{2,1,0:T(8,128)(2,1)S(1)} %bitcast.44, ...), custom_call_target="tpu_custom_call" | custom-call | flops 5804916736 | bytes 12582912 | tf_op jit(solution)/shard_map/pallas_call | solution.py:262
  292.9 0.0 copy-done.8
  292.9 0.0 copy-done.3
  292.9 0.0 copy-done.6
  292.9 17.5 %shard_map.126 = bf16[64,128,128]{2,1,0:T(8,128)(2,1)} custom-call(s32[64]{0:T(128)S(1)} %get-tuple-element.14.place_ref, f32[1728]{0:T(1024)S(1)} %reshape.81.coeff_ref, bf16[256,256]{1,0:T(8,128)(2,1)S(1)} %copy-done.1, bf16[64,256,128]{2,1,0:T(8,128)(2,1)S(1)} %bitcast.50, f32[64,128,128]{2,1,0:T(8,128)S(1)} %shard_map.125.other_ref, ...), custom_call_target="tpu_custom_call" | custom-call | flops 5536481280 | bytes 12582912 | tf_op jit(solution)/shard_map/pallas_call | solution.py:262
  310.4 0.0 all-gather.8.cloned.1.call-done
  310.4 1.4 convert_reduce_fusion
  311.8 0.8 sqrt_convert_fusion
  (4 shorter events, 0.0 us)
Async XLA Ops:
  7.2 21.1 %copy-start.12 = (bf16[1,64]{1,0:T(2,128)(2,1)S(1)}, bf16[1,64]{1,0:T(2,128)(2,1)}, u32[]{:S(2)}) copy-start(bf16[1,64]{1,0:T(2,128)(2,1)} %param.13) | copy-start | bytes 388
  7.2 21.1 %copy-start.11 = (s32[1,64]{1,0:T(1,128)S(1)}, s32[1,64]{1,0:T(1,128)}, u32[]{:S(2)}) copy-start(s32[1,64]{1,0:T(1,128)} %param.12) | copy-start | bytes 772
  7.2 21.1 %copy-start.10 = (s32[1,64,1]{1,2,0:T(1,128)S(1)}, s32[1,64,1]{1,2,0:T(1,128)}, u32[]{:S(2)}) copy-start(s32[1,64,1]{1,2,0:T(1,128)} %param.11) | copy-start | bytes 772
  11.1 75.4 %all-to-all-start = ((bf16[64,64,128]{2,1,0:T(8,128)(2,1)}), bf16[64,64,128]{2,1,0:T(8,128)(2,1)S(1)}, u32[]{:S(2)}, u32[]{:S(2)}) async-start(bf16[64,64,128]{2,1,0:T(8,128)(2,1)} %shard_map.122), calls=%async_computation | async-start | bytes 2097152 | tf_op jit(solution)/shard_map/all_to_all | solution.py:294
  28.2 153.5 %all-gather.10.cloned.1.call-start = ((), (), s32[]{:S(2)}) async-start(), calls=%async_computation.3 | async-start | bytes 4259840 | tf_op jit(solution)/shard_map/all_gather | solution.py:299
  86.5 187.4 %copy-start.9 = (bf16[1,64,27]{1,2,0:T(8,128)(2,1)S(1)}, bf16[1,64,27]{1,2,0:T(8,128)(2,1)}, u32[]{:S(2)}) copy-start(bf16[1,64,27]{1,2,0:T(8,128)(2,1)} %param.14) | copy-start | bytes 10372
  86.5 187.6 %copy-start = (bf16[1,64,128,128]{3,2,1,0:T(8,128)(2,1)S(1)}, bf16[1,64,128,128]{3,2,1,0:T(8,128)(2,1)}, u32[]{:S(2)}) copy-start(bf16[1,64,128,128]{3,2,1,0:T(8,128)(2,1)} %param.10) | copy-start | bytes 6291460
  86.5 187.6 %copy-start.1 = (bf16[256,256]{1,0:T(8,128)(2,1)S(1)}, bf16[256,256]{1,0:T(8,128)(2,1)}, u32[]{:S(2)}) copy-start(bf16[256,256]{1,0:T(8,128)(2,1)} %constant.55.clone.exchange_ref) | copy-start | bytes 393220
  86.5 187.6 %copy-start.7 = (bf16[128,128]{1,0:T(8,128)(2,1)S(1)}, bf16[128,128]{1,0:T(8,128)(2,1)}, u32[]{:S(2)}) copy-start(bf16[128,128]{1,0:T(8,128)(2,1)} %constant.54.clone.smoother_ref) | copy-start | bytes 98308
  87.9 186.3 %copy-start.4 = (bf16[256,1408]{1,0:T(8,128)(2,1)S(1)}, bf16[256,1408]{1,0:T(8,128)(2,1)}, u32[]{:S(2)}) copy-start(bf16[256,1408]{1,0:T(8,128)(2,1)} %constant.51.clone.across_ref) | copy-start | bytes 2162692
  87.9 186.3 %copy-start.5 = (bf16[128,1008]{1,0:T(8,128)(2,1)S(1)}, bf16[128,1008]{1,0:T(8,128)(2,1)}, u32[]{:S(2)}) copy-start(bf16[128,1008]{1,0:T(8,128)(2,1)} %constant.52.clone.down_ref) | copy-start | bytes 774148
  87.9 181.3 %all-gather.12.cloned.1.call-start = ((), (), s32[]{:S(2)}) async-start(), calls=%async_computation.4 | async-start | bytes 4259840 | tf_op jit(solution)/shard_map/all_gather | solution.py:302
  115.8 194.6 %all-gather.8.cloned.1.call-start = ((), (), s32[]{:S(2)}) async-start(), calls=%async_computation.2 | async-start | bytes 1179648 | tf_op jit(solution)/shard_map/all_gather | solution.py:322
  272.2 20.7 %copy-start.8 = (bf16[1,256,256]{2,1,0:T(8,128)(2,1)}, bf16[1,256,256]{2,1,0:T(8,128)(2,1)S(1)}, u32[]{:S(2)}) copy-start(bf16[1,256,256]{2,1,0:T(8,128)(2,1)S(1)} %reshape.78) | copy-start | bytes 393220
  274.2 2.2 copy-start.2
  276.4 16.5 %copy-start.3 = (bf16[16384,128]{1,0:T(8,128)(2,1)S(1)}, bf16[16384,128]{1,0:T(8,128)(2,1)}, u32[]{:S(2)}) copy-start(bf16[16384,128]{1,0:T(8,128)(2,1)} %all-gather.12.cloned.1.call-done) | copy-start | bytes 12582916
  276.4 16.5 %copy-start.6 = (bf16[128,880]{1,0:T(8,128)(2,1)S(1)}, bf16[128,880]{1,0:T(8,128)(2,1)}, u32[]{:S(2)}) copy-start(bf16[128,880]{1,0:T(8,128)(2,1)} %constant.53.clone.down_ref) | copy-start | bytes 675844
Sparse Core Ops, SparseCore 0:
  88.0 93.6 all-gather.9
  185.4 83.8 all-gather.11
  274.0 29.8 all-gather.7

commit v2 on v1

v2 whole, which is shorter than its diff:
```python
import jax
import jax.numpy as jnp
import ml_dtypes
import numpy as np
from jax import lax
from jax.experimental import pallas as pl
from jax.experimental.pallas import tpu as pltpu
from jax.sharding import PartitionSpec as P

KR = 10
SB = 2
PIX = 128
HALF = 64
HALO = 16
SPAN = PIX + 2 * HALO
META = 16
BINS = 256
GROUP = 4
NB = 27
SIGMAS = (0.7, 1.5, 3.0)
DEGREES = (4, 2, 2)
BF16 = jnp.bfloat16
F32 = jnp.float32

PAIRS = [(s, p) for s in range(3) for p in range(DEGREES[s] + 1)]
BASIS = [
    (s, i, j)
    for s in range(3)
    for i in range(DEGREES[s] + 1)
    for j in range(DEGREES[s] + 1 - i)
]


def rounded(values):
    return np.asarray(values, np.float32).astype(ml_dtypes.bfloat16)


def kernel_taps(sigma_value, exponent):
    offsets = np.arange(-KR, KR + 1).astype(np.float32)
    gaussian = np.exp(-offsets * offsets / np.float32(2.0 * sigma_value * sigma_value))
    taps = gaussian * (offsets / np.float32(sigma_value)) ** exponent / np.sum(gaussian)
    return rounded(taps).astype(np.float64)


def smooth_taps():
    offsets = np.arange(-KR, KR + 1).astype(np.float32)
    gaussian = np.exp(-offsets * offsets / np.float32(8.0))
    return rounded(gaussian / np.sum(gaussian)).astype(np.float64)


def tap_matrix(taps, source, target):
    distance = source[:, None] - target[None, :]
    inside = np.abs(distance) <= KR
    return np.where(inside, taps[np.clip(distance + KR, 0, 2 * KR)], 0.0)


def constants():
    pixel = np.arange(PIX)
    smoother = tap_matrix(smooth_taps(), pixel, pixel)
    columns = np.concatenate([pixel, PIX + np.arange(64), np.arange(64) - 64])
    across = np.concatenate(
        [tap_matrix(kernel_taps(SIGMAS[s], i), columns, pixel) @ smoother.T for s, i in PAIRS], axis=1
    )
    rows = np.arange(SPAN) - HALO
    down = [-(smoother @ tap_matrix(kernel_taps(SIGMAS[s], j), rows, pixel).T) for s, j in PAIRS]
    return rounded(across), rounded(np.concatenate(down + [smoother], axis=1)), rounded(smoother.T)


def exchange_matrix():
    order = np.arange(256).reshape(16, 16).T.reshape(256)
    return np.eye(256, dtype=np.float32)[order].astype(ml_dtypes.bfloat16)


def swap_blocks(exchange, read, write, count):
    for first in range(0, count, 2):
        pair = jnp.concatenate(
            [read(first).reshape(256, PIX), read(first + 1).reshape(256, PIX)], axis=1
        )
        moved = jnp.dot(exchange, pair, preferred_element_type=F32).astype(BF16)
        write(first, moved[:, :PIX].reshape(16, 16, PIX))
        write(first + 1, moved[:, PIX:].reshape(16, 16, PIX))


def pack_kernel(exchange_ref, about_ref, tile_ref, out_ref):
    step = pl.program_id(0)

    @pl.when(step < pl.num_programs(0) - 1)
    def _():
        def read(block):
            return tile_ref[:, block * 16 : block * 16 + 16, :]

        def write(block, value):
            out_ref[block * 16 : block * 16 + 16, :, :] = value

        swap_blocks(exchange_ref[...], read, write, HALF // 16)

    @pl.when(step == pl.num_programs(0) - 1)
    def _():
        out_ref[...] = jnp.broadcast_to(about_ref[...][None], out_ref.shape)


def pack(exchange, about, tiles):
    count = tiles.shape[0]
    parts = count // 16
    return pl.pallas_call(
        pack_kernel,
        grid=(2 * parts + 1,),
        in_specs=[
            pl.BlockSpec((256, 256), lambda g: (0, 0)),
            pl.BlockSpec((META, PIX), lambda g: (0, 0)),
            pl.BlockSpec(
                (16, HALF, PIX), lambda g: (g % parts, jnp.minimum(g // parts, 1), 0)
            ),
        ],
        out_specs=pl.BlockSpec((HALF, 16, PIX), lambda g: (0, g, 0)),
        out_shape=jax.ShapeDtypeStruct((HALF, 2 * count + META, PIX), BF16),
        cost_estimate=pl.CostEstimate(
            flops=4 * 256 * count * HALF * PIX, bytes_accessed=8 * count * HALF * PIX, transcendentals=0
        ),
    )(exchange, about, tiles)


def coadd_kernel(row_ref, coadd_ref, sum_ref):
    sources = row_ref.shape[0]
    count = (row_ref.shape[1] - META) // 2
    numbers = lax.broadcasted_iota(jnp.int32, (BINS, PIX), 0).astype(F32)
    ones = jnp.ones((4 * count, PIX), BF16)
    running = jnp.zeros((BINS, 3 * PIX), F32)
    for first in range(0, sources, 4):
        loading = []
        for source in (first, first + 2):
            about = row_ref[source, 2 * count :, :].astype(F32) + row_ref[source + 1, 2 * count :, :].astype(F32)
            loading.append(jnp.where(about[0:1] == numbers, about[1:2], 0.0).astype(BF16))
        values = jnp.concatenate(
            [
                row_ref[first : first + 4, 0:count, :].reshape(4 * count, PIX),
                row_ref[first : first + 4, count : 2 * count, :].reshape(4 * count, PIX),
                ones,
            ],
            axis=1,
        )
        running = running + jnp.dot(
            jnp.concatenate(loading, axis=1), values, preferred_element_type=F32
        )
    weight_sum = running[:, 2 * PIX :]
    scale = jnp.maximum(weight_sum, 1.0)
    coadd_ref[0:BINS, :] = (running[:, :PIX] / scale).astype(BF16)
    coadd_ref[BINS:, :] = (running[:, PIX : 2 * PIX] / scale).astype(BF16)
    sum_ref[...] = weight_sum


def coadd_rows(rows):
    return pl.pallas_call(
        coadd_kernel,
        out_shape=(
            jax.ShapeDtypeStruct((2 * BINS, PIX), BF16),
            jax.ShapeDtypeStruct((BINS, PIX), F32),
        ),
        compiler_params=pltpu.CompilerParams(vmem_limit_bytes=24 * 1024 * 1024),
        cost_estimate=pl.CostEstimate(
            flops=6 * BINS * 4096 * PIX, bytes_accessed=4 * 4096 * PIX, transcendentals=0
        ),
    )(rows)


def detect_kernel(
    place_ref,
    coeff_ref,
    exchange_ref,
    gathered_ref,
    tile_ref,
    across_ref,
    down_ref,
    smoother_ref,
    out_ref,
    image_ref,
    window_ref,
    mixed_ref,
):
    exchange = exchange_ref[...]
    lane = lax.broadcasted_iota(jnp.int32, (SPAN, PIX), 1)
    row = lax.broadcasted_iota(jnp.int32, (SPAN, PIX), 0)
    tile_count = out_ref.shape[0]

    def regroup(block, carry):
        base = pl.multiple_of(block * 16, 16)
        for half in range(2):

            def read(number):
                start = pl.multiple_of(base + half * BINS, 16)
                return gathered_ref[number * 16 : number * 16 + 16, pl.ds(start, 16), :]

            def write(number, value):
                spot = half * HALF + number * 16
                image_ref[pl.ds(base, 16), spot : spot + 16, :] = value

            swap_blocks(exchange, read, write, HALF // 16)
        return carry

    lax.fori_loop(0, BINS // 16, regroup, 0)

    def group(number, carry):
        for local in range(GROUP):
            place = place_ref[number * GROUP + local]
            column = place // 128
            level = place % 128
            other = place + 128 - 256 * column
            outside = ((level == 0) & (row < HALO)) | ((level == 127) & (row >= HALO + PIX))
            wrong_side = (lane // 64) != column
            back = jnp.where(level == 0, 0, 1)
            ahead = jnp.where(level == 127, 0, 1)
            for spot, block, unwanted in ((0, place, outside), (PIX, other, outside | wrong_side)):
                value = jnp.concatenate(
                    [
                        image_ref[block - back, PIX - HALO :, :],
                        image_ref[block],
                        image_ref[block + ahead, 0:HALO, :],
                    ],
                    axis=0,
                )
                value = jnp.where(unwanted, 0.0, value.astype(F32)).astype(BF16)
                window_ref[local * SPAN : (local + 1) * SPAN, spot : spot + PIX] = value
        window = window_ref[...]
        for scale in range(3):
            members = [k for k, pair in enumerate(PAIRS) if pair[0] == scale]
            first, last = members[0], members[-1] + 1
            filtered = jnp.dot(
                window, across_ref[:, first * PIX : last * PIX], preferred_element_type=F32
            )
            for local in range(GROUP):
                rows = slice(local * SPAN, (local + 1) * SPAN)
                base = (number * GROUP + local) * NB
                for power_y in range(DEGREES[scale] + 1):
                    total = None
                    for power_x in range(DEGREES[scale] + 1 - power_y):
                        scalar = coeff_ref[base + BASIS.index((scale, power_x, power_y))]
                        term = scalar * filtered[rows, power_x * PIX : (power_x + 1) * PIX]
                        total = term if total is None else total + term
                    spot = (first + power_y) * SPAN
                    mixed_ref[spot : spot + SPAN, local * PIX : (local + 1) * PIX] = total.astype(BF16)
        begin = pl.multiple_of(number * GROUP, GROUP)
        tiles = tile_ref[pl.ds(begin, GROUP)].reshape(GROUP * PIX, PIX)
        smooth = jnp.dot(tiles, smoother_ref[...], preferred_element_type=F32).astype(BF16)
        spot = len(PAIRS) * SPAN
        for local in range(GROUP):
            mixed_ref[spot : spot + PIX, local * PIX : (local + 1) * PIX] = smooth[
                local * PIX : (local + 1) * PIX
            ]
        result = jnp.dot(down_ref[...], mixed_ref[...], preferred_element_type=F32)
        for local in range(GROUP):
            out_ref[begin + local] = result[:, local * PIX : (local + 1) * PIX].astype(BF16)
        return carry

    lax.fori_loop(0, tile_count // GROUP, group, 0)


def detect(place, coeff, exchange, gathered, tiles, across, down, smoother):
    tile_count = tiles.shape[0]
    depth = down.shape[1]
    smem = pl.BlockSpec(memory_space=pltpu.SMEM)
    vmem = pl.BlockSpec(memory_space=pltpu.VMEM)
    return pl.pallas_call(
        detect_kernel,
        in_specs=[smem, smem] + [vmem] * 6,
        out_specs=vmem,
        out_shape=jax.ShapeDtypeStruct((tile_count, PIX, PIX), BF16),
        scratch_shapes=[
            pltpu.VMEM((BINS, PIX, PIX), BF16),
            pltpu.VMEM((GROUP * SPAN, 2 * PIX), BF16),
            pltpu.VMEM((depth, GROUP * PIX), BF16),
        ],
        compiler_params=pltpu.CompilerParams(vmem_limit_bytes=48 * 1024 * 1024),
        cost_estimate=pl.CostEstimate(
            flops=2 * tile_count * (SPAN * 256 * 1408 + depth * PIX * PIX),
            bytes_accessed=12 * 1024 * 1024,
            transcendentals=0,
        ),
    )(place, coeff, exchange, gathered, tiles, across, down, smoother)


def body(visit_tiles, tile_patch, tile_slot, tile_weight, psf_coeff):
    tiles = visit_tiles[0]
    across, down, smoother = (jnp.asarray(m) for m in constants())
    exchange = jnp.asarray(exchange_matrix())
    patch = lax.axis_index("patch")
    patch_count = lax.axis_size("patch")
    band_count = lax.axis_size("band")
    place = (tile_slot[0] % 2) * 128 + 2 * tile_patch[0, :, 0] + tile_slot[0] // 2
    facts = jnp.stack([place.astype(F32), tile_weight[0].astype(F32)])
    even = (patch % 2) == 0
    facts = jnp.concatenate([jnp.where(even, facts, 0.0), jnp.where(even, 0.0, facts)], axis=1)
    about = jnp.pad(facts, ((0, META - 2), (0, 0))).astype(BF16)
    coeff = psf_coeff[0].astype(F32).reshape(-1)

    def exchanged(array, axis):
        return lax.all_to_all(array, axis, split_axis=0, concat_axis=0, tiled=True)

    rows = exchanged(pack(exchange, about, tiles), "patch")
    coadd, weight_sum = coadd_rows(rows)
    gathered = lax.all_gather(coadd, "patch", axis=0, tiled=False)

    own = coadd.reshape(4, patch_count, 2, PIX).transpose(1, 0, 2, 3).reshape(patch_count, 8, PIX)
    own = exchanged(own, "patch").reshape(HALF, 2, 2, 2, PIX)
    coadd_image = own.transpose(3, 1, 0, 2, 4)
    own_sum = lax.dynamic_slice_in_dim(weight_sum.reshape(2, 128, PIX), 2 * patch, 2, axis=1)
    own_sum = own_sum.transpose(1, 0, 2)[:, None, None]
    coadd_float = coadd_image.astype(F32)
    terms = (own_sum * coadd_float * coadd_float).reshape(SB * PIX, SB * PIX).astype(BF16)
    terms = exchanged(jnp.broadcast_to(terms[None], (band_count,) + terms.shape), "band")
    chi_image = jnp.sqrt(1.0 + jnp.sum(terms.astype(F32), axis=0)).astype(BF16)
    coadd_image = coadd_image.reshape(1, SB * PIX, SB * PIX)

    gathered, chi_image, coadd_image = lax.optimization_barrier((gathered, chi_image, coadd_image))
    detection = detect(place, coeff, exchange, gathered, tiles, across, down, smoother)
    return (coadd_image, detection[None], chi_image)


def solution(mesh):
    return jax.shard_map(
        body,
        mesh=mesh,
        in_specs=(
            P("band", "patch", None, None),
            P("band", "patch", None),
            P("band", "patch"),
            P("band", "patch"),
            P("band", "patch", None),
        ),
        out_specs=(P("band", "patch", None), P("band", "patch", None, None), P("patch", None)),
        check_vma=False,
    )
```

time: 323 us -> 229 us (0.71)
  waiting for transfers between devices: 150 us -> 71.6 us
  Pallas kernels: 44.4 us -> 37.6 us
  blocking collectives: 80.4 us -> 75.4 us
    all_gather x3 -> x1, waiting for transfers between devices: 150 us -> 48.6 us  [body(): gathered = lax.all_gather(coadd, 'patch', axis=0, tiled=False)]
    all_gather x1 -> x0, blocking collectives: 54 us -> none  [body(): about = lax.all_gather(about, 'patch', axis=0, tiled=True)]
    all_to_all x1, blocking collectives: 26.4 us -> 75.4 us  [exchanged(): return lax.all_to_all(array, axis, split_axis=0, concat_axis=0, tiled=True)]
    all_to_all x1 -> x2, waiting for transfers between devices: 0.01 us -> 23.1 us  [exchanged(): return lax.all_to_all(array, axis, split_axis=0, concat_axis=0, tiled=True)]
    pallas_call x6 -> x3, Pallas kernels: 44.4 us -> 37.6 us  [the longest x1 28.6 us: detect(): pl.pallas_call(detect_kernel, in_specs=[smem, smem] + [vmem] * 6, out_spe...]
    all_to_all x1 -> x2, starting transfers between devices: 17.1 us -> 18 us  [exchanged(): return lax.all_to_all(array, axis, split_axis=0, concat_axis=0, tiled=True)]
  transfers between devices with their start and end apart: 4 -> 3, of which waited for: 2 -> 3; matrix products, arithmetic and copies ran while one was open for 1% -> 4% of each run, Pallas kernels for 12% -> 0%
where the time goes in v2:
time: 229 us; the launch traced here: 228 us
  blocking collectives  75.4 us (33%)
  waiting for transfers between devices  71.6 us (31%)
  Pallas kernels  37.6 us (16%)
  starting transfers between devices  18.1 us (8%)
  between operations  14.2 us (6%)
  local copies, waits for them, and re-layouts  7.14 us (3%)
  other arithmetic  4.22 us (2%)
    all_to_all x1, blocking collectives, exchanged(): return lax.all_to_all(array, axis, split_axis=0, concat_axis=0, tiled=True)  75.4 us
    all_gather x1, waiting for transfers between devices, body(): gathered = lax.all_gather(coadd, 'patch', axis=0, tiled=False)  48.6 us
    pallas_call x1, Pallas kernels, detect(): pl.pallas_call(detect_kernel, in_specs=[smem, smem] + [vmem] * 6, out_spe...  28.6 us
    all_to_all x2, waiting for transfers between devices, exchanged(): return lax.all_to_all(array, axis, split_axis=0, concat_axis=0, tiled=True)  23.1 us
    all_to_all x2, starting transfers between devices, exchanged(): return lax.all_to_all(array, axis, split_axis=0, concat_axis=0, tiled=True)  18 us
    pallas_call x1, Pallas kernels, pack(): pl.pallas_call(pack_kernel, grid=(2 * parts + 1,), in_specs=[pl.BlockSpec...  7.03 us
  transfers between devices with their start and end apart: 3, of which 3 were waited for; matrix products, arithmetic and copies ran while one was open for 4% of the time, Pallas kernels for 0%

profile of v2, /device:TPU:1, one launch (start us, length us, event | category | flops | bytes accessed | tf_op | source)
XLA Modules:
  0.0 228.2 jit_solution(14936957493535855898)
XLA Ops:
  7.2 0.0 all-gather.3.cloned.1.call-start
  7.2 0.7 fusion.10
  7.9 0.7 select_convert_fusion.1
  8.6 0.7 fusion.3.about_ref
  9.2 7.0 %shard_map.112 = bf16[64,144,128]{2,1,0:T(8,128)(2,1)} custom-call(bf16[256,256]{1,0:T(8,128)(2,1)} %constant.63.clone.exchange_ref, bf16[16,128]{1,0:T(8,128)(2,1)} %fusion.3.about_ref, bf16[64,128,128]{2,1,0:T(8,128)(2,1)} %bitcast.37), custom_call_target="tpu_custom_call" | custom-call | flops 536870912 | bytes 4194304 | tf_op jit(solution)/shard_map/pallas_call | solution.py:105
  16.3 75.4 %all_to_all.15.row_ref = bf16[64,144,128]{2,1,0:T(8,128)(2,1)S(1)} all-to-all(bf16[64,144,128]{2,1,0:T(8,128)(2,1)} %shard_map.112), channel_id=1, replica_groups=mesh['patch'=64,'band'=8] {'patch'}, dimensions={0} | all-to-all | bytes 4718592 | tf_op jit(solution)/shard_map/all_to_all | solution.py:296
  91.7 1.9 shard_map.113
  93.6 0.0 all-gather.3.cloned.1.call-update
  93.6 0.9 copy.25
  94.5 0.7 copy.26
  95.3 0.0 copy-start.6
  95.3 0.0 copy-start.7
  95.3 0.0 copy-start.8
  95.3 10.5 %all-to-all-start.1 = ((bf16[64,8,128]{2,1,0:T(8,128)(2,1)}), bf16[64,8,128]{2,1,0:T(8,128)(2,1)S(1)}, u32[]{:S(2)}, u32[]{:S(2)}) async-start(bf16[64,8,128]{2,1,0:T(8,128)(2,1)} %copy.26), calls=%async_computation.1 | async-start | bytes 262144 | tf_op jit(solution)/shard_map/all_to_all | solution.py:296
  105.8 11.5 %all-to-all-done.1 = bf16[64,8,128]{2,1,0:T(8,128)(2,1)S(1)} async-done(((bf16[64,8,128]{2,1,0:T(8,128)(2,1)}), bf16[64,8,128]{2,1,0:T(8,128)(2,1)S(1)}, u32[]{:S(2)}, u32[]{:S(2)}) %all-to-all-start.1) | async-done | bytes 131104 | tf_op jit(solution)/shard_map/all_to_all | solution.py:296
  117.3 0.0 copy-start.5
  117.3 0.6 copy-done.5
  118.0 0.1 copy.28
  118.2 1.0 broadcast_in_dim.17
  119.2 0.0 copy-start
  119.2 0.0 copy-start.1
  119.2 0.0 copy-start.2
  119.2 0.0 copy-start.3
  119.2 0.0 copy-start.4
  119.2 7.6 %all-to-all-start.2 = ((bf16[8,256,256]{2,1,0:T(8,128)(2,1)}), bf16[8,256,256]{2,1,0:T(8,128)(2,1)}, u32[]{:S(2)}, u32[]{:S(2)}) async-start(bf16[8,256,256]{2,1,0:T(8,128)(2,1)} %broadcast_in_dim.17), calls=%async_computation.2 | async-start | bytes 2097152 | tf_op jit(solution)/shard_map/all_to_all | solution.py:296
  126.8 0.0 copy-done.6
  126.8 0.1 copy.30
  126.9 0.1 reshape.52.coeff_ref
  127.0 0.0 copy-done.7
  127.0 0.0 copy-done.8
  127.1 1.7 copy.29
  128.8 1.6 reshape.51
  130.4 11.6 %all-to-all-done.2 = bf16[8,256,256]{2,1,0:T(8,128)(2,1)} async-done(((bf16[8,256,256]{2,1,0:T(8,128)(2,1)}), bf16[8,256,256]{2,1,0:T(8,128)(2,1)}, u32[]{:S(2)}, u32[]{:S(2)}) %all-to-all-start.2) | async-done | bytes 1048608 | tf_op jit(solution)/shard_map/all_to_all | solution.py:296
  142.0 1.4 convert_reduce_fusion
  143.4 0.8 sqrt_convert_fusion
  144.1 48.6 %all-gather.3.cloned.1.call-done = bf16[32768,128]{1,0:T(8,128)(2,1)} async-done(((bf16[512,128]{1,0:T(8,128)(2,1)}), bf16[32768,128]{1,0:T(8,128)(2,1)}) %all-gather.3.cloned.1.call-update) | async-done | bytes 8388624 | tf_op jit(solution)/shard_map/all_gather | solution.py:300
  192.7 0.0 copy-done
  192.7 0.0 copy-done.1
  192.7 0.0 copy-done.2
  192.7 0.0 copy-done.3
  192.7 0.0 copy-done.4
  192.7 28.6 %shard_map.114 = bf16[64,128,128]{2,1,0:T(8,128)(2,1)} custom-call(s32[64]{0:T(128)S(1)} %fusion.9.place_ref, f32[1728]{0:T(1024)S(1)} %reshape.52.coeff_ref, bf16[256,256]{1,0:T(8,128)(2,1)S(1)} %copy-done.1, bf16[64,512,128]{2,1,0:T(8,128)(2,1)} %bitcast.45, bf16[64,128,128]{2,1,0:T(8,128)(2,1)S(1)} %bitcast.38, bf16[256,1408]{1,0:T(8,128)(2,1)S(1)} %copy-done.2, ...), custom_call_target="tpu_custom_call" | custom-call | flops 11341398016 | bytes 12582912 | tf_op jit(solution)/shard_map/pallas_call | solution.py:262
  (5 shorter events, 0.1 us)
Async XLA Ops:
  7.2 185.5 %all-gather.3.cloned.1.call-start = ((), (), s32[]{:S(2)}) async-start(), calls=%async_computation.3 | async-start | bytes 8519680 | tf_op jit(solution)/shard_map/all_gather | solution.py:300
  95.3 31.5 %copy-start.6 = (bf16[1,64,27]{1,2,0:T(8,128)(2,1)S(1)}, bf16[1,64,27]{1,2,0:T(8,128)(2,1)}, u32[]{:S(2)}) copy-start(bf16[1,64,27]{1,2,0:T(8,128)(2,1)} %param.13) | copy-start | bytes 10372
  95.3 31.8 %copy-start.7 = (s32[1,64]{1,0:T(1,128)S(1)}, s32[1,64]{1,0:T(1,128)}, u32[]{:S(2)}) copy-start(s32[1,64]{1,0:T(1,128)} %param.11) | copy-start | bytes 772
  95.3 31.8 %copy-start.8 = (s32[1,64,1]{1,2,0:T(1,128)S(1)}, s32[1,64,1]{1,2,0:T(1,128)}, u32[]{:S(2)}) copy-start(s32[1,64,1]{1,2,0:T(1,128)} %param.10) | copy-start | bytes 772
  95.3 22.0 %all-to-all-start.1 = ((bf16[64,8,128]{2,1,0:T(8,128)(2,1)}), bf16[64,8,128]{2,1,0:T(8,128)(2,1)S(1)}, u32[]{:S(2)}, u32[]{:S(2)}) async-start(bf16[64,8,128]{2,1,0:T(8,128)(2,1)} %copy.26), calls=%async_computation.1 | async-start | bytes 262144 | tf_op jit(solution)/shard_map/all_to_all | solution.py:296
  117.3 0.7 copy-start.5
  119.2 73.5 %copy-start = (bf16[1,64,128,128]{3,2,1,0:T(8,128)(2,1)S(1)}, bf16[1,64,128,128]{3,2,1,0:T(8,128)(2,1)}, u32[]{:S(2)}) copy-start(bf16[1,64,128,128]{3,2,1,0:T(8,128)(2,1)} %param.9) | copy-start | bytes 6291460
  119.2 73.5 %copy-start.1 = (bf16[256,256]{1,0:T(8,128)(2,1)S(1)}, bf16[256,256]{1,0:T(8,128)(2,1)}, u32[]{:S(2)}) copy-start(bf16[256,256]{1,0:T(8,128)(2,1)} %constant.63.clone.exchange_ref) | copy-start | bytes 393220
  119.2 73.5 %copy-start.2 = (bf16[256,1408]{1,0:T(8,128)(2,1)S(1)}, bf16[256,1408]{1,0:T(8,128)(2,1)}, u32[]{:S(2)}) copy-start(bf16[256,1408]{1,0:T(8,128)(2,1)} %constant.60.clone.across_ref) | copy-start | bytes 2162692
  119.2 73.5 %copy-start.3 = (bf16[128,1888]{1,0:T(8,128)(2,1)S(1)}, bf16[128,1888]{1,0:T(8,128)(2,1)}, u32[]{:S(2)}) copy-start(bf16[128,1888]{1,0:T(8,128)(2,1)} %constant.61.clone.down_ref) | copy-start | bytes 1449988
  119.2 73.5 %copy-start.4 = (bf16[128,128]{1,0:T(8,128)(2,1)S(1)}, bf16[128,128]{1,0:T(8,128)(2,1)}, u32[]{:S(2)}) copy-start(bf16[128,128]{1,0:T(8,128)(2,1)} %constant.62.clone.smoother_ref) | copy-start | bytes 98308
  119.2 22.8 %all-to-all-start.2 = ((bf16[8,256,256]{2,1,0:T(8,128)(2,1)}), bf16[8,256,256]{2,1,0:T(8,128)(2,1)}, u32[]{:S(2)}, u32[]{:S(2)}) async-start(bf16[8,256,256]{2,1,0:T(8,128)(2,1)} %broadcast_in_dim.17), calls=%async_computation.2 | async-start | bytes 2097152 | tf_op jit(solution)/shard_map/all_to_all | solution.py:296
Sparse Core Ops, SparseCore 0:
  93.7 98.9 all-gather.2

commit v3 on v2

--- a/solution.py
+++ b/solution.py
@@ -1,3 +1,5 @@
+import functools
+
 import jax
 import jax.numpy as jnp
 import ml_dtypes
@@ -16,6 +18,7 @@
 META = 16
 BINS = 256
 GROUP = 4
+BUFFERS = 2
 NB = 27
 SIGMAS = (0.7, 1.5, 3.0)
 DEGREES = (4, 2, 2)
@@ -81,102 +84,93 @@
         write(first + 1, moved[:, PIX:].reshape(16, 16, PIX))
 
 
-def pack_kernel(exchange_ref, about_ref, tile_ref, out_ref):
-    step = pl.program_id(0)
-
-    @pl.when(step < pl.num_programs(0) - 1)
-    def _():
+def pack_kernel(half, exchange_ref, *refs):
+    about_ref, tile_ref, out_ref = refs if len(refs) == 3 else (None,) + refs
+    exchange = exchange_ref[...]
+    count = tile_ref.shape[0]
+    for start in range(0, count, 16):
+
         def read(block):
-            return tile_ref[:, block * 16 : block * 16 + 16, :]
+            return tile_ref[start : start + 16, block * 16 : block * 16 + 16, :]
 
         def write(block, value):
-            out_ref[block * 16 : block * 16 + 16, :, :] = value
-
-        swap_blocks(exchange_ref[...], read, write, HALF // 16)
-
-    @pl.when(step == pl.num_programs(0) - 1)
-    def _():
-        out_ref[...] = jnp.broadcast_to(about_ref[...][None], out_ref.shape)
-
-
-def pack(exchange, about, tiles):
+            out_ref[block * 16 : block * 16 + 16, start : start + 16, :] = value
+
+        swap_blocks(exchange, read, write, HALF // 16)
+    if about_ref is not None:
+        about = about_ref[...]
+        for device in range(out_ref.shape[0]):
+            out_ref[device, count:, :] = about
+
+
+def pack(half, exchange, tiles, about=None):
     count = tiles.shape[0]
-    parts = count // 16
+    extra = 0 if about is None else META
+    whole = pl.BlockSpec(memory_space=pltpu.VMEM)
     return pl.pallas_call(
-        pack_kernel,
-        grid=(2 * parts + 1,),
-        in_specs=[
-            pl.BlockSpec((256, 256), lambda g: (0, 0)),
-            pl.BlockSpec((META, PIX), lambda g: (0, 0)),
-            pl.BlockSpec(
-                (16, HALF, PIX), lambda g: (g % parts, jnp.minimum(g // parts, 1), 0)
-            ),
-        ],
-        out_specs=pl.BlockSpec((HALF, 16, PIX), lambda g: (0, g, 0)),
-        out_shape=jax.ShapeDtypeStruct((HALF, 2 * count + META, PIX), BF16),
+        functools.partial(pack_kernel, half),
+        grid=(1,),
+        in_specs=[whole] * (1 if about is None else 2)
+        + [pl.BlockSpec((count, HALF, PIX), lambda g: (0, half, 0))],
+        out_specs=whole,
+        out_shape=jax.ShapeDtypeStruct((HALF, count + extra, PIX), BF16),
+        compiler_params=pltpu.CompilerParams(vmem_limit_bytes=24 * 1024 * 1024),
         cost_estimate=pl.CostEstimate(
-            flops=4 * 256 * count * HALF * PIX, bytes_accessed=8 * count * HALF * PIX, transcendentals=0
-        ),
-    )(exchange, about, tiles)
-
-
-def coadd_kernel(row_ref, coadd_ref, sum_ref):
-    sources = row_ref.shape[0]
-    count = (row_ref.shape[1] - META) // 2
+            flops=2 * 256 * count * HALF * PIX, bytes_accessed=4 * count * HALF * PIX, transcendentals=0
+        ),
+    )(*((exchange, tiles) if about is None else (exchange, about, tiles)))
+
+
+def coadd_kernel(about_ref, row_ref, coadd_ref, sum_ref):
+    sources, count = row_ref.shape[0], about_ref.shape[1] - META
     numbers = lax.broadcasted_iota(jnp.int32, (BINS, PIX), 0).astype(F32)
     ones = jnp.ones((4 * count, PIX), BF16)
-    running = jnp.zeros((BINS, 3 * PIX), F32)
+    running = jnp.zeros((BINS, 2 * PIX), F32)
     for first in range(0, sources, 4):
         loading = []
         for source in (first, first + 2):
-            about = row_ref[source, 2 * count :, :].astype(F32) + row_ref[source + 1, 2 * count :, :].astype(F32)
+            about = about_ref[source, count:, :].astype(F32) + about_ref[source + 1, count:, :].astype(F32)
             loading.append(jnp.where(about[0:1] == numbers, about[1:2], 0.0).astype(BF16))
         values = jnp.concatenate(
-            [
-                row_ref[first : first + 4, 0:count, :].reshape(4 * count, PIX),
-                row_ref[first : first + 4, count : 2 * count, :].reshape(4 * count, PIX),
-                ones,
-            ],
-            axis=1,
+            [row_ref[first : first + 4, 0:count, :].reshape(4 * count, PIX), ones], axis=1
         )
         running = running + jnp.dot(
             jnp.concatenate(loading, axis=1), values, preferred_element_type=F32
         )
-    weight_sum = running[:, 2 * PIX :]
-    scale = jnp.maximum(weight_sum, 1.0)
-    coadd_ref[0:BINS, :] = (running[:, :PIX] / scale).astype(BF16)
-    coadd_ref[BINS:, :] = (running[:, PIX : 2 * PIX] / scale).astype(BF16)
+    weight_sum = running[:, PIX:]
+    coadd_ref[...] = (running[:, :PIX] / jnp.maximum(weight_sum, 1.0)).astype(BF16)
     sum_ref[...] = weight_sum
 
 
-def coadd_rows(rows):
+def coadd_rows(about, rows):
     return pl.pallas_call(
         coadd_kernel,
         out_shape=(
-            jax.ShapeDtypeStruct((2 * BINS, PIX), BF16),
+            jax.ShapeDtypeStruct((BINS, PIX), BF16),
             jax.ShapeDtypeStruct((BINS, PIX), F32),
         ),
         compiler_params=pltpu.CompilerParams(vmem_limit_bytes=24 * 1024 * 1024),
         cost_estimate=pl.CostEstimate(
-            flops=6 * BINS * 4096 * PIX, bytes_accessed=4 * 4096 * PIX, transcendentals=0
-        ),
-    )(rows)
+            flops=4 * BINS * 4096 * PIX, bytes_accessed=4 * 4096 * PIX, transcendentals=0
+        ),
+    )(about, rows)
 
 
 def detect_kernel(
     place_ref,
     coeff_ref,
     exchange_ref,
-    gathered_ref,
+    upper_ref,
+    lower_ref,
     tile_ref,
     across_ref,
     down_ref,
     smoother_ref,
     out_ref,
     image_ref,
-    window_ref,
-    mixed_ref,
+    *scratch,
 ):
+    window_refs, mixed_refs = scratch[:BUFFERS], scratch[BUFFERS:]
     exchange = exchange_ref[...]
     lane = lax.broadcasted_iota(jnp.int32, (SPAN, PIX), 1)
     row = lax.broadcasted_iota(jnp.int32, (SPAN, PIX), 0)
@@ -184,11 +178,10 @@
 
     def regroup(block, carry):
         base = pl.multiple_of(block * 16, 16)
-        for half in range(2):
+        for half, gathered_ref in enumerate((upper_ref, lower_ref)):
 
             def read(number):
-                start = pl.multiple_of(base + half * BINS, 16)
-                return gathered_ref[number * 16 : number * 16 + 16, pl.ds(start, 16), :]
+                return gathered_ref[number * 16 : number * 16 + 16, pl.ds(base, 16), :]
 
             def write(number, value):
                 spot = half * HALF + number * 16
@@ -199,7 +192,7 @@
 
     lax.fori_loop(0, BINS // 16, regroup, 0)
 
-    def group(number, carry):
+    def group(number, window_ref, mixed_ref):
         for local in range(GROUP):
             place = place_ref[number * GROUP + local]
             column = place // 128
@@ -249,33 +242,59 @@
         result = jnp.dot(down_ref[...], mixed_ref[...], preferred_element_type=F32)
         for local in range(GROUP):
             out_ref[begin + local] = result[:, local * PIX : (local + 1) * PIX].astype(BF16)
+
+    def groups(number, carry):
+        for which in range(BUFFERS):
+            group(number * BUFFERS + which, window_refs[which], mixed_refs[which])
         return carry
 
-    lax.fori_loop(0, tile_count // GROUP, group, 0)
-
-
-def detect(place, coeff, exchange, gathered, tiles, across, down, smoother):
+    lax.fori_loop(0, tile_count // (GROUP * BUFFERS), groups, 0)
+
+
+def detect(place, coeff, exchange, upper, lower, tiles, across, down, smoother):
     tile_count = tiles.shape[0]
     depth = down.shape[1]
     smem = pl.BlockSpec(memory_space=pltpu.SMEM)
     vmem = pl.BlockSpec(memory_space=pltpu.VMEM)
     return pl.pallas_call(
         detect_kernel,
-        in_specs=[smem, smem] + [vmem] * 6,
+        in_specs=[smem, smem] + [vmem] * 7,
         out_specs=vmem,
         out_shape=jax.ShapeDtypeStruct((tile_count, PIX, PIX), BF16),
         scratch_shapes=[
             pltpu.VMEM((BINS, PIX, PIX), BF16),
-            pltpu.VMEM((GROUP * SPAN, 2 * PIX), BF16),
-            pltpu.VMEM((depth, GROUP * PIX), BF16),
-        ],
+        ]
+        + [pltpu.VMEM((GROUP * SPAN, 2 * PIX), BF16)] * BUFFERS
+        + [pltpu.VMEM((depth, GROUP * PIX), BF16)] * BUFFERS,
         compiler_params=pltpu.CompilerParams(vmem_limit_bytes=48 * 1024 * 1024),
         cost_estimate=pl.CostEstimate(
             flops=2 * tile_count * (SPAN * 256 * 1408 + depth * PIX * PIX),
             bytes_accessed=12 * 1024 * 1024,
             transcendentals=0,
         ),
-    )(place, coeff, exchange, gathered, tiles, across, down, smoother)
+    )(place, coeff, exchange, upper, lower, tiles, across, down, smoother)
+
+
+SIDE = 8
+
+
+def ring_gather(block, row, axis):
+    up = [(p, (p + SIDE) % (SIDE * SIDE)) for p in range(SIDE * SIDE)]
+    down = [(q, p) for p, q in up]
+    result = jnp.zeros((SIDE,) + block.shape, block.dtype)
+
+    def put(array, piece, offset, start=0):
+        spot = lax.rem(row + offset + SIDE, SIDE)
+        return lax.dynamic_update_slice(array, piece[None], (spot, start) + (0,) * (block.ndim - 1))
+
+    result = put(result, block, 0)
+    rising = falling = block
+    for step in range(1, SIDE // 2):
+        rising, falling = lax.ppermute(rising, axis, up), lax.ppermute(falling, axis, down)
+        result = put(put(result, rising, -step), falling, step)
+    middle = block.shape[0] // 2
+    result = put(result, lax.ppermute(rising[:middle], axis, up), SIDE // 2)
+    return put(result, lax.ppermute(falling[middle:], axis, down), SIDE // 2, middle)
 
 
 def body(visit_tiles, tile_patch, tile_slot, tile_weight, psf_coeff):
@@ -283,8 +302,6 @@
     across, down, smoother = (jnp.asarray(m) for m in constants())
     exchange = jnp.asarray(exchange_matrix())
     patch = lax.axis_index("patch")
-    patch_count = lax.axis_size("patch")
-    band_count = lax.axis_size("band")
     place = (tile_slot[0] % 2) * 128 + 2 * tile_patch[0, :, 0] + tile_slot[0] // 2
     facts = jnp.stack([place.astype(F32), tile_weight[0].astype(F32)])
     even = (patch % 2) == 0
@@ -292,27 +309,35 @@
     about = jnp.pad(facts, ((0, META - 2), (0, 0))).astype(BF16)
     coeff = psf_coeff[0].astype(F32).reshape(-1)
 
-    def exchanged(array, axis):
-        return lax.all_to_all(array, axis, split_axis=0, concat_axis=0, tiled=True)
-
-    rows = exchanged(pack(exchange, about, tiles), "patch")
-    coadd, weight_sum = coadd_rows(rows)
-    gathered = lax.all_gather(coadd, "patch", axis=0, tiled=False)
-
-    own = coadd.reshape(4, patch_count, 2, PIX).transpose(1, 0, 2, 3).reshape(patch_count, 8, PIX)
-    own = exchanged(own, "patch").reshape(HALF, 2, 2, 2, PIX)
-    coadd_image = own.transpose(3, 1, 0, 2, 4)
+    def exchanged(array, groups=None):
+        return lax.all_to_all(
+            array, "patch", split_axis=0, concat_axis=0, tiled=True, axis_index_groups=groups
+        )
+
+    upper_rows = exchanged(pack(0, exchange, tiles, about))
+    upper_coadd, weight_sum = coadd_rows(upper_rows, upper_rows)
+    lower_packed, upper_coadd = lax.optimization_barrier((pack(1, exchange, tiles), upper_coadd))
+    upper = lax.all_gather(upper_coadd, "patch", axis=0, tiled=False)
+
+    lower_coadd, _ = coadd_rows(upper_rows, exchanged(lower_packed))
+    along = [[y * SIDE + z for z in range(SIDE)] for y in range(SIDE)]
+    lower = exchanged(jnp.broadcast_to(lower_coadd[None], (SIDE,) + lower_coadd.shape), along)
+    lower = ring_gather(lower, patch // SIDE, "patch").reshape(SIDE * SIDE, BINS, PIX)
+
+    detection = detect(place, coeff, exchange, upper, lower, tiles, across, down, smoother)
+
+    def own_part(gathered):
+        shaped = gathered.reshape(HALF, 2, 128, PIX)
+        return lax.dynamic_slice_in_dim(shaped, 2 * patch, 2, axis=2).transpose(2, 0, 1, 3)
+
+    coadd_image = jnp.stack([own_part(upper), own_part(lower)], axis=1)
     own_sum = lax.dynamic_slice_in_dim(weight_sum.reshape(2, 128, PIX), 2 * patch, 2, axis=1)
     own_sum = own_sum.transpose(1, 0, 2)[:, None, None]
     coadd_float = coadd_image.astype(F32)
     terms = (own_sum * coadd_float * coadd_float).reshape(SB * PIX, SB * PIX).astype(BF16)
-    terms = exchanged(jnp.broadcast_to(terms[None], (band_count,) + terms.shape), "band")
+    terms = lax.all_gather(terms, "band", axis=0, tiled=False)
     chi_image = jnp.sqrt(1.0 + jnp.sum(terms.astype(F32), axis=0)).astype(BF16)
-    coadd_image = coadd_image.reshape(1, SB * PIX, SB * PIX)
-
-    gathered, chi_image, coadd_image = lax.optimization_barrier((gathered, chi_image, coadd_image))
-    detection = detect(place, coeff, exchange, gathered, tiles, across, down, smoother)
-    return (coadd_image, detection[None], chi_image)
+    return (coadd_image.reshape(1, SB * PIX, SB * PIX), detection[None], chi_image)
 
 
 def solution(mesh):

time: 229 us -> 244 us (1.066); the launches traced: 228 us -> 240 us
  starting transfers between devices: 18.1 us -> 51.4 us
  blocking collectives: 75.4 us -> 54.8 us
  local copies, waits for them, and re-layouts: 7.14 us -> 18.2 us
  waiting for transfers between devices: 71.6 us -> 64.3 us
  Pallas kernels: 37.6 us -> 31.2 us
    all_gather x1 -> x2, waiting for transfers between devices: 48.6 us -> 8.06 us  [the longest x1 8.04 us: body(): terms = lax.all_gather(terms, 'band', axis=0, tiled=False)]
    ppermute x0 -> x8, starting transfers between devices: none -> 34.2 us  [the longest x3 21.3 us: ring_gather(): lax.ppermute(falling, axis, down)]
    ppermute x0 -> x8, waiting for transfers between devices: none -> 25.6 us  [the longest x3 20.1 us: ring_gather(): lax.ppermute(rising, axis, up)]
    all_to_all x1 -> x2, blocking collectives: 75.4 us -> 54.8 us  [exchanged(): lax.all_to_all(array, 'patch', split_axis=0, concat_axis=0, tiled=True, a...]
    all_to_all x2 -> x1, waiting for transfers between devices: 23.1 us -> 30.6 us  [exchanged(): lax.all_to_all(array, 'patch', split_axis=0, concat_axis=0, tiled=True, a...]
    unnamed x19 -> x30, local copies, waits for them, and re-layouts: 0.7 us -> 7.88 us
    pallas_call x3 -> x5, Pallas kernels: 37.6 us -> 31.2 us  [the longest x1 28.2 us: detect(): pl.pallas_call(detect_kernel, in_specs=[smem, smem] + [vmem] * 7, out_spe...]
    dynamic_update_slice x0 -> x9, local copies, waits for them, and re-layouts: none -> 3.82 us  [put(): lax.dynamic_update_slice(array, piece[None], (spot, start) + (0,) * (bloc...]
  transfers between devices with their start and end apart: 3 -> 11, of which waited for: 3 -> 7; matrix products, arithmetic and copies ran while one was open for 4% -> 3% of each run, Pallas kernels for 0% -> 13%
where the time goes in v3:
time: 244 us; the launch traced here: 240 us
  waiting for transfers between devices  64.3 us (26%)
  blocking collectives  54.8 us (22%)
  starting transfers between devices  51.4 us (21%)
  Pallas kernels  31.2 us (13%)
  local copies, waits for them, and re-layouts  18.2 us (7%)
  between operations  14.6 us (6%)
  other arithmetic  5.45 us (2%)
    all_to_all x2, blocking collectives, exchanged(): lax.all_to_all(array, 'patch', split_axis=0, concat_axis=0, tiled=True, a...  54.8 us
    all_to_all x1, waiting for transfers between devices, exchanged(): lax.all_to_all(array, 'patch', split_axis=0, concat_axis=0, tiled=True, a...  30.6 us
    pallas_call x1, Pallas kernels, detect(): pl.pallas_call(detect_kernel, in_specs=[smem, smem] + [vmem] * 7, out_spe...  28.2 us
    ppermute x3, starting transfers between devices, ring_gather(): lax.ppermute(falling, axis, down)  21.3 us
    ppermute x3, waiting for transfers between devices, ring_gather(): lax.ppermute(rising, axis, up)  20.1 us
    all_to_all x1, starting transfers between devices, exchanged(): lax.all_to_all(array, 'patch', split_axis=0, concat_axis=0, tiled=True, a...  17.1 us
    all_gather x1, waiting for transfers between devices, body(): terms = lax.all_gather(terms, 'band', axis=0, tiled=False)  8.04 us
    unnamed x30, local copies, waits for them, and re-layouts  7.88 us
  transfers between devices with their start and end apart: 11, of which 7 were waited for; matrix products, arithmetic and copies ran while one was open for 3% of the time, Pallas kernels for 13%

profile of v3, /device:TPU:1, one launch (start us, length us, event | category | flops | bytes accessed | tf_op | source)
XLA Modules:
  0.0 239.9 jit_solution(7978073186651652109)
XLA Ops:
  7.2 0.7 fusion.11
  7.9 0.7 select_convert_fusion.1
  8.5 0.1 fusion.3.refs_0_
  8.6 1.6 copy-done
  10.2 0.9 copy-done.4
  11.1 0.5 shard_map.113
  11.6 1.0 copy-done.2
  12.7 17.1 %all-to-all-start = ((bf16[64,80,128]{2,1,0:T(8,128)(2,1)}), bf16[64,80,128]{2,1,0:T(8,128)(2,1)S(1)}, u32[]{:S(2)}, u32[]{:S(2)}) async-start(bf16[64,80,128]{2,1,0:T(8,128)(2,1)} %copy-done.2), calls=%async_computation | async-start | bytes 2621440 | tf_op jit(solution)/shard_map/all_to_all | solution.py:313
  29.8 0.0 all-gather.6.cloned.1.call-start
  29.9 0.5 shard_map.112
  30.3 1.0 copy-done.3
  31.4 30.6 %all-to-all-done.about_ref.row_ref = bf16[64,80,128]{2,1,0:T(8,128)(2,1)S(1)} async-done(((bf16[64,80,128]{2,1,0:T(8,128)(2,1)}), bf16[64,80,128]{2,1,0:T(8,128)(2,1)S(1)}, u32[]{:S(2)}, u32[]{:S(2)}) %all-to-all-start) | async-done | bytes 1310752 | tf_op jit(solution)/shard_map/all_to_all | solution.py:313
  62.0 0.7 shard_map.114
  62.7 0.6 copy-done.6
  63.3 0.7 copy-done.7
  64.0 0.0 all-gather.6.cloned.1.call-update
  64.0 0.0 all-gather.4.cloned.1.call-start
  64.0 36.2 %all_to_all.15.row_ref = bf16[64,64,128]{2,1,0:T(8,128)(2,1)S(1)} all-to-all(bf16[64,64,128]{2,1,0:T(8,128)(2,1)} %copy-done.3), channel_id=1, replica_groups=mesh['patch'=64,'band'=8] {'patch'}, dimensions={0} | all-to-all | bytes 2097152 | tf_op jit(solution)/shard_map/all_to_all | solution.py:313
  100.2 1.4 shard_map.115
  101.6 0.1 broadcast_in_dim.48
  101.7 18.6 %all_to_all.16 = bf16[8,256,128]{2,1,0:T(8,128)(2,1)S(1)} all-to-all(bf16[8,256,128]{2,1,0:T(8,128)(2,1)S(1)} %broadcast_in_dim.48), channel_id=1, replica_groups={{0,8,16,24,32,40,48,56},{64,72,80,88,96,104,112,120},{128,136,144,152,1..., dimensions={0} | all-to-all | bytes 1048576 | tf_op jit(solution)/shard_map/all_to_all | solution.py:313
  120.3 2.6 %collective-permute-start = (bf16[8,256,128]{2,1,0:T(8,128)(2,1)S(1)}, bf16[8,256,128]{2,1,0:T(8,128)(2,1)}, u32[]{:S(2)}, u32[]{:S(2)}) collective-permute-start(bf16[8,256,128]{2,1,0:T(8,128)(2,1)S(1)} %all_to_all.16), channel_id=1, source_target_pairs={{0,64},{8,72},{16,80},{24,88},{32,96},{40,104},{48,112},{56,120},{... | collective-permute-start | bytes 1572872 | tf_op jit(solution)/shard_map/ppermute | solution.py:293
  122.9 3.9 %collective-permute-start.1 = (bf16[8,256,128]{2,1,0:T(8,128)(2,1)S(1)}, bf16[8,256,128]{2,1,0:T(8,128)(2,1)S(1)}, u32[]{:S(2)}, u32[]{:S(2)}) collective-permute-start(bf16[8,256,128]{2,1,0:T(8,128)(2,1)S(1)} %all_to_all.16), channel_id=1, source_target_pairs={{64,0},{72,8},{80,16},{88,24},{96,32},{104,40},{112,48},{120,56},{... | collective-permute-start | bytes 1572872 | tf_op jit(solution)/shard_map/ppermute | solution.py:293
  126.9 5.0 %collective-permute-done = bf16[8,256,128]{2,1,0:T(8,128)(2,1)} collective-permute-done((bf16[8,256,128]{2,1,0:T(8,128)(2,1)S(1)}, bf16[8,256,128]{2,1,0:T(8,128)(2,1)}, u32[]{:S(2)}, u32[]{:S(2)}) %collective-permute-start) | collective-permute-done | bytes 524320 | tf_op jit(solution)/shard_map/ppermute | solution.py:293
  131.8 1.9 collective-permute-start.2
  133.8 9.5 %collective-permute-start.3 = (bf16[8,256,128]{2,1,0:T(8,128)(2,1)S(1)}, bf16[8,256,128]{2,1,0:T(8,128)(2,1)}, u32[]{:S(2)}, u32[]{:S(2)}) collective-permute-start(bf16[8,256,128]{2,1,0:T(8,128)(2,1)S(1)} %collective-permute-done.1), channel_id=1, source_target_pairs={{64,0},{72,8},{80,16},{88,24},{96,32},{104,40},{112,48},{120,56},{... | collective-permute-start | bytes 1572872 | tf_op jit(solution)/shard_map/ppermute | solution.py:293
  143.3 0.7 fusion.4
  144.1 0.1 mul.70
  144.1 0.9 mul.71
  145.0 1.0 broadcast_in_dim.47
  146.1 0.1 bitcast_dynamic-update-slice_fusion.6
  146.1 1.1 bitcast_dynamic-update-slice_fusion.5
  147.3 11.3 %collective-permute-done.2 = bf16[8,256,128]{2,1,0:T(8,128)(2,1)} collective-permute-done((bf16[8,256,128]{2,1,0:T(8,128)(2,1)}, bf16[8,256,128]{2,1,0:T(8,128)(2,1)}, u32[]{:S(2)}, u32[]{:S(2)}) %collective-permute-start.2) | collective-permute-done | bytes 524320 | tf_op jit(solution)/shard_map/ppermute | solution.py:293
  158.6 1.9 collective-permute-start.4
  160.5 7.8 %collective-permute-start.5 = (bf16[8,256,128]{2,1,0:T(8,128)(2,1)}, bf16[8,256,128]{2,1,0:T(8,128)(2,1)S(1)}, u32[]{:S(2)}, u32[]{:S(2)}) collective-permute-start(bf16[8,256,128]{2,1,0:T(8,128)(2,1)} %collective-permute-done.3), channel_id=1, source_target_pairs={{64,0},{72,8},{80,16},{88,24},{96,32},{104,40},{112,48},{120,56},{... | collective-permute-start | bytes 1572872 | tf_op jit(solution)/shard_map/ppermute | solution.py:293
  168.3 0.1 bitcast_dynamic-update-slice_fusion.4
  168.4 0.0 copy-start.12
  168.4 0.0 copy-start.8
  168.4 0.0 copy-start.9
  168.5 0.0 copy-start.10
  168.5 1.2 bitcast_dynamic-update-slice_fusion.3
  169.7 1.1 bitcast_dynamic-update-slice_fusion.2
  170.8 3.8 %collective-permute-done.4 = bf16[8,256,128]{2,1,0:T(8,128)(2,1)S(1)} collective-permute-done((bf16[8,256,128]{2,1,0:T(8,128)(2,1)}, bf16[8,256,128]{2,1,0:T(8,128)(2,1)S(1)}, u32[]{:S(2)}, u32[]{:S(2)}) %collective-permute-start.4) | collective-permute-done | bytes 524320 | tf_op jit(solution)/shard_map/ppermute | solution.py:293
  174.7 1.9 collective-permute-start.6
  176.6 4.6 %collective-permute-start.7 = (bf16[4,256,128]{2,1,0:T(8,128)(2,1)S(1)}, bf16[4,256,128]{2,1,0:T(8,128)(2,1)S(1)}, u32[]{:S(2)}, u32[]{:S(2)}) collective-permute-start(bf16[4,256,128]{2,1,0:T(8,128)(2,1)S(1)} %slice.9), channel_id=1, source_target_pairs={{64,0},{72,8},{80,16},{88,24},{96,32},{104,40},{112,48},{120,56},{... | collective-permute-start | bytes 786440 | tf_op jit(solution)/shard_map/ppermute | solution.py:297
  181.2 0.1 bitcast_dynamic-update-slice_fusion.1
  181.3 0.1 bitcast_dynamic-update-slice_fusion
  181.4 3.8 %collective-permute-done.6 = bf16[4,256,128]{2,1,0:T(8,128)(2,1)S(1)} collective-permute-done((bf16[4,256,128]{2,1,0:T(8,128)(2,1)S(1)}, bf16[4,256,128]{2,1,0:T(8,128)(2,1)S(1)}, u32[]{:S(2)}, u32[]{:S(2)}) %collective-permute-start.6) | collective-permute-done | bytes 262176 | tf_op jit(solution)/shard_map/ppermute | solution.py:296
  185.2 1.7 collective-permute-done.7
  187.0 2.0 copy-done.11
  189.0 0.1 dynamic-slice_bitcast_fusion
  189.1 0.0 all-gather.6.cloned.1.call-done
  189.1 1.0 dynamic-slice_bitcast_fusion.1
  190.2 0.2 pad_maximum_fusion
  190.4 0.7 copy.17
  191.1 1.6 reshape.68
  192.7 1.7 fusion
  194.4 0.0 all-gather.4.cloned.1.call-update
  194.4 0.1 copy.18
  194.5 0.1 reshape.71.coeff_ref
  194.7 28.2 %shard_map.116 = bf16[64,128,128]{2,1,0:T(8,128)(2,1)} custom-call(s32[64]{0:T(128)S(1)} %fusion.10.place_ref, f32[1728]{0:T(1024)S(1)} %reshape.71.coeff_ref, bf16[256,256]{1,0:T(8,128)(2,1)S(1)} %copy-done.5, bf16[64,256,128]{2,1,0:T(8,128)(2,1)} %bitcast.61, bf16[64,256,128]{2,1,0:T(8,128)(2,1)} %bitcast.59, bf16[64,128,128]{2,1,0:T(8,128)(2,1)S(1)} %bitcast.56, ...), custom_call_target="tpu_custom_call" | custom-call | flops 11341398016 | bytes 12582912 | tf_op jit(solution)/shard_map/pallas_call | solution.py:259
  222.9 8.0 %all-gather.4.cloned.1.call-done = bf16[8,256,256]{2,1,0:T(8,128)(2,1)} async-done(((bf16[1,256,256]{2,1,0:T(8,128)(2,1)}), bf16[8,256,256]{2,1,0:T(8,128)(2,1)}) %all-gather.4.cloned.1.call-update) | async-done | bytes 1048592 | tf_op jit(solution)/shard_map/all_gather | solution.py:338
  230.9 1.4 convert_reduce_fusion
  232.3 0.8 sqrt_convert_fusion
  (28 shorter events, 0.2 us)
Async XLA Ops:
  8.6 1.6 copy-start
  10.2 0.9 copy-start.4
  11.1 18.7 %copy-start.1 = (bf16[1,64,128,128]{3,2,1,0:T(8,128)(2,1)S(1)}, bf16[1,64,128,128]{3,2,1,0:T(8,128)(2,1)}, u32[]{:S(2)}) copy-start(bf16[1,64,128,128]{3,2,1,0:T(8,128)(2,1)} %param.9) | copy-start | bytes 6291460
  11.1 18.7 %copy-start.5 = (bf16[256,256]{1,0:T(8,128)(2,1)S(1)}, bf16[256,256]{1,0:T(8,128)(2,1)}, u32[]{:S(2)}) copy-start(bf16[256,256]{1,0:T(8,128)(2,1)} %constant.114.clone.exchange_ref) | copy-start | bytes 393220
  11.6 1.1 copy-start.2
  12.7 49.3 %all-to-all-start = ((bf16[64,80,128]{2,1,0:T(8,128)(2,1)}), bf16[64,80,128]{2,1,0:T(8,128)(2,1)S(1)}, u32[]{:S(2)}, u32[]{:S(2)}) async-start(bf16[64,80,128]{2,1,0:T(8,128)(2,1)} %copy-done.2), calls=%async_computation | async-start | bytes 2621440 | tf_op jit(solution)/shard_map/all_to_all | solution.py:313
  29.8 159.3 %all-gather.6.cloned.1.call-start = ((), (), s32[]{:S(2)}) async-start(), calls=%async_computation.4 | async-start | bytes 4259840 | tf_op jit(solution)/shard_map/all_gather | solution.py:320
  30.3 1.0 copy-start.3
  62.7 0.6 copy-start.6
  63.3 0.7 copy-start.7
  64.0 166.9 %all-gather.4.cloned.1.call-start = ((), (), s32[]{:S(2)}) async-start(), calls=%async_computation.3 | async-start | bytes 1179648 | tf_op jit(solution)/shard_map/all_gather | solution.py:338
  120.3 11.6 %collective-permute-start = (bf16[8,256,128]{2,1,0:T(8,128)(2,1)S(1)}, bf16[8,256,128]{2,1,0:T(8,128)(2,1)}, u32[]{:S(2)}, u32[]{:S(2)}) collective-permute-start(bf16[8,256,128]{2,1,0:T(8,128)(2,1)S(1)} %all_to_all.16), channel_id=1, source_target_pairs={{0,64},{8,72},{16,80},{24,88},{32,96},{40,104},{48,112},{56,120},{... | collective-permute-start | bytes 1572872 | tf_op jit(solution)/shard_map/ppermute | solution.py:293
  122.9 10.9 %collective-permute-start.1 = (bf16[8,256,128]{2,1,0:T(8,128)(2,1)S(1)}, bf16[8,256,128]{2,1,0:T(8,128)(2,1)S(1)}, u32[]{:S(2)}, u32[]{:S(2)}) collective-permute-start(bf16[8,256,128]{2,1,0:T(8,128)(2,1)S(1)} %all_to_all.16), channel_id=1, source_target_pairs={{64,0},{72,8},{80,16},{88,24},{96,32},{104,40},{112,48},{120,56},{... | collective-permute-start | bytes 1572872 | tf_op jit(solution)/shard_map/ppermute | solution.py:293
  131.8 26.7 %collective-permute-start.2 = (bf16[8,256,128]{2,1,0:T(8,128)(2,1)}, bf16[8,256,128]{2,1,0:T(8,128)(2,1)}, u32[]{:S(2)}, u32[]{:S(2)}) collective-permute-start(bf16[8,256,128]{2,1,0:T(8,128)(2,1)} %collective-permute-done), channel_id=1, source_target_pairs={{0,64},{8,72},{16,80},{24,88},{32,96},{40,104},{48,112},{56,120},{... | collective-permute-start | bytes 1572872 | tf_op jit(solution)/shard_map/ppermute | solution.py:293
  133.8 26.7 %collective-permute-start.3 = (bf16[8,256,128]{2,1,0:T(8,128)(2,1)S(1)}, bf16[8,256,128]{2,1,0:T(8,128)(2,1)}, u32[]{:S(2)}, u32[]{:S(2)}) collective-permute-start(bf16[8,256,128]{2,1,0:T(8,128)(2,1)S(1)} %collective-permute-done.1), channel_id=1, source_target_pairs={{64,0},{72,8},{80,16},{88,24},{96,32},{104,40},{112,48},{120,56},{... | collective-permute-start | bytes 1572872 | tf_op jit(solution)/shard_map/ppermute | solution.py:293
  158.6 16.1 %collective-permute-start.4 = (bf16[8,256,128]{2,1,0:T(8,128)(2,1)}, bf16[8,256,128]{2,1,0:T(8,128)(2,1)S(1)}, u32[]{:S(2)}, u32[]{:S(2)}) collective-permute-start(bf16[8,256,128]{2,1,0:T(8,128)(2,1)} %collective-permute-done.2), channel_id=1, source_target_pairs={{0,64},{8,72},{16,80},{24,88},{32,96},{40,104},{48,112},{56,120},{... | collective-permute-start | bytes 1572872 | tf_op jit(solution)/shard_map/ppermute | solution.py:293
  160.5 16.1 %collective-permute-start.5 = (bf16[8,256,128]{2,1,0:T(8,128)(2,1)}, bf16[8,256,128]{2,1,0:T(8,128)(2,1)S(1)}, u32[]{:S(2)}, u32[]{:S(2)}) collective-permute-start(bf16[8,256,128]{2,1,0:T(8,128)(2,1)} %collective-permute-done.3), channel_id=1, source_target_pairs={{64,0},{72,8},{80,16},{88,24},{96,32},{104,40},{112,48},{120,56},{... | collective-permute-start | bytes 1572872 | tf_op jit(solution)/shard_map/ppermute | solution.py:293
  168.4 26.0 %copy-start.12 = (bf16[1,64,27]{1,2,0:T(8,128)(2,1)S(1)}, bf16[1,64,27]{1,2,0:T(8,128)(2,1)}, u32[]{:S(2)}) copy-start(bf16[1,64,27]{1,2,0:T(8,128)(2,1)} %param.13) | copy-start | bytes 10372
  168.4 26.3 %copy-start.13 = (s32[1,64]{1,0:T(1,128)S(1)}, s32[1,64]{1,0:T(1,128)}, u32[]{:S(2)}) copy-start(s32[1,64]{1,0:T(1,128)} %param.11) | copy-start | bytes 772
  168.4 26.3 %copy-start.14 = (s32[1,64,1]{1,2,0:T(1,128)S(1)}, s32[1,64,1]{1,2,0:T(1,128)}, u32[]{:S(2)}) copy-start(s32[1,64,1]{1,2,0:T(1,128)} %param.10) | copy-start | bytes 772
  168.4 26.3 %copy-start.8 = (bf16[256,1408]{1,0:T(8,128)(2,1)S(1)}, bf16[256,1408]{1,0:T(8,128)(2,1)}, u32[]{:S(2)}) copy-start(bf16[256,1408]{1,0:T(8,128)(2,1)} %constant.111.clone.across_ref) | copy-start | bytes 2162692
  168.4 26.3 %copy-start.9 = (bf16[128,1888]{1,0:T(8,128)(2,1)S(1)}, bf16[128,1888]{1,0:T(8,128)(2,1)}, u32[]{:S(2)}) copy-start(bf16[128,1888]{1,0:T(8,128)(2,1)} %constant.112.clone.down_ref) | copy-start | bytes 1449988
  168.5 26.3 %copy-start.10 = (bf16[128,128]{1,0:T(8,128)(2,1)S(1)}, bf16[128,128]{1,0:T(8,128)(2,1)}, u32[]{:S(2)}) copy-start(bf16[128,128]{1,0:T(8,128)(2,1)} %constant.113.clone.smoother_ref) | copy-start | bytes 98308
  174.7 10.5 %collective-permute-start.6 = (bf16[4,256,128]{2,1,0:T(8,128)(2,1)S(1)}, bf16[4,256,128]{2,1,0:T(8,128)(2,1)S(1)}, u32[]{:S(2)}, u32[]{:S(2)}) collective-permute-start(bf16[4,256,128]{2,1,0:T(8,128)(2,1)S(1)} %slice.8), channel_id=1, source_target_pairs={{0,64},{8,72},{16,80},{24,88},{32,96},{40,104},{48,112},{56,120},{... | collective-permute-start | bytes 786440 | tf_op jit(solution)/shard_map/ppermute | solution.py:296
  176.6 10.3 %collective-permute-start.7 = (bf16[4,256,128]{2,1,0:T(8,128)(2,1)S(1)}, bf16[4,256,128]{2,1,0:T(8,128)(2,1)S(1)}, u32[]{:S(2)}, u32[]{:S(2)}) collective-permute-start(bf16[4,256,128]{2,1,0:T(8,128)(2,1)S(1)} %slice.9), channel_id=1, source_target_pairs={{64,0},{72,8},{80,16},{88,24},{96,32},{104,40},{112,48},{120,56},{... | collective-permute-start | bytes 786440 | tf_op jit(solution)/shard_map/ppermute | solution.py:297
  187.0 2.0 copy-start.11
Sparse Core Ops, SparseCore 0:
  64.1 106.5 all-gather.5
  194.5 36.3 all-gather.3

commit v4 on v2

--- a/solution.py
+++ b/solution.py
@@ -16,6 +16,7 @@
 META = 16
 BINS = 256
 GROUP = 4
+BUFFERS = 2
 NB = 27
 SIGMAS = (0.7, 1.5, 3.0)
 DEGREES = (4, 2, 2)
@@ -82,38 +83,31 @@
 
 
 def pack_kernel(exchange_ref, about_ref, tile_ref, out_ref):
-    step = pl.program_id(0)
-
-    @pl.when(step < pl.num_programs(0) - 1)
-    def _():
-        def read(block):
-            return tile_ref[:, block * 16 : block * 16 + 16, :]
-
-        def write(block, value):
-            out_ref[block * 16 : block * 16 + 16, :, :] = value
-
-        swap_blocks(exchange_ref[...], read, write, HALF // 16)
-
-    @pl.when(step == pl.num_programs(0) - 1)
-    def _():
-        out_ref[...] = jnp.broadcast_to(about_ref[...][None], out_ref.shape)
+    exchange = exchange_ref[...]
+    count = tile_ref.shape[0]
+    for half in range(2):
+        for start in range(0, count, 16):
+
+            def read(block):
+                spot = half * HALF + block * 16
+                return tile_ref[start : start + 16, spot : spot + 16, :]
+
+            def write(block, value):
+                spot = half * count + start
+                out_ref[block * 16 : block * 16 + 16, spot : spot + 16, :] = value
+
+            swap_blocks(exchange, read, write, HALF // 16)
+    about = about_ref[...]
+    for device in range(out_ref.shape[0]):
+        out_ref[device, 2 * count :, :] = about
 
 
 def pack(exchange, about, tiles):
     count = tiles.shape[0]
-    parts = count // 16
     return pl.pallas_call(
         pack_kernel,
-        grid=(2 * parts + 1,),
-        in_specs=[
-            pl.BlockSpec((256, 256), lambda g: (0, 0)),
-            pl.BlockSpec((META, PIX), lambda g: (0, 0)),
-            pl.BlockSpec(
-                (16, HALF, PIX), lambda g: (g % parts, jnp.minimum(g // parts, 1), 0)
-            ),
-        ],
-        out_specs=pl.BlockSpec((HALF, 16, PIX), lambda g: (0, g, 0)),
         out_shape=jax.ShapeDtypeStruct((HALF, 2 * count + META, PIX), BF16),
+        compiler_params=pltpu.CompilerParams(vmem_limit_bytes=24 * 1024 * 1024),
         cost_estimate=pl.CostEstimate(
             flops=4 * 256 * count * HALF * PIX, bytes_accessed=8 * count * HALF * PIX, transcendentals=0
         ),
@@ -174,9 +168,9 @@
     smoother_ref,
     out_ref,
     image_ref,
-    window_ref,
-    mixed_ref,
+    *scratch,
 ):
+    window_refs, mixed_refs = scratch[:BUFFERS], scratch[BUFFERS:]
     exchange = exchange_ref[...]
     lane = lax.broadcasted_iota(jnp.int32, (SPAN, PIX), 1)
     row = lax.broadcasted_iota(jnp.int32, (SPAN, PIX), 0)
@@ -199,7 +193,7 @@
 
     lax.fori_loop(0, BINS // 16, regroup, 0)
 
-    def group(number, carry):
+    def group(number, window_ref, mixed_ref):
         for local in range(GROUP):
             place = place_ref[number * GROUP + local]
             column = place // 128
@@ -249,9 +243,13 @@
         result = jnp.dot(down_ref[...], mixed_ref[...], preferred_element_type=F32)
         for local in range(GROUP):
             out_ref[begin + local] = result[:, local * PIX : (local + 1) * PIX].astype(BF16)
+
+    def groups(number, carry):
+        for which in range(BUFFERS):
+            group(number * BUFFERS + which, window_refs[which], mixed_refs[which])
         return carry
 
-    lax.fori_loop(0, tile_count // GROUP, group, 0)
+    lax.fori_loop(0, tile_count // (GROUP * BUFFERS), groups, 0)
 
 
 def detect(place, coeff, exchange, gathered, tiles, across, down, smoother):
@@ -266,9 +264,9 @@
         out_shape=jax.ShapeDtypeStruct((tile_count, PIX, PIX), BF16),
         scratch_shapes=[
             pltpu.VMEM((BINS, PIX, PIX), BF16),
-            pltpu.VMEM((GROUP * SPAN, 2 * PIX), BF16),
-            pltpu.VMEM((depth, GROUP * PIX), BF16),
-        ],
+        ]
+        + [pltpu.VMEM((GROUP * SPAN, 2 * PIX), BF16)] * BUFFERS
+        + [pltpu.VMEM((depth, GROUP * PIX), BF16)] * BUFFERS,
         compiler_params=pltpu.CompilerParams(vmem_limit_bytes=48 * 1024 * 1024),
         cost_estimate=pl.CostEstimate(
             flops=2 * tile_count * (SPAN * 256 * 1408 + depth * PIX * PIX),

time: 229 us -> 223 us (0.974)
  Pallas kernels: 37.6 us -> 30.2 us
  local copies, waits for them, and re-layouts: 7.14 us -> 9.65 us
    pallas_call x1, Pallas kernels: 7.03 us -> 0.71 us  [pack(): pl.pallas_call(pack_kernel, out_shape=jax.ShapeDtypeStruct((HALF, 2 * cou...]
    unnamed x19 -> x23, local copies, waits for them, and re-layouts: 0.7 us -> 3.2 us
where the time goes in v4:
time: 223 us; the launch traced here: 222 us
  blocking collectives  75.3 us (34%)
  waiting for transfers between devices  71.6 us (32%)
  Pallas kernels  30.2 us (14%)
  starting transfers between devices  17.9 us (8%)
  between operations  14.2 us (6%)
  local copies, waits for them, and re-layouts  9.65 us (4%)
  other arithmetic  3.63 us (2%)
    all_to_all x1, blocking collectives, exchanged(): return lax.all_to_all(array, axis, split_axis=0, concat_axis=0, tiled=True)  75.3 us
    all_gather x1, waiting for transfers between devices, body(): gathered = lax.all_gather(coadd, 'patch', axis=0, tiled=False)  48.6 us
    pallas_call x1, Pallas kernels, detect(): pl.pallas_call(detect_kernel, in_specs=[smem, smem] + [vmem] * 6, out_spe...  27.6 us
    all_to_all x2, waiting for transfers between devices, exchanged(): return lax.all_to_all(array, axis, split_axis=0, concat_axis=0, tiled=True)  23.1 us
    all_to_all x2, starting transfers between devices, exchanged(): return lax.all_to_all(array, axis, split_axis=0, concat_axis=0, tiled=True)  17.8 us
  transfers between devices with their start and end apart: 3, of which 3 were waited for; matrix products, arithmetic and copies ran while one was open for 4% of the time, Pallas kernels for 0%

profile of v4, /device:TPU:1, one launch (start us, length us, event | category | flops | bytes accessed | tf_op | source)
XLA Modules:
  0.0 222.5 jit_solution(9603055991289395784)
XLA Ops:
  7.2 0.0 all-gather.3.cloned.1.call-start
  7.2 0.7 fusion.10
  7.9 0.7 select_convert_fusion.1
  8.6 0.1 fusion.3.about_ref
  8.7 0.0 copy-start
  8.7 1.6 copy-done
  10.2 0.0 copy-start.2
  10.3 0.9 copy-done.2
  11.2 0.7 shard_map.112
  11.9 75.3 %all_to_all.15.row_ref = bf16[64,144,128]{2,1,0:T(8,128)(2,1)S(1)} all-to-all(bf16[64,144,128]{2,1,0:T(8,128)(2,1)S(1)} %shard_map.112), channel_id=1, replica_groups=mesh['patch'=64,'band'=8] {'patch'}, dimensions={0} | all-to-all | bytes 4718592 | tf_op jit(solution)/shard_map/all_to_all | solution.py:294
  87.1 1.9 shard_map.113
  89.1 0.0 all-gather.3.cloned.1.call-update
  89.1 0.9 copy.25
  90.0 0.7 copy.26
  90.8 0.0 copy-start.8
  90.8 0.0 copy-start.9
  90.8 0.0 copy-start.10
  90.8 10.4 %all-to-all-start.1 = ((bf16[64,8,128]{2,1,0:T(8,128)(2,1)}), bf16[64,8,128]{2,1,0:T(8,128)(2,1)S(1)}, u32[]{:S(2)}, u32[]{:S(2)}) async-start(bf16[64,8,128]{2,1,0:T(8,128)(2,1)} %copy.26), calls=%async_computation.1 | async-start | bytes 262144 | tf_op jit(solution)/shard_map/all_to_all | solution.py:294
  101.2 11.5 %all-to-all-done.1 = bf16[64,8,128]{2,1,0:T(8,128)(2,1)S(1)} async-done(((bf16[64,8,128]{2,1,0:T(8,128)(2,1)}), bf16[64,8,128]{2,1,0:T(8,128)(2,1)S(1)}, u32[]{:S(2)}, u32[]{:S(2)}) %all-to-all-start.1) | async-done | bytes 131104 | tf_op jit(solution)/shard_map/all_to_all | solution.py:294
  112.7 0.0 copy-start.7
  112.7 0.6 copy-done.7
  113.4 0.1 copy.28
  113.6 1.0 broadcast_in_dim.17
  114.6 0.0 copy-start.1
  114.6 0.0 copy-start.3
  114.6 0.0 copy-start.4
  114.6 0.0 copy-start.5
  114.7 0.0 copy-start.6
  114.7 7.4 %all-to-all-start.2 = ((bf16[8,256,256]{2,1,0:T(8,128)(2,1)}), bf16[8,256,256]{2,1,0:T(8,128)(2,1)}, u32[]{:S(2)}, u32[]{:S(2)}) async-start(bf16[8,256,256]{2,1,0:T(8,128)(2,1)} %broadcast_in_dim.17), calls=%async_computation.2 | async-start | bytes 2097152 | tf_op jit(solution)/shard_map/all_to_all | solution.py:294
  122.1 0.0 copy-done.8
  122.1 0.1 copy.30
  122.2 0.1 reshape.52.coeff_ref
  122.3 0.0 copy-done.9
  122.3 0.0 copy-done.10
  122.4 1.7 copy.29
  124.1 1.6 reshape.51
  125.7 11.6 %all-to-all-done.2 = bf16[8,256,256]{2,1,0:T(8,128)(2,1)} async-done(((bf16[8,256,256]{2,1,0:T(8,128)(2,1)}), bf16[8,256,256]{2,1,0:T(8,128)(2,1)}, u32[]{:S(2)}, u32[]{:S(2)}) %all-to-all-start.2) | async-done | bytes 1048608 | tf_op jit(solution)/shard_map/all_to_all | solution.py:294
  137.3 1.4 convert_reduce_fusion
  138.7 0.8 sqrt_convert_fusion
  139.4 48.6 %all-gather.3.cloned.1.call-done = bf16[32768,128]{1,0:T(8,128)(2,1)} async-done(((bf16[512,128]{1,0:T(8,128)(2,1)}), bf16[32768,128]{1,0:T(8,128)(2,1)}) %all-gather.3.cloned.1.call-update) | async-done | bytes 8388624 | tf_op jit(solution)/shard_map/all_gather | solution.py:298
  188.0 0.0 copy-done.1
  188.0 0.0 copy-done.3
  188.0 0.0 copy-done.4
  188.0 0.0 copy-done.5
  188.0 0.0 copy-done.6
  188.0 27.6 %shard_map.114 = bf16[64,128,128]{2,1,0:T(8,128)(2,1)} custom-call(s32[64]{0:T(128)S(1)} %fusion.9.place_ref, f32[1728]{0:T(1024)S(1)} %reshape.52.coeff_ref, bf16[256,256]{1,0:T(8,128)(2,1)S(1)} %copy-done.3, bf16[64,512,128]{2,1,0:T(8,128)(2,1)} %bitcast.45, bf16[64,128,128]{2,1,0:T(8,128)(2,1)S(1)} %bitcast.38, bf16[256,1408]{1,0:T(8,128)(2,1)S(1)} %copy-done.4, ...), custom_call_target="tpu_custom_call" | custom-call | flops 11341398016 | bytes 12582912 | tf_op jit(solution)/shard_map/pallas_call | solution.py:260
  (5 shorter events, 0.1 us)
Async XLA Ops:
  7.2 180.8 %all-gather.3.cloned.1.call-start = ((), (), s32[]{:S(2)}) async-start(), calls=%async_computation.3 | async-start | bytes 8519680 | tf_op jit(solution)/shard_map/all_gather | solution.py:298
  8.7 1.6 copy-start
  10.2 0.9 copy-start.2
  90.8 31.3 %copy-start.8 = (bf16[1,64,27]{1,2,0:T(8,128)(2,1)S(1)}, bf16[1,64,27]{1,2,0:T(8,128)(2,1)}, u32[]{:S(2)}) copy-start(bf16[1,64,27]{1,2,0:T(8,128)(2,1)} %param.13) | copy-start | bytes 10372
  90.8 31.6 %copy-start.9 = (s32[1,64]{1,0:T(1,128)S(1)}, s32[1,64]{1,0:T(1,128)}, u32[]{:S(2)}) copy-start(s32[1,64]{1,0:T(1,128)} %param.11) | copy-start | bytes 772
  90.8 31.6 %copy-start.10 = (s32[1,64,1]{1,2,0:T(1,128)S(1)}, s32[1,64,1]{1,2,0:T(1,128)}, u32[]{:S(2)}) copy-start(s32[1,64,1]{1,2,0:T(1,128)} %param.10) | copy-start | bytes 772
  90.8 21.9 %all-to-all-start.1 = ((bf16[64,8,128]{2,1,0:T(8,128)(2,1)}), bf16[64,8,128]{2,1,0:T(8,128)(2,1)S(1)}, u32[]{:S(2)}, u32[]{:S(2)}) async-start(bf16[64,8,128]{2,1,0:T(8,128)(2,1)} %copy.26), calls=%async_computation.1 | async-start | bytes 262144 | tf_op jit(solution)/shard_map/all_to_all | solution.py:294
  112.7 0.7 copy-start.7
  114.6 73.4 %copy-start.1 = (bf16[1,64,128,128]{3,2,1,0:T(8,128)(2,1)S(1)}, bf16[1,64,128,128]{3,2,1,0:T(8,128)(2,1)}, u32[]{:S(2)}) copy-start(bf16[1,64,128,128]{3,2,1,0:T(8,128)(2,1)} %param.9) | copy-start | bytes 6291460
  114.6 73.4 %copy-start.3 = (bf16[256,256]{1,0:T(8,128)(2,1)S(1)}, bf16[256,256]{1,0:T(8,128)(2,1)}, u32[]{:S(2)}) copy-start(bf16[256,256]{1,0:T(8,128)(2,1)} %constant.63.clone.exchange_ref) | copy-start | bytes 393220
  114.6 73.4 %copy-start.4 = (bf16[256,1408]{1,0:T(8,128)(2,1)S(1)}, bf16[256,1408]{1,0:T(8,128)(2,1)}, u32[]{:S(2)}) copy-start(bf16[256,1408]{1,0:T(8,128)(2,1)} %constant.60.clone.across_ref) | copy-start | bytes 2162692
  114.6 73.4 %copy-start.5 = (bf16[128,1888]{1,0:T(8,128)(2,1)S(1)}, bf16[128,1888]{1,0:T(8,128)(2,1)}, u32[]{:S(2)}) copy-start(bf16[128,1888]{1,0:T(8,128)(2,1)} %constant.61.clone.down_ref) | copy-start | bytes 1449988
  114.7 73.4 %copy-start.6 = (bf16[128,128]{1,0:T(8,128)(2,1)S(1)}, bf16[128,128]{1,0:T(8,128)(2,1)}, u32[]{:S(2)}) copy-start(bf16[128,128]{1,0:T(8,128)(2,1)} %constant.62.clone.smoother_ref) | copy-start | bytes 98308
  114.7 22.6 %all-to-all-start.2 = ((bf16[8,256,256]{2,1,0:T(8,128)(2,1)}), bf16[8,256,256]{2,1,0:T(8,128)(2,1)}, u32[]{:S(2)}, u32[]{:S(2)}) async-start(bf16[8,256,256]{2,1,0:T(8,128)(2,1)} %broadcast_in_dim.17), calls=%async_computation.2 | async-start | bytes 2097152 | tf_op jit(solution)/shard_map/all_to_all | solution.py:294
Sparse Core Ops, SparseCore 0:
  89.2 98.7 all-gather.2

commit v5 on v4

--- a/solution.py
+++ b/solution.py
@@ -1,3 +1,5 @@
+import functools
+
 import jax
 import jax.numpy as jnp
 import ml_dtypes
@@ -162,36 +164,60 @@
     coeff_ref,
     exchange_ref,
     gathered_ref,
+    tile_source,
+    across_source,
+    down_source,
+    smoother_ref,
+    out_ref,
+    image_ref,
+    held_ref,
     tile_ref,
     across_ref,
     down_ref,
-    smoother_ref,
-    out_ref,
-    image_ref,
+    arrived,
     *scratch,
 ):
     window_refs, mixed_refs = scratch[:BUFFERS], scratch[BUFFERS:]
+
+    def piece(part):
+        spot = pl.ds(part * 16, 16)
+        return pltpu.make_async_copy(gathered_ref.at[spot], held_ref.at[spot], arrived.at[part])
+
+    others = [
+        pltpu.make_async_copy(source, target, arrived.at[HALF // 16 + number])
+        for number, (source, target) in enumerate(
+            ((tile_source, tile_ref), (across_source, across_ref), (down_source, down_ref))
+        )
+    ]
+    for part in range(HALF // 16):
+        piece(part).start()
+    for other in others:
+        other.start()
     exchange = exchange_ref[...]
     lane = lax.broadcasted_iota(jnp.int32, (SPAN, PIX), 1)
     row = lax.broadcasted_iota(jnp.int32, (SPAN, PIX), 0)
     tile_count = out_ref.shape[0]
 
-    def regroup(block, carry):
+    def regroup(part, block, carry):
         base = pl.multiple_of(block * 16, 16)
-        for half in range(2):
-
-            def read(number):
-                start = pl.multiple_of(base + half * BINS, 16)
-                return gathered_ref[number * 16 : number * 16 + 16, pl.ds(start, 16), :]
-
-            def write(number, value):
-                spot = half * HALF + number * 16
-                image_ref[pl.ds(base, 16), spot : spot + 16, :] = value
-
-            swap_blocks(exchange, read, write, HALF // 16)
+
+        def read(half):
+            start = pl.multiple_of(base + half * BINS, 16)
+            return held_ref[part * 16 : part * 16 + 16, pl.ds(start, 16), :]
+
+        def write(half, value):
+            spot = half * HALF + part * 16
+            image_ref[pl.ds(base, 16), spot : spot + 16, :] = value
+
+        swap_blocks(exchange, read, write, 2)
         return carry
 
-    lax.fori_loop(0, BINS // 16, regroup, 0)
+    for part in range(HALF // 16):
+        piece(part).wait()
+        lax.fori_loop(0, BINS // 16, functools.partial(regroup, part), 0, unroll=16)
+
+    for other in others:
+        other.wait()
 
     def group(number, window_ref, mixed_ref):
         for local in range(GROUP):
@@ -259,11 +285,16 @@
     vmem = pl.BlockSpec(memory_space=pltpu.VMEM)
     return pl.pallas_call(
         detect_kernel,
-        in_specs=[smem, smem] + [vmem] * 6,
+        in_specs=[smem, smem, vmem] + [pl.BlockSpec(memory_space=pl.ANY)] * 4 + [vmem],
         out_specs=vmem,
         out_shape=jax.ShapeDtypeStruct((tile_count, PIX, PIX), BF16),
         scratch_shapes=[
             pltpu.VMEM((BINS, PIX, PIX), BF16),
+            pltpu.VMEM(gathered.shape, BF16),
+            pltpu.VMEM(tiles.shape, BF16),
+            pltpu.VMEM(across.shape, BF16),
+            pltpu.VMEM(down.shape, BF16),
+            pltpu.SemaphoreType.DMA((HALF // 16 + 3,)),
         ]
         + [pltpu.VMEM((GROUP * SPAN, 2 * PIX), BF16)] * BUFFERS
         + [pltpu.VMEM((depth, GROUP * PIX), BF16)] * BUFFERS,

time: 223 us -> 220 us (0.987)
  Pallas kernels: 30.2 us -> 27.1 us
    pallas_call x1, Pallas kernels: 27.6 us -> 24.5 us  [detect(): pl.pallas_call(detect_kernel, in_specs=[smem, smem, vmem] + [pl.BlockSpec...]
where the time goes in v5:
time: 220 us; the launch traced here: 219 us
  blocking collectives  75.3 us (34%)
  waiting for transfers between devices  71.6 us (33%)
  Pallas kernels  27.1 us (12%)
  starting transfers between devices  17.9 us (8%)
  between operations  14.2 us (6%)
  local copies, waits for them, and re-layouts  9.65 us (4%)
  other arithmetic  3.63 us (2%)
    all_to_all x1, blocking collectives, exchanged(): return lax.all_to_all(array, axis, split_axis=0, concat_axis=0, tiled=True)  75.3 us
    all_gather x1, waiting for transfers between devices, body(): gathered = lax.all_gather(coadd, 'patch', axis=0, tiled=False)  48.6 us
    pallas_call x1, Pallas kernels, detect(): pl.pallas_call(detect_kernel, in_specs=[smem, smem, vmem] + [pl.BlockSpec...  24.5 us
    all_to_all x2, waiting for transfers between devices, exchanged(): return lax.all_to_all(array, axis, split_axis=0, concat_axis=0, tiled=True)  23.1 us
    all_to_all x2, starting transfers between devices, exchanged(): return lax.all_to_all(array, axis, split_axis=0, concat_axis=0, tiled=True)  17.8 us
  transfers between devices with their start and end apart: 3, of which 3 were waited for; matrix products, arithmetic and copies ran while one was open for 4% of the time, Pallas kernels for 0%

profile of v5, /device:TPU:1, one launch (start us, length us, event | category | flops | bytes accessed | tf_op | source)
XLA Modules:
  0.0 219.4 jit_solution(9388666173812988732)
XLA Ops:
  7.2 0.0 all-gather.3.cloned.1.call-start
  7.2 0.7 fusion.10
  7.9 0.7 select_convert_fusion.1
  8.6 0.1 fusion.3.about_ref
  8.7 0.0 copy-start
  8.7 1.6 copy-done
  10.2 0.0 copy-start.2
  10.3 0.9 copy-done.2
  11.2 0.7 shard_map.112
  11.9 75.3 %all_to_all.15.row_ref = bf16[64,144,128]{2,1,0:T(8,128)(2,1)S(1)} all-to-all(bf16[64,144,128]{2,1,0:T(8,128)(2,1)S(1)} %shard_map.112), channel_id=1, replica_groups=mesh['patch'=64,'band'=8] {'patch'}, dimensions={0} | all-to-all | bytes 4718592 | tf_op jit(solution)/shard_map/all_to_all | solution.py:325
  87.1 1.9 shard_map.113
  89.1 0.0 all-gather.3.cloned.1.call-update
  89.1 0.9 copy.25
  90.0 0.7 copy.26
  90.8 0.0 copy-start.8
  90.8 0.0 copy-start.9
  90.8 0.0 copy-start.10
  90.8 10.4 %all-to-all-start.1 = ((bf16[64,8,128]{2,1,0:T(8,128)(2,1)}), bf16[64,8,128]{2,1,0:T(8,128)(2,1)S(1)}, u32[]{:S(2)}, u32[]{:S(2)}) async-start(bf16[64,8,128]{2,1,0:T(8,128)(2,1)} %copy.26), calls=%async_computation.1 | async-start | bytes 262144 | tf_op jit(solution)/shard_map/all_to_all | solution.py:325
  101.2 11.5 %all-to-all-done.1 = bf16[64,8,128]{2,1,0:T(8,128)(2,1)S(1)} async-done(((bf16[64,8,128]{2,1,0:T(8,128)(2,1)}), bf16[64,8,128]{2,1,0:T(8,128)(2,1)S(1)}, u32[]{:S(2)}, u32[]{:S(2)}) %all-to-all-start.1) | async-done | bytes 131104 | tf_op jit(solution)/shard_map/all_to_all | solution.py:325
  112.7 0.0 copy-start.7
  112.7 0.6 copy-done.7
  113.4 0.1 copy.28
  113.6 1.0 broadcast_in_dim.17
  114.6 0.0 copy-start.1
  114.6 0.0 copy-start.3
  114.6 0.0 copy-start.4
  114.6 0.0 copy-start.5
  114.7 0.0 copy-start.6
  114.7 7.4 %all-to-all-start.2 = ((bf16[8,256,256]{2,1,0:T(8,128)(2,1)}), bf16[8,256,256]{2,1,0:T(8,128)(2,1)}, u32[]{:S(2)}, u32[]{:S(2)}) async-start(bf16[8,256,256]{2,1,0:T(8,128)(2,1)} %broadcast_in_dim.17), calls=%async_computation.2 | async-start | bytes 2097152 | tf_op jit(solution)/shard_map/all_to_all | solution.py:325
  122.1 0.0 copy-done.8
  122.1 0.1 copy.30
  122.2 0.1 reshape.52.coeff_ref
  122.3 0.0 copy-done.9
  122.3 0.0 copy-done.10
  122.4 1.7 copy.29
  124.1 1.6 reshape.51
  125.7 11.6 %all-to-all-done.2 = bf16[8,256,256]{2,1,0:T(8,128)(2,1)} async-done(((bf16[8,256,256]{2,1,0:T(8,128)(2,1)}), bf16[8,256,256]{2,1,0:T(8,128)(2,1)}, u32[]{:S(2)}, u32[]{:S(2)}) %all-to-all-start.2) | async-done | bytes 1048608 | tf_op jit(solution)/shard_map/all_to_all | solution.py:325
  137.3 1.4 convert_reduce_fusion
  138.7 0.8 sqrt_convert_fusion
  139.4 48.6 %all-gather.3.cloned.1.call-done = bf16[32768,128]{1,0:T(8,128)(2,1)} async-done(((bf16[512,128]{1,0:T(8,128)(2,1)}), bf16[32768,128]{1,0:T(8,128)(2,1)}) %all-gather.3.cloned.1.call-update) | async-done | bytes 8388624 | tf_op jit(solution)/shard_map/all_gather | solution.py:329
  188.0 0.0 copy-done.1
  188.0 0.0 copy-done.3
  188.0 0.0 copy-done.4
  188.0 0.0 copy-done.5
  188.0 0.0 copy-done.6
  188.0 24.5 %shard_map.114 = bf16[64,128,128]{2,1,0:T(8,128)(2,1)} custom-call(s32[64]{0:T(128)S(1)} %fusion.9.place_ref, f32[1728]{0:T(1024)S(1)} %reshape.52.coeff_ref, bf16[256,256]{1,0:T(8,128)(2,1)S(1)} %copy-done.3, bf16[64,512,128]{2,1,0:T(8,128)(2,1)} %bitcast.45, bf16[64,128,128]{2,1,0:T(8,128)(2,1)S(1)} %bitcast.38, bf16[256,1408]{1,0:T(8,128)(2,1)S(1)} %copy-done.4, ...), custom_call_target="tpu_custom_call" | custom-call | flops 11341398016 | bytes 12582912 | tf_op jit(solution)/shard_map/pallas_call | solution.py:286
  (5 shorter events, 0.1 us)
Async XLA Ops:
  7.2 180.8 %all-gather.3.cloned.1.call-start = ((), (), s32[]{:S(2)}) async-start(), calls=%async_computation.3 | async-start | bytes 8519680 | tf_op jit(solution)/shard_map/all_gather | solution.py:329
  8.7 1.6 copy-start
  10.2 0.9 copy-start.2
  90.8 31.3 %copy-start.8 = (bf16[1,64,27]{1,2,0:T(8,128)(2,1)S(1)}, bf16[1,64,27]{1,2,0:T(8,128)(2,1)}, u32[]{:S(2)}) copy-start(bf16[1,64,27]{1,2,0:T(8,128)(2,1)} %param.13) | copy-start | bytes 10372
  90.8 31.6 %copy-start.9 = (s32[1,64]{1,0:T(1,128)S(1)}, s32[1,64]{1,0:T(1,128)}, u32[]{:S(2)}) copy-start(s32[1,64]{1,0:T(1,128)} %param.11) | copy-start | bytes 772
  90.8 31.6 %copy-start.10 = (s32[1,64,1]{1,2,0:T(1,128)S(1)}, s32[1,64,1]{1,2,0:T(1,128)}, u32[]{:S(2)}) copy-start(s32[1,64,1]{1,2,0:T(1,128)} %param.10) | copy-start | bytes 772
  90.8 21.9 %all-to-all-start.1 = ((bf16[64,8,128]{2,1,0:T(8,128)(2,1)}), bf16[64,8,128]{2,1,0:T(8,128)(2,1)S(1)}, u32[]{:S(2)}, u32[]{:S(2)}) async-start(bf16[64,8,128]{2,1,0:T(8,128)(2,1)} %copy.26), calls=%async_computation.1 | async-start | bytes 262144 | tf_op jit(solution)/shard_map/all_to_all | solution.py:325
  112.7 0.7 copy-start.7
  114.6 73.4 %copy-start.1 = (bf16[1,64,128,128]{3,2,1,0:T(8,128)(2,1)S(1)}, bf16[1,64,128,128]{3,2,1,0:T(8,128)(2,1)}, u32[]{:S(2)}) copy-start(bf16[1,64,128,128]{3,2,1,0:T(8,128)(2,1)} %param.9) | copy-start | bytes 6291460
  114.6 73.4 %copy-start.3 = (bf16[256,256]{1,0:T(8,128)(2,1)S(1)}, bf16[256,256]{1,0:T(8,128)(2,1)}, u32[]{:S(2)}) copy-start(bf16[256,256]{1,0:T(8,128)(2,1)} %constant.63.clone.exchange_ref) | copy-start | bytes 393220
  114.6 73.4 %copy-start.4 = (bf16[256,1408]{1,0:T(8,128)(2,1)S(1)}, bf16[256,1408]{1,0:T(8,128)(2,1)}, u32[]{:S(2)}) copy-start(bf16[256,1408]{1,0:T(8,128)(2,1)} %constant.60.clone.across_source) | copy-start | bytes 2162692
  114.6 73.4 %copy-start.5 = (bf16[128,1888]{1,0:T(8,128)(2,1)S(1)}, bf16[128,1888]{1,0:T(8,128)(2,1)}, u32[]{:S(2)}) copy-start(bf16[128,1888]{1,0:T(8,128)(2,1)} %constant.61.clone.down_source) | copy-start | bytes 1449988
  114.7 73.4 %copy-start.6 = (bf16[128,128]{1,0:T(8,128)(2,1)S(1)}, bf16[128,128]{1,0:T(8,128)(2,1)}, u32[]{:S(2)}) copy-start(bf16[128,128]{1,0:T(8,128)(2,1)} %constant.62.clone.smoother_ref) | copy-start | bytes 98308
  114.7 22.6 %all-to-all-start.2 = ((bf16[8,256,256]{2,1,0:T(8,128)(2,1)}), bf16[8,256,256]{2,1,0:T(8,128)(2,1)}, u32[]{:S(2)}, u32[]{:S(2)}) async-start(bf16[8,256,256]{2,1,0:T(8,128)(2,1)} %broadcast_in_dim.17), calls=%async_computation.2 | async-start | bytes 2097152 | tf_op jit(solution)/shard_map/all_to_all | solution.py:325
Sparse Core Ops, SparseCore 0:
  89.2 98.7 all-gather.2

commit v6 on v5

--- a/solution.py
+++ b/solution.py
@@ -66,12 +66,13 @@
     )
     rows = np.arange(SPAN) - HALO
     down = [-(smoother @ tap_matrix(kernel_taps(SIGMAS[s], j), rows, pixel).T) for s, j in PAIRS]
-    return rounded(across), rounded(np.concatenate(down + [smoother], axis=1)), rounded(smoother.T)
+    return rounded(across), rounded(np.concatenate(down, axis=1)), rounded(smoother.T)
 
 
 def exchange_matrix():
-    order = np.arange(256).reshape(16, 16).T.reshape(256)
-    return np.eye(256, dtype=np.float32)[order].astype(ml_dtypes.bfloat16)
+    row = lax.broadcasted_iota(jnp.int32, (256, 256), 0)
+    column = lax.broadcasted_iota(jnp.int32, (256, 256), 1)
+    return jnp.where(column == (row % 16) * 16 + row // 16, 1.0, 0.0).astype(BF16)
 
 
 def swap_blocks(exchange, read, write, count):
@@ -84,8 +85,12 @@
         write(first + 1, moved[:, PIX:].reshape(16, 16, PIX))
 
 
-def pack_kernel(exchange_ref, about_ref, tile_ref, out_ref):
-    exchange = exchange_ref[...]
+def block_number(patch, slot):
+    return (slot & 1) * 128 + 2 * patch + (slot >> 1)
+
+
+def pack_kernel(patch_ref, slot_ref, weight_ref, tile_ref, out_ref):
+    exchange = exchange_matrix()
     count = tile_ref.shape[0]
     for half in range(2):
         for start in range(0, count, 16):
@@ -99,12 +104,17 @@
                 out_ref[block * 16 : block * 16 + 16, spot : spot + 16, :] = value
 
             swap_blocks(exchange, read, write, HALF // 16)
-    about = about_ref[...]
+    number = block_number(patch_ref[...], slot_ref[...]).astype(F32)
+    weight = weight_ref[...].astype(F32)
+    number = jnp.concatenate([number, number], axis=1)
+    weight = jnp.concatenate([weight, weight], axis=1)
+    row = lax.broadcasted_iota(jnp.int32, (META, PIX), 0)
+    about = jnp.where(row == 0, number, jnp.where(row == 1, weight, 0.0)).astype(BF16)
     for device in range(out_ref.shape[0]):
         out_ref[device, 2 * count :, :] = about
 
 
-def pack(exchange, about, tiles):
+def pack(patch, slot, weight, tiles):
     count = tiles.shape[0]
     return pl.pallas_call(
         pack_kernel,
@@ -113,19 +123,55 @@
         cost_estimate=pl.CostEstimate(
             flops=4 * 256 * count * HALF * PIX, bytes_accessed=8 * count * HALF * PIX, transcendentals=0
         ),
-    )(exchange, about, tiles)
+    )(patch, slot, weight, tiles)
+
+
+def smooth_kernel(tile_ref, smoother_ref, out_ref):
+    smoother = smoother_ref[...]
+    across = jnp.dot(
+        tile_ref[...].reshape(-1, PIX), smoother, preferred_element_type=F32
+    ).astype(BF16)
+    for tile in range(tile_ref.shape[0]):
+        out_ref[tile] = lax.dot_general(
+            smoother,
+            across[tile * PIX : (tile + 1) * PIX],
+            (((0,), (0,)), ((), ())),
+            preferred_element_type=F32,
+        )
+
+
+def smooth_tiles(tiles, smoother):
+    count = tiles.shape[0]
+    return pl.pallas_call(
+        smooth_kernel,
+        grid=(count // 8,),
+        in_specs=[
+            pl.BlockSpec((8, PIX, PIX), lambda g: (g, 0, 0)),
+            pl.BlockSpec((PIX, PIX), lambda g: (0, 0)),
+        ],
+        out_specs=pl.BlockSpec((8, PIX, PIX), lambda g: (g, 0, 0)),
+        out_shape=jax.ShapeDtypeStruct(tiles.shape, F32),
+        cost_estimate=pl.CostEstimate(
+            flops=4 * count * PIX**3, bytes_accessed=6 * count * PIX * PIX, transcendentals=0
+        ),
+    )(tiles, smoother)
 
 
 def coadd_kernel(row_ref, coadd_ref, sum_ref):
     sources = row_ref.shape[0]
     count = (row_ref.shape[1] - META) // 2
     numbers = lax.broadcasted_iota(jnp.int32, (BINS, PIX), 0).astype(F32)
+    first_source = lax.broadcasted_iota(jnp.int32, (META, PIX), 1) < count
     ones = jnp.ones((4 * count, PIX), BF16)
     running = jnp.zeros((BINS, 3 * PIX), F32)
     for first in range(0, sources, 4):
         loading = []
         for source in (first, first + 2):
-            about = row_ref[source, 2 * count :, :].astype(F32) + row_ref[source + 1, 2 * count :, :].astype(F32)
+            about = jnp.where(
+                first_source,
+                row_ref[source, 2 * count :, :].astype(F32),
+                row_ref[source + 1, 2 * count :, :].astype(F32),
+            )
             loading.append(jnp.where(about[0:1] == numbers, about[1:2], 0.0).astype(BF16))
         values = jnp.concatenate(
             [
@@ -162,12 +208,10 @@
 def detect_kernel(
     place_ref,
     coeff_ref,
-    exchange_ref,
     gathered_ref,
     tile_source,
     across_source,
     down_source,
-    smoother_ref,
     out_ref,
     image_ref,
     held_ref,
@@ -193,7 +237,7 @@
         piece(part).start()
     for other in others:
         other.start()
-    exchange = exchange_ref[...]
+    exchange = exchange_matrix()
     lane = lax.broadcasted_iota(jnp.int32, (SPAN, PIX), 1)
     row = lax.broadcasted_iota(jnp.int32, (SPAN, PIX), 0)
     tile_count = out_ref.shape[0]
@@ -259,16 +303,10 @@
                     spot = (first + power_y) * SPAN
                     mixed_ref[spot : spot + SPAN, local * PIX : (local + 1) * PIX] = total.astype(BF16)
         begin = pl.multiple_of(number * GROUP, GROUP)
-        tiles = tile_ref[pl.ds(begin, GROUP)].reshape(GROUP * PIX, PIX)
-        smooth = jnp.dot(tiles, smoother_ref[...], preferred_element_type=F32).astype(BF16)
-        spot = len(PAIRS) * SPAN
-        for local in range(GROUP):
-            mixed_ref[spot : spot + PIX, local * PIX : (local + 1) * PIX] = smooth[
-                local * PIX : (local + 1) * PIX
-            ]
         result = jnp.dot(down_ref[...], mixed_ref[...], preferred_element_type=F32)
         for local in range(GROUP):
-            out_ref[begin + local] = result[:, local * PIX : (local + 1) * PIX].astype(BF16)
+            piece = result[:, local * PIX : (local + 1) * PIX] + tile_ref[begin + local]
+            out_ref[begin + local] = piece.astype(BF16)
 
     def groups(number, carry):
         for which in range(BUFFERS):
@@ -278,20 +316,20 @@
     lax.fori_loop(0, tile_count // (GROUP * BUFFERS), groups, 0)
 
 
-def detect(place, coeff, exchange, gathered, tiles, across, down, smoother):
+def detect(place, coeff, gathered, tiles, across, down):
     tile_count = tiles.shape[0]
     depth = down.shape[1]
     smem = pl.BlockSpec(memory_space=pltpu.SMEM)
     vmem = pl.BlockSpec(memory_space=pltpu.VMEM)
     return pl.pallas_call(
         detect_kernel,
-        in_specs=[smem, smem, vmem] + [pl.BlockSpec(memory_space=pl.ANY)] * 4 + [vmem],
+        in_specs=[smem, smem] + [pl.BlockSpec(memory_space=pl.ANY)] * 4,
         out_specs=vmem,
         out_shape=jax.ShapeDtypeStruct((tile_count, PIX, PIX), BF16),
         scratch_shapes=[
             pltpu.VMEM((BINS, PIX, PIX), BF16),
             pltpu.VMEM(gathered.shape, BF16),
-            pltpu.VMEM(tiles.shape, BF16),
+            pltpu.VMEM(tiles.shape, F32),
             pltpu.VMEM(across.shape, BF16),
             pltpu.VMEM(down.shape, BF16),
             pltpu.SemaphoreType.DMA((HALF // 16 + 3,)),
@@ -304,27 +342,23 @@
             bytes_accessed=12 * 1024 * 1024,
             transcendentals=0,
         ),
-    )(place, coeff, exchange, gathered, tiles, across, down, smoother)
+    )(place, coeff, gathered, tiles, across, down)
 
 
 def body(visit_tiles, tile_patch, tile_slot, tile_weight, psf_coeff):
     tiles = visit_tiles[0]
     across, down, smoother = (jnp.asarray(m) for m in constants())
-    exchange = jnp.asarray(exchange_matrix())
     patch = lax.axis_index("patch")
     patch_count = lax.axis_size("patch")
     band_count = lax.axis_size("band")
-    place = (tile_slot[0] % 2) * 128 + 2 * tile_patch[0, :, 0] + tile_slot[0] // 2
-    facts = jnp.stack([place.astype(F32), tile_weight[0].astype(F32)])
-    even = (patch % 2) == 0
-    facts = jnp.concatenate([jnp.where(even, facts, 0.0), jnp.where(even, 0.0, facts)], axis=1)
-    about = jnp.pad(facts, ((0, META - 2), (0, 0))).astype(BF16)
+    tile_patch = tile_patch.reshape(tile_slot.shape)
+    place = block_number(tile_patch[0], tile_slot[0])
     coeff = psf_coeff[0].astype(F32).reshape(-1)
 
     def exchanged(array, axis):
         return lax.all_to_all(array, axis, split_axis=0, concat_axis=0, tiled=True)
 
-    rows = exchanged(pack(exchange, about, tiles), "patch")
+    rows = exchanged(pack(tile_patch, tile_slot, tile_weight, tiles), "patch")
     coadd, weight_sum = coadd_rows(rows)
     gathered = lax.all_gather(coadd, "patch", axis=0, tiled=False)
 
@@ -339,8 +373,12 @@
     chi_image = jnp.sqrt(1.0 + jnp.sum(terms.astype(F32), axis=0)).astype(BF16)
     coadd_image = coadd_image.reshape(1, SB * PIX, SB * PIX)
 
-    gathered, chi_image, coadd_image = lax.optimization_barrier((gathered, chi_image, coadd_image))
-    detection = detect(place, coeff, exchange, gathered, tiles, across, down, smoother)
+    later, coadd = lax.optimization_barrier((tiles, coadd))
+    smoothed = smooth_tiles(later, smoother)
+    gathered, smoothed, chi_image, coadd_image = lax.optimization_barrier(
+        (gathered, smoothed, chi_image, coadd_image)
+    )
+    detection = detect(place, coeff, gathered, smoothed, across, down)
     return (coadd_image, detection[None], chi_image)
 
 

time: 220 us -> 221 us (level)
  Pallas kernels: 27.1 us -> 34.2 us
  waiting for transfers between devices: 71.6 us -> 68.7 us
  other arithmetic: 3.63 us -> 0.95 us
    pallas_call x1 -> x2, Pallas kernels: 24.5 us -> 31.6 us  [the longest x1 24 us: detect(): pl.pallas_call(detect_kernel, in_specs=[smem, smem] + [pl.BlockSpec(memor...]
    all_to_all x2, waiting for transfers between devices: 23.1 us -> 17.8 us  [exchanged(): return lax.all_to_all(array, axis, split_axis=0, concat_axis=0, tiled=True)]
    unnamed x23 -> x21, local copies, waits for them, and re-layouts: 3.2 us -> 5.78 us
    all_gather x1, waiting for transfers between devices: 48.6 us -> 50.9 us  [body(): gathered = lax.all_gather(coadd, 'patch', axis=0, tiled=False)]
  transfers between devices with their start and end apart: 3 -> 3, of which waited for: 3 -> 3; matrix products, arithmetic and copies ran while one was open for 4% -> 2% of each run, Pallas kernels for 0% -> 3%
where the time goes in v6:
time: 221 us
  blocking collectives  75 us (34%)
  waiting for transfers between devices  68.7 us (31%)
  Pallas kernels  34.2 us (15%)
  starting transfers between devices  17.9 us (8%)
  between operations  14.2 us (6%)
  local copies, waits for them, and re-layouts  9.77 us (4%)
    all_to_all x1, blocking collectives, exchanged(): return lax.all_to_all(array, axis, split_axis=0, concat_axis=0, tiled=True)  75 us
    all_gather x1, waiting for transfers between devices, body(): gathered = lax.all_gather(coadd, 'patch', axis=0, tiled=False)  50.9 us
    pallas_call x1, Pallas kernels, detect(): pl.pallas_call(detect_kernel, in_specs=[smem, smem] + [pl.BlockSpec(memor...  24 us
    all_to_all x2, starting transfers between devices, exchanged(): return lax.all_to_all(array, axis, split_axis=0, concat_axis=0, tiled=True)  17.8 us
    all_to_all x2, waiting for transfers between devices, exchanged(): return lax.all_to_all(array, axis, split_axis=0, concat_axis=0, tiled=True)  17.8 us
    pallas_call x1, Pallas kernels, smooth_tiles(): pl.pallas_call(smooth_kernel, grid=(count // 8,), in_specs=[pl.BlockSpec(...  7.59 us
    unnamed x21, local copies, waits for them, and re-layouts  5.78 us
  transfers between devices with their start and end apart: 3, of which 3 were waited for; matrix products, arithmetic and copies ran while one was open for 2% of the time, Pallas kernels for 3%

profile of v6, /device:TPU:1, one launch (start us, length us, event | category | flops | bytes accessed | tf_op | source)
XLA Modules:
  0.0 220.7 jit_solution(13807735020047666964)
XLA Ops:
  7.2 0.0 all-gather.3.cloned.1.call-start
  7.2 0.0 copy-start
  7.2 1.6 copy-done
  8.8 0.0 copy-start.2
  8.8 0.7 copy-done.2
  9.5 0.0 copy-start.3
  9.5 0.7 copy-done.3
  10.1 0.0 copy-start.5
  10.1 0.7 copy-done.5
  10.8 0.7 shard_map.103
  11.5 75.0 %all_to_all.15.row_ref = bf16[64,144,128]{2,1,0:T(8,128)(2,1)S(1)} all-to-all(bf16[64,144,128]{2,1,0:T(8,128)(2,1)S(1)} %shard_map.103), channel_id=1, replica_groups=mesh['patch'=64,'band'=8] {'patch'}, dimensions={0} | all-to-all | bytes 4718592 | tf_op jit(solution)/shard_map/all_to_all | solution.py:359
  86.5 1.9 shard_map.104
  88.4 0.0 all-gather.3.cloned.1.call-update
  88.5 0.9 copy.24
  89.4 0.7 copy.25
  90.1 0.0 copy-start.9
  90.1 0.0 copy-start.4
  90.1 0.0 copy-start.6
  90.1 10.6 %all-to-all-start.1 = ((bf16[64,8,128]{2,1,0:T(8,128)(2,1)}), bf16[64,8,128]{2,1,0:T(8,128)(2,1)S(1)}, u32[]{:S(2)}, u32[]{:S(2)}) async-start(bf16[64,8,128]{2,1,0:T(8,128)(2,1)} %copy.25), calls=%async_computation.1 | async-start | bytes 262144 | tf_op jit(solution)/shard_map/all_to_all | solution.py:359
  100.8 11.5 %all-to-all-done.1 = bf16[64,8,128]{2,1,0:T(8,128)(2,1)S(1)} async-done(((bf16[64,8,128]{2,1,0:T(8,128)(2,1)}), bf16[64,8,128]{2,1,0:T(8,128)(2,1)S(1)}, u32[]{:S(2)}, u32[]{:S(2)}) %all-to-all-start.1) | async-done | bytes 131104 | tf_op jit(solution)/shard_map/all_to_all | solution.py:359
  112.4 0.1 copy.27
  112.5 1.0 broadcast_in_dim.4
  113.6 7.2 %all-to-all-start.2 = ((bf16[8,256,256]{2,1,0:T(8,128)(2,1)}), bf16[8,256,256]{2,1,0:T(8,128)(2,1)S(1)}, u32[]{:S(2)}, u32[]{:S(2)}) async-start(bf16[8,256,256]{2,1,0:T(8,128)(2,1)} %broadcast_in_dim.4), calls=%async_computation.2 | async-start | bytes 2097152 | tf_op jit(solution)/shard_map/all_to_all | solution.py:359
  120.8 0.0 copy-done.9
  120.8 0.1 copy.29
  120.9 0.1 reshape.50.coeff_ref
  121.0 0.0 copy-done.4
  121.0 0.0 copy-done.6
  121.1 0.0 copy-start.7
  121.1 0.0 copy-start.8
  121.1 7.6 %shard_map.105.tile_source = f32[64,128,128]{2,1,0:T(8,128)} custom-call(bf16[64,128,128]{2,1,0:T(8,128)(2,1)} %bitcast.27, bf16[128,128]{1,0:T(8,128)(2,1)} %constant.28.clone.smoother_ref), custom_call_target="tpu_custom_call" | custom-call | flops 536870912 | bytes 6291456 | tf_op jit(solution)/shard_map/pallas_call | solution.py:145
  128.7 0.1 copy.28
  128.8 0.7 reshape.49
  129.6 6.3 %all-to-all-done.2 = bf16[8,256,256]{2,1,0:T(8,128)(2,1)S(1)} async-done(((bf16[8,256,256]{2,1,0:T(8,128)(2,1)}), bf16[8,256,256]{2,1,0:T(8,128)(2,1)S(1)}, u32[]{:S(2)}, u32[]{:S(2)}) %all-to-all-start.2) | async-done | bytes 1048608 | tf_op jit(solution)/shard_map/all_to_all | solution.py:359
  135.9 0.1 convert_reduce_fusion
  136.0 0.8 sqrt_convert_fusion
  136.8 50.9 %all-gather.3.cloned.1.call-done = bf16[32768,128]{1,0:T(8,128)(2,1)} async-done(((bf16[512,128]{1,0:T(8,128)(2,1)}), bf16[32768,128]{1,0:T(8,128)(2,1)}) %all-gather.3.cloned.1.call-update) | async-done | bytes 8388624 | tf_op jit(solution)/shard_map/all_gather | solution.py:363
  187.7 0.0 copy-done.7
  187.7 0.0 copy-done.8
  187.7 0.0 copy-start.1
  187.7 2.2 copy-done.1
  189.8 24.0 %shard_map.106 = bf16[64,128,128]{2,1,0:T(8,128)(2,1)} custom-call(s32[64]{0:T(128)S(1)} %bitcast_add_fusion.place_ref, f32[1728]{0:T(1024)S(1)} %reshape.50.coeff_ref, bf16[64,512,128]{2,1,0:T(8,128)(2,1)} %bitcast.36, f32[64,128,128]{2,1,0:T(8,128)S(1)} %copy-done.1, bf16[256,1408]{1,0:T(8,128)(2,1)S(1)} %copy-done.7, bf16[128,1760]{1,0:T(8,128)(2,1)S(1)} %copy-done.8), custom_call_target="tpu_custom_call" | custom-call | flops 11072962560 | bytes 12582912 | tf_op jit(solution)/shard_map/pallas_call | solution.py:324
  (5 shorter events, 0.1 us)
Async XLA Ops:
  7.2 180.5 %all-gather.3.cloned.1.call-start = ((), (), s32[]{:S(2)}) async-start(), calls=%async_computation.3 | async-start | bytes 8519680 | tf_op jit(solution)/shard_map/all_gather | solution.py:363
  7.2 1.6 copy-start
  8.8 0.7 copy-start.2
  9.5 0.7 copy-start.3
  10.1 0.7 copy-start.5
  90.1 30.7 %copy-start.9 = (bf16[1,64,27]{1,2,0:T(8,128)(2,1)S(1)}, bf16[1,64,27]{1,2,0:T(8,128)(2,1)}, u32[]{:S(2)}) copy-start(bf16[1,64,27]{1,2,0:T(8,128)(2,1)} %param.12) | copy-start | bytes 10372
  90.1 30.9 %copy-start.4 = (s32[1,64,1]{1,2,0:T(1,128)S(1)}, s32[1,64,1]{1,2,0:T(1,128)}, u32[]{:S(2)}) copy-start(s32[1,64,1]{1,2,0:T(1,128)} %param.9) | copy-start | bytes 772
  90.1 30.9 %copy-start.6 = (s32[1,64]{1,0:T(1,128)S(1)}, s32[1,64]{1,0:T(1,128)}, u32[]{:S(2)}) copy-start(s32[1,64]{1,0:T(1,128)} %slot_ref.1) | copy-start | bytes 772
  90.1 22.2 %all-to-all-start.1 = ((bf16[64,8,128]{2,1,0:T(8,128)(2,1)}), bf16[64,8,128]{2,1,0:T(8,128)(2,1)S(1)}, u32[]{:S(2)}, u32[]{:S(2)}) async-start(bf16[64,8,128]{2,1,0:T(8,128)(2,1)} %copy.25), calls=%async_computation.1 | async-start | bytes 262144 | tf_op jit(solution)/shard_map/all_to_all | solution.py:359
  113.6 22.3 %all-to-all-start.2 = ((bf16[8,256,256]{2,1,0:T(8,128)(2,1)}), bf16[8,256,256]{2,1,0:T(8,128)(2,1)S(1)}, u32[]{:S(2)}, u32[]{:S(2)}) async-start(bf16[8,256,256]{2,1,0:T(8,128)(2,1)} %broadcast_in_dim.4), calls=%async_computation.2 | async-start | bytes 2097152 | tf_op jit(solution)/shard_map/all_to_all | solution.py:359
  121.1 66.6 %copy-start.7 = (bf16[256,1408]{1,0:T(8,128)(2,1)S(1)}, bf16[256,1408]{1,0:T(8,128)(2,1)}, u32[]{:S(2)}) copy-start(bf16[256,1408]{1,0:T(8,128)(2,1)} %constant.26.clone.across_source) | copy-start | bytes 2162692
  121.1 66.6 %copy-start.8 = (bf16[128,1760]{1,0:T(8,128)(2,1)S(1)}, bf16[128,1760]{1,0:T(8,128)(2,1)}, u32[]{:S(2)}) copy-start(bf16[128,1760]{1,0:T(8,128)(2,1)} %constant.27.clone.down_source) | copy-start | bytes 1351684
  187.7 2.2 copy-start.1
Sparse Core Ops, SparseCore 0:
  88.6 99.0 all-gather.2

commit v7 on v6

--- a/solution.py
+++ b/solution.py
@@ -336,7 +336,7 @@
         ]
         + [pltpu.VMEM((GROUP * SPAN, 2 * PIX), BF16)] * BUFFERS
         + [pltpu.VMEM((depth, GROUP * PIX), BF16)] * BUFFERS,
-        compiler_params=pltpu.CompilerParams(vmem_limit_bytes=48 * 1024 * 1024),
+        compiler_params=pltpu.CompilerParams(vmem_limit_bytes=60 * 1024 * 1024),
         cost_estimate=pl.CostEstimate(
             flops=2 * tile_count * (SPAN * 256 * 1408 + depth * PIX * PIX),
             bytes_accessed=12 * 1024 * 1024,

time: 221 us -> 220 us (level)
    unnamed x21 -> x15, local copies, waits for them, and re-layouts: 5.78 us -> 3.58 us
  transfers between devices with their start and end apart: 3 -> 3, of which waited for: 3 -> 3; matrix products, arithmetic and copies ran while one was open for 2% -> 3% of each run, Pallas kernels for 3% -> 3%
where the time goes in v7:
time: 220 us; the launch traced here: 219 us
  blocking collectives  75 us (34%)
  waiting for transfers between devices  67.7 us (31%)
  Pallas kernels  34.7 us (16%)
  starting transfers between devices  17.9 us (8%)
  between operations  14.1 us (6%)
  local copies, waits for them, and re-layouts  8.16 us (4%)
    all_to_all x1, blocking collectives, exchanged(): return lax.all_to_all(array, axis, split_axis=0, concat_axis=0, tiled=True)  75 us
    all_gather x1, waiting for transfers between devices, body(): gathered = lax.all_gather(coadd, 'patch', axis=0, tiled=False)  50.9 us
    pallas_call x1, Pallas kernels, detect(): pl.pallas_call(detect_kernel, in_specs=[smem, smem] + [pl.BlockSpec(memor...  24.6 us
    all_to_all x2, starting transfers between devices, exchanged(): return lax.all_to_all(array, axis, split_axis=0, concat_axis=0, tiled=True)  17.8 us
    all_to_all x2, waiting for transfers between devices, exchanged(): return lax.all_to_all(array, axis, split_axis=0, concat_axis=0, tiled=True)  16.9 us
    pallas_call x1, Pallas kernels, smooth_tiles(): pl.pallas_call(smooth_kernel, grid=(count // 8,), in_specs=[pl.BlockSpec(...  7.48 us
  transfers between devices with their start and end apart: 3, of which 3 were waited for; matrix products, arithmetic and copies ran while one was open for 3% of the time, Pallas kernels for 3%

profile of v7, /device:TPU:1, one launch (start us, length us, event | category | flops | bytes accessed | tf_op | source)
XLA Modules:
  0.0 219.1 jit_solution(14129909942504357136)
XLA Ops:
  7.2 0.0 all-gather.3.cloned.1.call-start
  7.2 0.0 copy-start
  7.2 1.6 copy-done
  8.8 0.0 copy-start.1
  8.8 0.7 copy-done.1
  9.5 0.0 copy-start.2
  9.5 0.7 copy-done.2
  10.1 0.0 copy-start.4
  10.1 0.7 copy-done.4
  10.8 0.7 shard_map.103
  11.5 75.0 %all_to_all.15.row_ref = bf16[64,144,128]{2,1,0:T(8,128)(2,1)S(1)} all-to-all(bf16[64,144,128]{2,1,0:T(8,128)(2,1)S(1)} %shard_map.103), channel_id=1, replica_groups=mesh['patch'=64,'band'=8] {'patch'}, dimensions={0} | all-to-all | bytes 4718592 | tf_op jit(solution)/shard_map/all_to_all | solution.py:359
  86.5 1.9 shard_map.104
  88.5 0.0 all-gather.3.cloned.1.call-update
  88.5 0.9 copy.24
  89.4 0.7 copy.25
  90.2 0.0 copy-start.6
  90.2 0.0 copy-start.3
  90.2 0.0 copy-start.5
  90.2 10.6 %all-to-all-start.1 = ((bf16[64,8,128]{2,1,0:T(8,128)(2,1)}), bf16[64,8,128]{2,1,0:T(8,128)(2,1)S(1)}, u32[]{:S(2)}, u32[]{:S(2)}) async-start(bf16[64,8,128]{2,1,0:T(8,128)(2,1)} %copy.25), calls=%async_computation.1 | async-start | bytes 262144 | tf_op jit(solution)/shard_map/all_to_all | solution.py:359
  100.8 11.5 %all-to-all-done.1 = bf16[64,8,128]{2,1,0:T(8,128)(2,1)S(1)} async-done(((bf16[64,8,128]{2,1,0:T(8,128)(2,1)}), bf16[64,8,128]{2,1,0:T(8,128)(2,1)S(1)}, u32[]{:S(2)}, u32[]{:S(2)}) %all-to-all-start.1) | async-done | bytes 131104 | tf_op jit(solution)/shard_map/all_to_all | solution.py:359
  112.4 0.1 copy.27
  112.6 1.0 broadcast_in_dim.4
  113.6 7.2 %all-to-all-start.2 = ((bf16[8,256,256]{2,1,0:T(8,128)(2,1)}), bf16[8,256,256]{2,1,0:T(8,128)(2,1)S(1)}, u32[]{:S(2)}, u32[]{:S(2)}) async-start(bf16[8,256,256]{2,1,0:T(8,128)(2,1)} %broadcast_in_dim.4), calls=%async_computation.2 | async-start | bytes 2097152 | tf_op jit(solution)/shard_map/all_to_all | solution.py:359
  120.8 0.0 copy-done.6
  120.8 0.1 copy.29
  120.9 0.7 reshape.50.coeff_ref
  121.6 0.0 copy-done.3
  121.6 0.0 copy-done.5
  121.6 0.5 bitcast_add_fusion.place_ref
  122.2 7.5 %shard_map.105.tile_source = f32[64,128,128]{2,1,0:T(8,128)} custom-call(bf16[64,128,128]{2,1,0:T(8,128)(2,1)} %bitcast.27, bf16[128,128]{1,0:T(8,128)(2,1)} %constant.28.clone.smoother_ref), custom_call_target="tpu_custom_call" | custom-call | flops 536870912 | bytes 6291456 | tf_op jit(solution)/shard_map/pallas_call | solution.py:145
  129.6 0.1 copy.28
  129.8 0.7 reshape.49
  130.5 5.4 %all-to-all-done.2 = bf16[8,256,256]{2,1,0:T(8,128)(2,1)S(1)} async-done(((bf16[8,256,256]{2,1,0:T(8,128)(2,1)}), bf16[8,256,256]{2,1,0:T(8,128)(2,1)S(1)}, u32[]{:S(2)}, u32[]{:S(2)}) %all-to-all-start.2) | async-done | bytes 1048608 | tf_op jit(solution)/shard_map/all_to_all | solution.py:359
  135.9 0.1 convert_reduce_fusion
  136.0 0.8 sqrt_convert_fusion
  136.8 50.9 %all-gather.3.cloned.1.call-done = bf16[32768,128]{1,0:T(8,128)(2,1)} async-done(((bf16[512,128]{1,0:T(8,128)(2,1)}), bf16[32768,128]{1,0:T(8,128)(2,1)}) %all-gather.3.cloned.1.call-update) | async-done | bytes 8388624 | tf_op jit(solution)/shard_map/all_gather | solution.py:363
  187.7 24.6 %shard_map.106 = bf16[64,128,128]{2,1,0:T(8,128)(2,1)} custom-call(s32[64]{0:T(128)} %bitcast_add_fusion.place_ref, f32[1728]{0:T(1024)} %reshape.50.coeff_ref, bf16[64,512,128]{2,1,0:T(8,128)(2,1)} %bitcast.36, f32[64,128,128]{2,1,0:T(8,128)} %shard_map.105.tile_source, bf16[256,1408]{1,0:T(8,128)(2,1)} %constant.26.clone.across_source, ...), custom_call_target="tpu_custom_call" | custom-call | flops 11072962560 | bytes 12582912 | tf_op jit(solution)/shard_map/pallas_call | solution.py:324
  (4 shorter events, 0.1 us)
Async XLA Ops:
  7.2 180.5 %all-gather.3.cloned.1.call-start = ((), (), s32[]{:S(2)}) async-start(), calls=%async_computation.3 | async-start | bytes 8519680 | tf_op jit(solution)/shard_map/all_gather | solution.py:363
  7.2 1.6 copy-start
  8.8 0.7 copy-start.1
  9.5 0.7 copy-start.2
  10.1 0.7 copy-start.4
  90.2 30.7 %copy-start.6 = (bf16[1,64,27]{1,2,0:T(8,128)(2,1)S(1)}, bf16[1,64,27]{1,2,0:T(8,128)(2,1)}, u32[]{:S(2)}) copy-start(bf16[1,64,27]{1,2,0:T(8,128)(2,1)} %param.12) | copy-start | bytes 10372
  90.2 31.5 %copy-start.3 = (s32[1,64,1]{1,2,0:T(1,128)S(1)}, s32[1,64,1]{1,2,0:T(1,128)}, u32[]{:S(2)}) copy-start(s32[1,64,1]{1,2,0:T(1,128)} %param.9) | copy-start | bytes 772
  90.2 31.5 %copy-start.5 = (s32[1,64]{1,0:T(1,128)S(1)}, s32[1,64]{1,0:T(1,128)}, u32[]{:S(2)}) copy-start(s32[1,64]{1,0:T(1,128)} %slot_ref.1) | copy-start | bytes 772
  90.2 22.2 %all-to-all-start.1 = ((bf16[64,8,128]{2,1,0:T(8,128)(2,1)}), bf16[64,8,128]{2,1,0:T(8,128)(2,1)S(1)}, u32[]{:S(2)}, u32[]{:S(2)}) async-start(bf16[64,8,128]{2,1,0:T(8,128)(2,1)} %copy.25), calls=%async_computation.1 | async-start | bytes 262144 | tf_op jit(solution)/shard_map/all_to_all | solution.py:359
  113.6 22.3 %all-to-all-start.2 = ((bf16[8,256,256]{2,1,0:T(8,128)(2,1)}), bf16[8,256,256]{2,1,0:T(8,128)(2,1)S(1)}, u32[]{:S(2)}, u32[]{:S(2)}) async-start(bf16[8,256,256]{2,1,0:T(8,128)(2,1)} %broadcast_in_dim.4), calls=%async_computation.2 | async-start | bytes 2097152 | tf_op jit(solution)/shard_map/all_to_all | solution.py:359
Sparse Core Ops, SparseCore 0:
  88.6 99.0 all-gather.2

commit v8 on v5

--- a/solution.py
+++ b/solution.py
@@ -84,8 +84,10 @@
         write(first + 1, moved[:, PIX:].reshape(16, 16, PIX))
 
 
-def pack_kernel(exchange_ref, about_ref, tile_ref, out_ref):
-    exchange = exchange_ref[...]
+def pack_kernel(about_ref, tile_ref, out_ref):
+    target = lax.broadcasted_iota(jnp.int32, (256, 256), 0)
+    origin = lax.broadcasted_iota(jnp.int32, (256, 256), 1)
+    exchange = jnp.where(origin == (target % 16) * 16 + target // 16, 1.0, 0.0).astype(BF16)
     count = tile_ref.shape[0]
     for half in range(2):
         for start in range(0, count, 16):
@@ -104,7 +106,7 @@
         out_ref[device, 2 * count :, :] = about
 
 
-def pack(exchange, about, tiles):
+def pack(about, tiles):
     count = tiles.shape[0]
     return pl.pallas_call(
         pack_kernel,
@@ -113,7 +115,7 @@
         cost_estimate=pl.CostEstimate(
             flops=4 * 256 * count * HALF * PIX, bytes_accessed=8 * count * HALF * PIX, transcendentals=0
         ),
-    )(exchange, about, tiles)
+    )(about, tiles)
 
 
 def coadd_kernel(row_ref, coadd_ref, sum_ref):
@@ -324,7 +326,7 @@
     def exchanged(array, axis):
         return lax.all_to_all(array, axis, split_axis=0, concat_axis=0, tiled=True)
 
-    rows = exchanged(pack(exchange, about, tiles), "patch")
+    rows = exchanged(pack(about, tiles), "patch")
     coadd, weight_sum = coadd_rows(rows)
     gathered = lax.all_gather(coadd, "patch", axis=0, tiled=False)
 

time: 220 us -> 219 us (level)
  no operation moved by 1% of the time
where the time goes in v8:
time: 219 us; the launch traced here: 218 us
  blocking collectives  75.3 us (34%)
  waiting for transfers between devices  71.6 us (33%)
  Pallas kernels  27.1 us (12%)
  starting transfers between devices  17.9 us (8%)
  between operations  14.2 us (6%)
  local copies, waits for them, and re-layouts  8.75 us (4%)
  other arithmetic  3.63 us (2%)
    all_to_all x1, blocking collectives, exchanged(): return lax.all_to_all(array, axis, split_axis=0, concat_axis=0, tiled=True)  75.3 us
    all_gather x1, waiting for transfers between devices, body(): gathered = lax.all_gather(coadd, 'patch', axis=0, tiled=False)  48.6 us
    pallas_call x1, Pallas kernels, detect(): pl.pallas_call(detect_kernel, in_specs=[smem, smem, vmem] + [pl.BlockSpec...  24.5 us
    all_to_all x2, waiting for transfers between devices, exchanged(): return lax.all_to_all(array, axis, split_axis=0, concat_axis=0, tiled=True)  23.1 us
    all_to_all x2, starting transfers between devices, exchanged(): return lax.all_to_all(array, axis, split_axis=0, concat_axis=0, tiled=True)  17.9 us
  transfers between devices with their start and end apart: 3, of which 3 were waited for; matrix products, arithmetic and copies ran while one was open for 4% of the time, Pallas kernels for 0%

profile of v8, /device:TPU:1, one launch (start us, length us, event | category | flops | bytes accessed | tf_op | source)
XLA Modules:
  0.0 218.5 jit_solution(2011291483375168729)
XLA Ops:
  7.2 0.0 all-gather.3.cloned.1.call-start
  7.2 0.7 fusion.10
  7.9 0.7 select_convert_fusion.1
  8.6 0.1 fusion.3.about_ref
  8.7 0.0 copy-start
  8.7 1.6 copy-done
  10.2 0.7 shard_map.112
  11.0 75.3 %all_to_all.15.row_ref = bf16[64,144,128]{2,1,0:T(8,128)(2,1)S(1)} all-to-all(bf16[64,144,128]{2,1,0:T(8,128)(2,1)S(1)} %shard_map.112), channel_id=1, replica_groups=mesh['patch'=64,'band'=8] {'patch'}, dimensions={0} | all-to-all | bytes 4718592 | tf_op jit(solution)/shard_map/all_to_all | solution.py:327
  86.2 1.9 shard_map.113
  88.2 0.0 all-gather.3.cloned.1.call-update
  88.2 0.9 copy.25
  89.1 0.7 copy.26
  89.8 0.0 copy-start.7
  89.8 0.0 copy-start.8
  89.9 0.0 copy-start.9
  89.9 10.4 %all-to-all-start.1 = ((bf16[64,8,128]{2,1,0:T(8,128)(2,1)}), bf16[64,8,128]{2,1,0:T(8,128)(2,1)S(1)}, u32[]{:S(2)}, u32[]{:S(2)}) async-start(bf16[64,8,128]{2,1,0:T(8,128)(2,1)} %copy.26), calls=%async_computation.1 | async-start | bytes 262144 | tf_op jit(solution)/shard_map/all_to_all | solution.py:327
  100.3 11.5 %all-to-all-done.1 = bf16[64,8,128]{2,1,0:T(8,128)(2,1)S(1)} async-done(((bf16[64,8,128]{2,1,0:T(8,128)(2,1)}), bf16[64,8,128]{2,1,0:T(8,128)(2,1)S(1)}, u32[]{:S(2)}, u32[]{:S(2)}) %all-to-all-start.1) | async-done | bytes 131104 | tf_op jit(solution)/shard_map/all_to_all | solution.py:327
  111.8 0.0 copy-start.6
  111.8 0.6 copy-done.6
  112.5 0.1 copy.28
  112.7 1.0 broadcast_in_dim.17
  113.7 0.0 copy-start.1
  113.7 0.0 copy-start.2
  113.7 0.0 copy-start.3
  113.7 0.0 copy-start.4
  113.7 0.0 copy-start.5
  113.8 7.5 %all-to-all-start.2 = ((bf16[8,256,256]{2,1,0:T(8,128)(2,1)}), bf16[8,256,256]{2,1,0:T(8,128)(2,1)}, u32[]{:S(2)}, u32[]{:S(2)}) async-start(bf16[8,256,256]{2,1,0:T(8,128)(2,1)} %broadcast_in_dim.17), calls=%async_computation.2 | async-start | bytes 2097152 | tf_op jit(solution)/shard_map/all_to_all | solution.py:327
  121.2 0.0 copy-done.7
  121.2 0.1 copy.30
  121.3 0.1 reshape.52.coeff_ref
  121.5 0.0 copy-done.8
  121.5 0.0 copy-done.9
  121.5 1.7 copy.29
  123.2 1.6 reshape.51
  124.9 11.6 %all-to-all-done.2 = bf16[8,256,256]{2,1,0:T(8,128)(2,1)} async-done(((bf16[8,256,256]{2,1,0:T(8,128)(2,1)}), bf16[8,256,256]{2,1,0:T(8,128)(2,1)}, u32[]{:S(2)}, u32[]{:S(2)}) %all-to-all-start.2) | async-done | bytes 1048608 | tf_op jit(solution)/shard_map/all_to_all | solution.py:327
  136.4 1.4 convert_reduce_fusion
  137.8 0.8 sqrt_convert_fusion
  138.6 48.6 %all-gather.3.cloned.1.call-done = bf16[32768,128]{1,0:T(8,128)(2,1)} async-done(((bf16[512,128]{1,0:T(8,128)(2,1)}), bf16[32768,128]{1,0:T(8,128)(2,1)}) %all-gather.3.cloned.1.call-update) | async-done | bytes 8388624 | tf_op jit(solution)/shard_map/all_gather | solution.py:331
  187.1 0.0 copy-done.1
  187.1 0.0 copy-done.2
  187.1 0.0 copy-done.3
  187.1 0.0 copy-done.4
  187.2 0.0 copy-done.5
  187.2 24.5 %shard_map.114 = bf16[64,128,128]{2,1,0:T(8,128)(2,1)} custom-call(s32[64]{0:T(128)S(1)} %fusion.9.place_ref, f32[1728]{0:T(1024)S(1)} %reshape.52.coeff_ref, bf16[256,256]{1,0:T(8,128)(2,1)S(1)} %copy-done.4, bf16[64,512,128]{2,1,0:T(8,128)(2,1)} %bitcast.45, bf16[64,128,128]{2,1,0:T(8,128)(2,1)S(1)} %bitcast.38, bf16[256,1408]{1,0:T(8,128)(2,1)S(1)} %copy-done.2, ...), custom_call_target="tpu_custom_call" | custom-call | flops 11341398016 | bytes 12582912 | tf_op jit(solution)/shard_map/pallas_call | solution.py:288
  (5 shorter events, 0.1 us)
Async XLA Ops:
  7.2 180.0 %all-gather.3.cloned.1.call-start = ((), (), s32[]{:S(2)}) async-start(), calls=%async_computation.3 | async-start | bytes 8519680 | tf_op jit(solution)/shard_map/all_gather | solution.py:331
  8.7 1.6 copy-start
  89.8 31.4 %copy-start.7 = (bf16[1,64,27]{1,2,0:T(8,128)(2,1)S(1)}, bf16[1,64,27]{1,2,0:T(8,128)(2,1)}, u32[]{:S(2)}) copy-start(bf16[1,64,27]{1,2,0:T(8,128)(2,1)} %param.13) | copy-start | bytes 10372
  89.8 31.6 %copy-start.8 = (s32[1,64]{1,0:T(1,128)S(1)}, s32[1,64]{1,0:T(1,128)}, u32[]{:S(2)}) copy-start(s32[1,64]{1,0:T(1,128)} %param.11) | copy-start | bytes 772
  89.9 31.6 %copy-start.9 = (s32[1,64,1]{1,2,0:T(1,128)S(1)}, s32[1,64,1]{1,2,0:T(1,128)}, u32[]{:S(2)}) copy-start(s32[1,64,1]{1,2,0:T(1,128)} %param.10) | copy-start | bytes 772
  89.9 21.9 %all-to-all-start.1 = ((bf16[64,8,128]{2,1,0:T(8,128)(2,1)}), bf16[64,8,128]{2,1,0:T(8,128)(2,1)S(1)}, u32[]{:S(2)}, u32[]{:S(2)}) async-start(bf16[64,8,128]{2,1,0:T(8,128)(2,1)} %copy.26), calls=%async_computation.1 | async-start | bytes 262144 | tf_op jit(solution)/shard_map/all_to_all | solution.py:327
  111.8 0.7 copy-start.6
  113.7 73.4 %copy-start.1 = (bf16[1,64,128,128]{3,2,1,0:T(8,128)(2,1)S(1)}, bf16[1,64,128,128]{3,2,1,0:T(8,128)(2,1)}, u32[]{:S(2)}) copy-start(bf16[1,64,128,128]{3,2,1,0:T(8,128)(2,1)} %param.9) | copy-start | bytes 6291460
  113.7 73.4 %copy-start.2 = (bf16[256,1408]{1,0:T(8,128)(2,1)S(1)}, bf16[256,1408]{1,0:T(8,128)(2,1)}, u32[]{:S(2)}) copy-start(bf16[256,1408]{1,0:T(8,128)(2,1)} %constant.60.clone.across_source) | copy-start | bytes 2162692
  113.7 73.4 %copy-start.3 = (bf16[128,1888]{1,0:T(8,128)(2,1)S(1)}, bf16[128,1888]{1,0:T(8,128)(2,1)}, u32[]{:S(2)}) copy-start(bf16[128,1888]{1,0:T(8,128)(2,1)} %constant.61.clone.down_source) | copy-start | bytes 1449988
  113.7 73.4 %copy-start.4 = (bf16[256,256]{1,0:T(8,128)(2,1)S(1)}, bf16[256,256]{1,0:T(8,128)(2,1)}, u32[]{:S(2)}) copy-start(bf16[256,256]{1,0:T(8,128)(2,1)} %constant.63.clone.exchange_ref) | copy-start | bytes 393220
  113.7 73.4 %copy-start.5 = (bf16[128,128]{1,0:T(8,128)(2,1)S(1)}, bf16[128,128]{1,0:T(8,128)(2,1)}, u32[]{:S(2)}) copy-start(bf16[128,128]{1,0:T(8,128)(2,1)} %constant.62.clone.smoother_ref) | copy-start | bytes 98308
  113.8 22.7 %all-to-all-start.2 = ((bf16[8,256,256]{2,1,0:T(8,128)(2,1)}), bf16[8,256,256]{2,1,0:T(8,128)(2,1)}, u32[]{:S(2)}, u32[]{:S(2)}) async-start(bf16[8,256,256]{2,1,0:T(8,128)(2,1)} %broadcast_in_dim.17), calls=%async_computation.2 | async-start | bytes 2097152 | tf_op jit(solution)/shard_map/all_to_all | solution.py:327
Sparse Core Ops, SparseCore 0:
  88.3 98.7 all-gather.2
